TPU v7x, 128 devices: a whole 4x4x4 slice. The times are simulated.
128 devices in a mesh: group: 16 (over y_hi, x, core), blk: 8 (over y_lo, z).
Axes of the slice: x: 4, y: 4 (y_hi: 2, y_lo: 2; y = y_hi * 2 + y_lo), z: 4, core: 2. Of those that a mesh axis runs over, the one named last changes fastest.
Arguments:
- embeddings: bfloat16 [131072, 512], P(('group', 'blk')), may hold values from -300 to 300
- cluster: int32 [131072], P(('group', 'blk')), may hold values from 0 to 63, as said below
Outputs:
- max_similarity: float32 [131072], P(('group', 'blk'))
Inputs may be any that keep to these rules, and one draw needn't show every extreme that they name: Cluster c belongs to group c // 4, the group of that index along the mesh axis group. Every cluster has 2 or more rows. On the rows of one device, at most 96 belong to clusters of one group, and in every draw some group has exactly 96 rows on every device.
All inputs are finite; a program needn't handle non-finite values.
Results may differ from a plain program's by a relative error of at most 0.00053.
Values may be sent and summed in bfloat16 or wider, within the bound.
No kernel may reach another device: no remote copies, remote signals or barrier semaphores. Data moves between devices by JAX's collectives and lax.ppermute only.
A program may use at most 64 MiB of HBM per device.

v0:
```python
import math

import jax
import jax.numpy as jnp
from jax import lax
from jax.sharding import PartitionSpec as P

CPG = 4


FLOOR = -4.0


def shifted(block, axis, distance):
    devices = range(lax.axis_size(axis))
    route = [((i - distance) % len(devices), i) for i in devices]
    return lax.ppermute(block, axis, route)


def unit_rows(rows):
    values = rows.astype(jnp.float32)
    scale = lax.rsqrt(jnp.mean(values * values, axis=1, keepdims=True) + 1e-06) / math.sqrt(
        values.shape[1]
    )
    return (values * scale).astype(jnp.bfloat16)


def tile_number(amount):
    number = max(1, amount // 512)
    while amount % number != 0:
        number = number - 1
    return number


def score_block(own_rows, own_labels, other_rows, other_labels, same):
    amount = own_rows.shape[0]
    pieces = tile_number(amount)
    height = amount // pieces
    tiles_rows = own_rows.reshape(pieces, height, own_rows.shape[1])
    tiles_labels = own_labels.reshape(pieces, height)
    starts = jnp.arange(pieces, dtype=jnp.int32) * height
    columns = jnp.arange(other_rows.shape[0], dtype=jnp.int32)

    def one_tile(col_best, inputs):
        rows, labels, first = inputs
        scores = lax.dot_general(
            rows, other_rows, (((1,), (1,)), ((), ())), preferred_element_type=jnp.float32
        )
        match = (labels[:, None] == other_labels[None, :]) & (labels[:, None] >= 0)
        if same:
            match = match & (
                (first + jnp.arange(height, dtype=jnp.int32))[:, None] != columns[None, :]
            )
        masked = jnp.where(match, scores, FLOOR)
        return (jnp.maximum(col_best, jnp.max(masked, axis=0)), jnp.max(masked, axis=1))

    start_best = jnp.full((other_rows.shape[0],), FLOOR, jnp.float32)
    col_best, row_best = lax.scan(one_tile, start_best, (tiles_rows, tiles_labels, starts))
    return (row_best.reshape(amount), col_best)


def shards(embeddings, cluster):
    rows_here = embeddings.shape[0]
    groups = lax.axis_size("group")
    blocks = lax.axis_size("blk")
    slots = 3 * rows_here // (2 * groups)
    width = slots * groups
    unit = unit_rows(embeddings)
    target = cluster // CPG
    onehot = (target[:, None] == jnp.arange(groups, dtype=jnp.int32)[None, :]).astype(jnp.int32)
    before = jnp.cumsum(onehot, axis=0) - onehot
    place = target * slots + jnp.sum(before * onehot, axis=1)
    send_rows = jnp.zeros((width, unit.shape[1]), jnp.bfloat16).at[place].set(unit)
    send_labels = jnp.full((width,), -1, jnp.int32).at[place].set(cluster)
    got_rows, got_labels = (
        lax.all_to_all(
            send_rows.reshape(groups, slots, unit.shape[1]),
            "group",
            split_axis=0,
            concat_axis=0,
            tiled=True,
        ),
        lax.all_to_all(
            send_labels.reshape(groups, slots), "group", split_axis=0, concat_axis=0, tiled=True
        ),
    )
    own_rows = got_rows.reshape(width, unit.shape[1])
    own_labels = got_labels.reshape(width)
    best, unused = score_block(own_rows, own_labels, own_rows, own_labels, True)

    def visit_every(step, carry):
        rows, labels, found = carry
        rows, labels = shifted((rows, labels), "blk", 1)
        row_part, col_part = score_block(own_rows, own_labels, rows, labels, False)
        return (rows, labels, jnp.maximum(found, row_part))

    carry = lax.fori_loop(0, blocks - 1, visit_every, (own_rows, own_labels, best))
    best = carry[2]
    answers = lax.all_to_all(
        best.reshape(groups, slots), "group", split_axis=0, concat_axis=0, tiled=True
    )
    return answers.reshape(width)[place]


def solution(mesh):
    in_specs = (P(("group", "blk"), None), P(("group", "blk")))
    out_specs = P(("group", "blk"))
    return jax.shard_map(shards, mesh=mesh, in_specs=in_specs, out_specs=out_specs, check_vma=False)
```

profile of v0, /device:TPU:1, one launch (start us, length us, event | category | flops | bytes accessed | tf_op | source)
XLA Modules:
  0.0 386.3 jit_solution(6918671369518005077)
XLA Ops:
  0.8 4.5 %reduce-window.6 = s32[16,8,128]{2,1,0:T(8,128)S(1)} reduce-window(s32[16,8,128]{2,1,0:T(8,128)S(1)} %fusion.20, s32[]{:T(128)} %constant.66.clone.1), window={size=1x1x128 pad=0_0x0_0x127_0}, to_apply=%region_0.0 | reduce-window | flops 2080768 | bytes 131076 | tf_op jit(solution)/shard_map/reduce-window
  6.5 4.5 %scatter_custom_fusion.1 = s32[1536]{0:T(1024)S(1)} fusion(s32[1024]{0:T(1024)S(1)} %get-tuple-element.168, s32[1024]{0:T(1024)} %param.9, s32[]{:T(128)} %constant.71.clone.1), kind=kCustom, calls=%fused_computation.42 | custom fusion | bytes 6656 | tf_op jit(solution)/shard_map/scatter | solution.py:74
  11.6 8.4 %all-to-all-start.1 = ((s32[16,1,96]{2,1,0:T(1,128)}), s32[16,1,96]{2,1,0:T(1,128)S(1)}, u32[]{:S(2)}, u32[]{:S(2)}) async-start(s32[16,1,96]{2,1,0:T(1,128)} %all_to_all.18), calls=%async_computation.1 | async-start | bytes 16384 | tf_op jit(solution)/shard_map/all_to_all | solution.py:83
  20.1 1.5 fusion.11
  21.6 6.8 %scatter_custom_fusion = bf16[1536,512]{1,0:T(8,128)(2,1)} fusion(s32[1024]{0:T(1024)S(1)} %get-tuple-element.168, bf16[1024,512]{1,0:T(8,128)(2,1)S(1)} %copy-done, f32[1024]{0:T(1024)S(1)} %rsqrt_multiply_fusion, bf16[]{:T(256)} %constant.67.clone.1), kind=kCustom, calls=%fused_computation.25 | custom fusion | flops 1572864 | bytes 2625538 | tf_op jit(solution)/shard_map/scatter | solution.py:73
  28.4 7.2 %all-to-all-start = ((bf16[16,96,512]{2,1,0:T(8,128)(2,1)}), bf16[16,96,512]{2,1,0:T(8,128)(2,1)S(1)}, u32[]{:S(2)}, u32[]{:S(2)}) async-start(bf16[16,96,512]{2,1,0:T(8,128)(2,1)} %bitcast.7), calls=%async_computation | async-start | bytes 3145728 | tf_op jit(solution)/shard_map/all_to_all | solution.py:76
  37.2 21.5 %all-to-all-done = bf16[16,96,512]{2,1,0:T(8,128)(2,1)S(1)} async-done(((bf16[16,96,512]{2,1,0:T(8,128)(2,1)}), bf16[16,96,512]{2,1,0:T(8,128)(2,1)S(1)}, u32[]{:S(2)}, u32[]{:S(2)}) %all-to-all-start) | async-done | bytes 1572896 | tf_op jit(solution)/shard_map/all_to_all | solution.py:76
  59.8 9.0 %while.40 = (s32[]{:T(128)}, f32[3,512]{1,0:T(4,128)S(1)}, s32[3,512]{1,0:T(4,128)S(1)}, s32[16,96]{1,0:T(8,128)}, s32[3]{0:T(128)S(1)}, /*index=5*/bf16[3,512,5...) while((s32[]{:T(128)}, f32[3,512]{1,0:T(4,128)S(1)}, ...), condition=%wide.wide.region_8.9_spmd.clone, body=%wide.wide.region_6.8_spmd.clone.sunk | while | flops 810025472 | bytes 2124929 | solution.py:58
  61.0 1.7 fusion.39
  64.0 1.7 fusion.39
  67.1 1.7 fusion.39
  68.8 283.9 %while.39 = (s32[]{:T(128)}, bf16[1536,512]{1,0:T(8,128)(2,1)}, s32[1536]{0:T(1024)S(1)}, f32[1536]{0:T(1024)S(1)}, bf16[16,96,512]{2,1,0:T(8,128)(2,1)S(1)}, /*...) while((s32[]{:T(128)}, bf16[1536,512]{1,0:T(8,128)(2,1)}, ...), condition=%wide.wide.region_13.14_spmd, body=%wide.wide.region_9.13_spmd.sunk | while | flops 808453632 | bytes 11625830 | solution.py:97
  68.8 1.7 collective-permute-start
  70.5 1.6 collective-permute-start.1
  72.2 35.1 %collective-permute-done.1 = s32[1536]{0:T(1024)S(1)} collective-permute-done((s32[1536]{0:T(1024)S(1)}, s32[1536]{0:T(1024)S(1)}, u32[]{:S(2)}, u32[]{:S(2)}) %collective-permute-start.1) | collective-permute-done | bytes 6176 | tf_op jit(solution)/shard_map/while/body/eval_jaxpr/ppermute | solution.py:17
  107.2 4.0 %while.41 = (s32[]{:T(128)}, f32[3,512]{1,0:T(4,128)S(1)}, s32[3,512]{1,0:T(4,128)S(1)}, s32[1536]{0:T(1024)S(1)}, bf16[3,512,512]{2,1,0:T(8,128)(2,1)S(1)}, /*i...) while((s32[]{:T(128)}, f32[3,512]{1,0:T(4,128)S(1)}, s32[3,512]{1,0:T(4,128)S(1)}, ...), condition=%wide.region_12.12_spmd, body=%wide.region_10.11_spmd.sunk | while | flops 808452096 | bytes 2120801 | solution.py:58
  107.3 1.3 fusion.42
  108.6 1.3 fusion.42
  110.0 1.3 fusion.42
  113.0 36.6 %collective-permute-done.1 = s32[1536]{0:T(1024)S(1)} collective-permute-done((s32[1536]{0:T(1024)S(1)}, s32[1536]{0:T(1024)S(1)}, u32[]{:S(2)}, u32[]{:S(2)}) %collective-permute-start.1) | collective-permute-done | bytes 6176 | tf_op jit(solution)/shard_map/while/body/eval_jaxpr/ppermute | solution.py:17
  149.6 4.0 %while.41 = (s32[]{:T(128)}, f32[3,512]{1,0:T(4,128)S(1)}, s32[3,512]{1,0:T(4,128)S(1)}, s32[1536]{0:T(1024)S(1)}, bf16[3,512,512]{2,1,0:T(8,128)(2,1)S(1)}, /*i...) while((s32[]{:T(128)}, f32[3,512]{1,0:T(4,128)S(1)}, s32[3,512]{1,0:T(4,128)S(1)}, ...), condition=%wide.region_12.12_spmd, body=%wide.region_10.11_spmd.sunk | while | flops 808452096 | bytes 2120801 | solution.py:58
  149.6 1.3 fusion.42
  151.0 1.3 fusion.42
  152.3 1.3 fusion.42
  154.8 36.2 %collective-permute-done.1 = s32[1536]{0:T(1024)S(1)} collective-permute-done((s32[1536]{0:T(1024)S(1)}, s32[1536]{0:T(1024)S(1)}, u32[]{:S(2)}, u32[]{:S(2)}) %collective-permute-start.1) | collective-permute-done | bytes 6176 | tf_op jit(solution)/shard_map/while/body/eval_jaxpr/ppermute | solution.py:17
  191.0 4.1 %while.41 = (s32[]{:T(128)}, f32[3,512]{1,0:T(4,128)S(1)}, s32[3,512]{1,0:T(4,128)S(1)}, s32[1536]{0:T(1024)S(1)}, bf16[3,512,512]{2,1,0:T(8,128)(2,1)S(1)}, /*i...) while((s32[]{:T(128)}, f32[3,512]{1,0:T(4,128)S(1)}, s32[3,512]{1,0:T(4,128)S(1)}, ...), condition=%wide.region_12.12_spmd, body=%wide.region_10.11_spmd.sunk | while | flops 808452096 | bytes 2120801 | solution.py:58
  191.0 1.3 fusion.42
  192.4 1.3 fusion.42
  193.8 1.3 fusion.42
  196.3 35.3 %collective-permute-done.1 = s32[1536]{0:T(1024)S(1)} collective-permute-done((s32[1536]{0:T(1024)S(1)}, s32[1536]{0:T(1024)S(1)}, u32[]{:S(2)}, u32[]{:S(2)}) %collective-permute-start.1) | collective-permute-done | bytes 6176 | tf_op jit(solution)/shard_map/while/body/eval_jaxpr/ppermute | solution.py:17
  231.5 4.0 %while.41 = (s32[]{:T(128)}, f32[3,512]{1,0:T(4,128)S(1)}, s32[3,512]{1,0:T(4,128)S(1)}, s32[1536]{0:T(1024)S(1)}, bf16[3,512,512]{2,1,0:T(8,128)(2,1)S(1)}, /*i...) while((s32[]{:T(128)}, f32[3,512]{1,0:T(4,128)S(1)}, s32[3,512]{1,0:T(4,128)S(1)}, ...), condition=%wide.region_12.12_spmd, body=%wide.region_10.11_spmd.sunk | while | flops 808452096 | bytes 2120801 | solution.py:58
  232.9 1.3 fusion.42
  234.3 1.3 fusion.42
  236.8 34.3 %collective-permute-done.1 = s32[1536]{0:T(1024)S(1)} collective-permute-done((s32[1536]{0:T(1024)S(1)}, s32[1536]{0:T(1024)S(1)}, u32[]{:S(2)}, u32[]{:S(2)}) %collective-permute-start.1) | collective-permute-done | bytes 6176 | tf_op jit(solution)/shard_map/while/body/eval_jaxpr/ppermute | solution.py:17
  271.1 4.0 %while.41 = (s32[]{:T(128)}, f32[3,512]{1,0:T(4,128)S(1)}, s32[3,512]{1,0:T(4,128)S(1)}, s32[1536]{0:T(1024)S(1)}, bf16[3,512,512]{2,1,0:T(8,128)(2,1)S(1)}, /*i...) while((s32[]{:T(128)}, f32[3,512]{1,0:T(4,128)S(1)}, s32[3,512]{1,0:T(4,128)S(1)}, ...), condition=%wide.region_12.12_spmd, body=%wide.region_10.11_spmd.sunk | while | flops 808452096 | bytes 2120801 | solution.py:58
  272.5 1.3 fusion.42
  273.8 1.3 fusion.42
  276.4 33.4 %collective-permute-done.1 = s32[1536]{0:T(1024)S(1)} collective-permute-done((s32[1536]{0:T(1024)S(1)}, s32[1536]{0:T(1024)S(1)}, u32[]{:S(2)}, u32[]{:S(2)}) %collective-permute-start.1) | collective-permute-done | bytes 6176 | tf_op jit(solution)/shard_map/while/body/eval_jaxpr/ppermute | solution.py:17
  309.8 4.1 %while.41 = (s32[]{:T(128)}, f32[3,512]{1,0:T(4,128)S(1)}, s32[3,512]{1,0:T(4,128)S(1)}, s32[1536]{0:T(1024)S(1)}, bf16[3,512,512]{2,1,0:T(8,128)(2,1)S(1)}, /*i...) while((s32[]{:T(128)}, f32[3,512]{1,0:T(4,128)S(1)}, s32[3,512]{1,0:T(4,128)S(1)}, ...), condition=%wide.region_12.12_spmd, body=%wide.region_10.11_spmd.sunk | while | flops 808452096 | bytes 2120801 | solution.py:58
  309.8 1.3 fusion.42
  311.2 1.3 fusion.42
  312.5 1.3 fusion.42
  315.0 32.5 %collective-permute-done.1 = s32[1536]{0:T(1024)S(1)} collective-permute-done((s32[1536]{0:T(1024)S(1)}, s32[1536]{0:T(1024)S(1)}, u32[]{:S(2)}, u32[]{:S(2)}) %collective-permute-start.1) | collective-permute-done | bytes 6176 | tf_op jit(solution)/shard_map/while/body/eval_jaxpr/ppermute | solution.py:17
  347.5 4.0 %while.41 = (s32[]{:T(128)}, f32[3,512]{1,0:T(4,128)S(1)}, s32[3,512]{1,0:T(4,128)S(1)}, s32[1536]{0:T(1024)S(1)}, bf16[3,512,512]{2,1,0:T(8,128)(2,1)S(1)}, /*i...) while((s32[]{:T(128)}, f32[3,512]{1,0:T(4,128)S(1)}, s32[3,512]{1,0:T(4,128)S(1)}, ...), condition=%wide.region_12.12_spmd, body=%wide.region_10.11_spmd.sunk | while | flops 808452096 | bytes 2120801 | solution.py:58
  348.9 1.3 fusion.42
  350.2 1.3 fusion.42
  352.8 21.7 %all_to_all.26 = f32[16,1,96]{2,1,0:T(1,128)S(1)} all-to-all(f32[16,1,96]{2,1,0:T(1,128)S(1)} %all_to_all.21), channel_id=1, replica_groups=mesh['group'=16,'blk'=8] {'group'}, dimensions={0} | all-to-all | bytes 12288 | tf_op jit(solution)/shard_map/all_to_all | solution.py:99
  375.7 10.5 %gather_fusion = f32[1024]{0:T(1024)} fusion(f32[1536]{0:T(1024)S(1)} %reshape.85, s32[1024]{0:T(1024)S(1)} %get-tuple-element.167), kind=kCustom, calls=%fused_computation | custom fusion | bytes 12288 | tf_op jit(solution)/shard_map/gather | solution.py:102
  (166 shorter events, 24.3 us)
Async XLA Ops:
  0.0 21.6 %copy-start = (bf16[1024,512]{1,0:T(8,128)(2,1)S(1)}, bf16[1024,512]{1,0:T(8,128)(2,1)}, u32[]{:S(2)}) copy-start(bf16[1024,512]{1,0:T(8,128)(2,1)} %param.8) | copy-start | bytes 3145732
  11.6 16.8 %all-to-all-start.1 = ((s32[16,1,96]{2,1,0:T(1,128)}), s32[16,1,96]{2,1,0:T(1,128)S(1)}, u32[]{:S(2)}, u32[]{:S(2)}) async-start(s32[16,1,96]{2,1,0:T(1,128)} %all_to_all.18), calls=%async_computation.1 | async-start | bytes 16384 | tf_op jit(solution)/shard_map/all_to_all | solution.py:83
  28.4 8.0 %copy-start.1 = (s32[16,1,96]{2,1,0:T(1,128)}, s32[16,1,96]{2,1,0:T(1,128)S(1)}, u32[]{:S(2)}) copy-start(s32[16,1,96]{2,1,0:T(1,128)S(1)} %all-to-all-done.1) | copy-start | bytes 18436
  28.4 30.2 %all-to-all-start = ((bf16[16,96,512]{2,1,0:T(8,128)(2,1)}), bf16[16,96,512]{2,1,0:T(8,128)(2,1)S(1)}, u32[]{:S(2)}, u32[]{:S(2)}) async-start(bf16[16,96,512]{2,1,0:T(8,128)(2,1)} %bitcast.7), calls=%async_computation | async-start | bytes 3145728 | tf_op jit(solution)/shard_map/all_to_all | solution.py:76
  68.8 38.4 %collective-permute-start = (bf16[1536,512]{1,0:T(8,128)(2,1)}, bf16[1536,512]{1,0:T(8,128)(2,1)S(1)}, u32[]{:S(2)}, u32[]{:S(2)}) collective-permute-start(bf16[1536,512]{1,0:T(8,128)(2,1)} %get-tuple-element.434), channel_id=1, source_target_pairs={{7,0},{0,1},{1,2},{2,3},{3,4},{4,5},{5,6},{6,7},{15,8},{8,9},{9,10... | collective-permute-start | bytes 4718600 | tf_op jit(solution)/shard_map/while/body/eval_jaxpr/ppermute | solution.py:17
  70.5 36.7 %collective-permute-start.1 = (s32[1536]{0:T(1024)S(1)}, s32[1536]{0:T(1024)S(1)}, u32[]{:S(2)}, u32[]{:S(2)}) collective-permute-start(s32[1536]{0:T(1024)S(1)} %get-tuple-element.435), channel_id=1, source_target_pairs={{7,0},{0,1},{1,2},{2,3},{3,4},{4,5},{5,6},{6,7},{15,8},{8,9},{9,10... | collective-permute-start | bytes 18440 | tf_op jit(solution)/shard_map/while/body/eval_jaxpr/ppermute | solution.py:17
  112.5 37.1 %collective-permute-start = (bf16[1536,512]{1,0:T(8,128)(2,1)}, bf16[1536,512]{1,0:T(8,128)(2,1)S(1)}, u32[]{:S(2)}, u32[]{:S(2)}) collective-permute-start(bf16[1536,512]{1,0:T(8,128)(2,1)} %get-tuple-element.434), channel_id=1, source_target_pairs={{7,0},{0,1},{1,2},{2,3},{3,4},{4,5},{5,6},{6,7},{15,8},{8,9},{9,10... | collective-permute-start | bytes 4718600 | tf_op jit(solution)/shard_map/while/body/eval_jaxpr/ppermute | solution.py:17
  112.5 37.1 %collective-permute-start.1 = (s32[1536]{0:T(1024)S(1)}, s32[1536]{0:T(1024)S(1)}, u32[]{:S(2)}, u32[]{:S(2)}) collective-permute-start(s32[1536]{0:T(1024)S(1)} %get-tuple-element.435), channel_id=1, source_target_pairs={{7,0},{0,1},{1,2},{2,3},{3,4},{4,5},{5,6},{6,7},{15,8},{8,9},{9,10... | collective-permute-start | bytes 18440 | tf_op jit(solution)/shard_map/while/body/eval_jaxpr/ppermute | solution.py:17
  154.8 36.2 %collective-permute-start = (bf16[1536,512]{1,0:T(8,128)(2,1)}, bf16[1536,512]{1,0:T(8,128)(2,1)S(1)}, u32[]{:S(2)}, u32[]{:S(2)}) collective-permute-start(bf16[1536,512]{1,0:T(8,128)(2,1)} %get-tuple-element.434), channel_id=1, source_target_pairs={{7,0},{0,1},{1,2},{2,3},{3,4},{4,5},{5,6},{6,7},{15,8},{8,9},{9,10... | collective-permute-start | bytes 4718600 | tf_op jit(solution)/shard_map/while/body/eval_jaxpr/ppermute | solution.py:17
  154.8 36.2 %collective-permute-start.1 = (s32[1536]{0:T(1024)S(1)}, s32[1536]{0:T(1024)S(1)}, u32[]{:S(2)}, u32[]{:S(2)}) collective-permute-start(s32[1536]{0:T(1024)S(1)} %get-tuple-element.435), channel_id=1, source_target_pairs={{7,0},{0,1},{1,2},{2,3},{3,4},{4,5},{5,6},{6,7},{15,8},{8,9},{9,10... | collective-permute-start | bytes 18440 | tf_op jit(solution)/shard_map/while/body/eval_jaxpr/ppermute | solution.py:17
  196.3 35.3 %collective-permute-start = (bf16[1536,512]{1,0:T(8,128)(2,1)}, bf16[1536,512]{1,0:T(8,128)(2,1)S(1)}, u32[]{:S(2)}, u32[]{:S(2)}) collective-permute-start(bf16[1536,512]{1,0:T(8,128)(2,1)} %get-tuple-element.434), channel_id=1, source_target_pairs={{7,0},{0,1},{1,2},{2,3},{3,4},{4,5},{5,6},{6,7},{15,8},{8,9},{9,10... | collective-permute-start | bytes 4718600 | tf_op jit(solution)/shard_map/while/body/eval_jaxpr/ppermute | solution.py:17
  196.3 35.3 %collective-permute-start.1 = (s32[1536]{0:T(1024)S(1)}, s32[1536]{0:T(1024)S(1)}, u32[]{:S(2)}, u32[]{:S(2)}) collective-permute-start(s32[1536]{0:T(1024)S(1)} %get-tuple-element.435), channel_id=1, source_target_pairs={{7,0},{0,1},{1,2},{2,3},{3,4},{4,5},{5,6},{6,7},{15,8},{8,9},{9,10... | collective-permute-start | bytes 18440 | tf_op jit(solution)/shard_map/while/body/eval_jaxpr/ppermute | solution.py:17
  236.8 34.3 %collective-permute-start = (bf16[1536,512]{1,0:T(8,128)(2,1)}, bf16[1536,512]{1,0:T(8,128)(2,1)S(1)}, u32[]{:S(2)}, u32[]{:S(2)}) collective-permute-start(bf16[1536,512]{1,0:T(8,128)(2,1)} %get-tuple-element.434), channel_id=1, source_target_pairs={{7,0},{0,1},{1,2},{2,3},{3,4},{4,5},{5,6},{6,7},{15,8},{8,9},{9,10... | collective-permute-start | bytes 4718600 | tf_op jit(solution)/shard_map/while/body/eval_jaxpr/ppermute | solution.py:17
  236.8 34.3 %collective-permute-start.1 = (s32[1536]{0:T(1024)S(1)}, s32[1536]{0:T(1024)S(1)}, u32[]{:S(2)}, u32[]{:S(2)}) collective-permute-start(s32[1536]{0:T(1024)S(1)} %get-tuple-element.435), channel_id=1, source_target_pairs={{7,0},{0,1},{1,2},{2,3},{3,4},{4,5},{5,6},{6,7},{15,8},{8,9},{9,10... | collective-permute-start | bytes 18440 | tf_op jit(solution)/shard_map/while/body/eval_jaxpr/ppermute | solution.py:17
  276.3 33.4 %collective-permute-start = (bf16[1536,512]{1,0:T(8,128)(2,1)}, bf16[1536,512]{1,0:T(8,128)(2,1)S(1)}, u32[]{:S(2)}, u32[]{:S(2)}) collective-permute-start(bf16[1536,512]{1,0:T(8,128)(2,1)} %get-tuple-element.434), channel_id=1, source_target_pairs={{7,0},{0,1},{1,2},{2,3},{3,4},{4,5},{5,6},{6,7},{15,8},{8,9},{9,10... | collective-permute-start | bytes 4718600 | tf_op jit(solution)/shard_map/while/body/eval_jaxpr/ppermute | solution.py:17
  276.4 33.4 %collective-permute-start.1 = (s32[1536]{0:T(1024)S(1)}, s32[1536]{0:T(1024)S(1)}, u32[]{:S(2)}, u32[]{:S(2)}) collective-permute-start(s32[1536]{0:T(1024)S(1)} %get-tuple-element.435), channel_id=1, source_target_pairs={{7,0},{0,1},{1,2},{2,3},{3,4},{4,5},{5,6},{6,7},{15,8},{8,9},{9,10... | collective-permute-start | bytes 18440 | tf_op jit(solution)/shard_map/while/body/eval_jaxpr/ppermute | solution.py:17
  315.0 32.5 %collective-permute-start = (bf16[1536,512]{1,0:T(8,128)(2,1)}, bf16[1536,512]{1,0:T(8,128)(2,1)S(1)}, u32[]{:S(2)}, u32[]{:S(2)}) collective-permute-start(bf16[1536,512]{1,0:T(8,128)(2,1)} %get-tuple-element.434), channel_id=1, source_target_pairs={{7,0},{0,1},{1,2},{2,3},{3,4},{4,5},{5,6},{6,7},{15,8},{8,9},{9,10... | collective-permute-start | bytes 4718600 | tf_op jit(solution)/shard_map/while/body/eval_jaxpr/ppermute | solution.py:17
  315.0 32.5 %collective-permute-start.1 = (s32[1536]{0:T(1024)S(1)}, s32[1536]{0:T(1024)S(1)}, u32[]{:S(2)}, u32[]{:S(2)}) collective-permute-start(s32[1536]{0:T(1024)S(1)} %get-tuple-element.435), channel_id=1, source_target_pairs={{7,0},{0,1},{1,2},{2,3},{3,4},{4,5},{5,6},{6,7},{15,8},{8,9},{9,10... | collective-permute-start | bytes 18440 | tf_op jit(solution)/shard_map/while/body/eval_jaxpr/ppermute | solution.py:17
where the time goes:
time: 387 us; the launch traced here: 386 us
  waiting for transfers between devices  265 us (68%)
  matrix products  31.5 us (8%)
  local copies, waits for them, and re-layouts  29.9 us (8%)
  blocking collectives  21.7 us (6%)
  starting transfers between devices  19.6 us (5%)
  other arithmetic  17.9 us (5%)
    ppermute x14, waiting for transfers between devices, shifted(): return lax.ppermute(block, axis, route)  243 us
    dot_general x24, matrix products, one_tile(): lax.dot_general(rows, other_rows, (((1,), (1,)), ((), ())), preferred_ele...  31.5 us
    all_to_all x1, blocking collectives, shards(): lax.all_to_all(best.reshape(groups, slots), 'group', split_axis=0, concat...  21.7 us
    all_to_all x1, waiting for transfers between devices, shards(): lax.all_to_all(send_rows.reshape(groups, slots, unit.shape[1]), 'group',...  21.5 us
    gather x1, local copies, waits for them, and re-layouts, shards(): return answers.reshape(width)[place]  10.5 us
    all_to_all x1, starting transfers between devices, shards(): lax.all_to_all(send_labels.reshape(groups, slots), 'group', split_axis=0,...  8.45 us
    while x14, local copies, waits for them, and re-layouts  8.09 us
  transfers between devices with their start and end apart: 16, of which 8 were waited for; matrix products, arithmetic and copies ran while one was open for 3% of the time, Pallas kernels for 0%

commit v1 on v0

v1 whole, which is shorter than its diff:
```python
import math

import jax
import jax.numpy as jnp
from jax import lax
from jax.experimental import pallas as pl
from jax.experimental.pallas import tpu as pltpu
from jax.sharding import Mesh, PartitionSpec as P

CPG = 4
GROUPS = 16
SLOTS = 96
WIDTH = GROUPS * SLOTS
ROWS = 1024
D = 512
FLOOR = -4.0

SIZES = {"yh": 2, "x": 4, "c": 2, "yl": 2, "z": 4}
AXES = ("yh", "x", "c", "yl", "z")
PLANE = ("yh", "x", "yl")
RING = ("c", "z")
NT = (((1,), (1,)), ((), ()))
VMEM_LIMIT = 48 * 1024 * 1024

CROSSED = (0, 3)


def to_above():
    return [(c * 4 + z, c * 4 + (z + 1) % 4) for c in range(2) for z in range(4)]


def to_below():
    pairs = []
    for c in range(2):
        for z in range(4):
            lands = (z - 1) % 4
            pairs.append((c * 4 + z, (c ^ 1 if lands in CROSSED else c) * 4 + lands))
    return pairs


def reverse(pairs):
    return [(b, a) for a, b in pairs]


def params():
    return pltpu.CompilerParams(vmem_limit_bytes=VMEM_LIMIT)


def place_kernel(cluster_ref, place_ref, counts_ref):
    step = 256
    kinds = lax.broadcasted_iota(jnp.int32, (128, step), 0)
    before = (
        lax.broadcasted_iota(jnp.int32, (step, step), 0)
        < lax.broadcasted_iota(jnp.int32, (step, step), 1)
    ).astype(jnp.bfloat16)
    total = jnp.zeros((128, 1), jnp.float32)
    row_total = jnp.zeros((8, 128), jnp.float32)
    hots, ranks = [], []
    for first in range(0, ROWS, step):
        hot = kinds == cluster_ref[:, first : first + step]
        hot16 = hot.astype(jnp.bfloat16)
        hots.append(hot)
        ranks.append(jnp.dot(hot16, before, preferred_element_type=jnp.float32) + total)
        total = total + jnp.sum(hot.astype(jnp.float32), axis=1, keepdims=True)
        row_total = row_total + lax.dot_general(
            jnp.ones((8, step), jnp.bfloat16), hot16, NT, preferred_element_type=jnp.float32
        )
    one = lax.broadcasted_iota(jnp.int32, (128, 128), 0)
    other = lax.broadcasted_iota(jnp.int32, (128, 128), 1)
    earlier = ((one // CPG == other // CPG) & (other < one)).astype(jnp.bfloat16)
    base = jnp.dot(
        earlier,
        jnp.broadcast_to(total, (128, 128)).astype(jnp.bfloat16),
        preferred_element_type=jnp.float32,
    )[:, :1]
    base = base + (lax.broadcasted_iota(jnp.int32, (128, 1), 0) // CPG * SLOTS).astype(jnp.float32)
    for k, first in enumerate(range(0, ROWS, step)):
        place = jnp.sum(jnp.where(hots[k], ranks[k] + base, 0.0), axis=0, keepdims=True)
        place_ref[:, first : first + step] = place.astype(jnp.int32)
    counts_ref[...] = row_total[:1].astype(jnp.int32)


def placed(cluster):
    return pl.pallas_call(
        place_kernel,
        out_shape=(
            jax.ShapeDtypeStruct((1, ROWS), jnp.int32),
            jax.ShapeDtypeStruct((1, 128), jnp.int32),
        ),
        compiler_params=params(),
        name="placed",
    )(cluster)


def send_kernel(rows_ref, place_ref, out_ref, unit):
    @pl.when(pl.program_id(0) == 0)
    def _():
        values = rows_ref[...].astype(jnp.float32)
        mean = jnp.mean(values * values, axis=1, keepdims=True)
        scale = lax.rsqrt(mean + 1e-06) / math.sqrt(D)
        unit[...] = (values * scale).astype(jnp.bfloat16)

    height = out_ref.shape[0]
    slot = lax.broadcasted_iota(jnp.int32, (height, ROWS), 0) + pl.program_id(0) * height
    hot = (slot == place_ref[...]).astype(jnp.bfloat16)
    out_ref[...] = jnp.dot(hot, unit[...], preferred_element_type=jnp.float32).astype(jnp.bfloat16)


def send_rows(rows, place):
    height = 256
    return pl.pallas_call(
        send_kernel,
        grid=(WIDTH // height,),
        in_specs=[
            pl.BlockSpec((ROWS, D), lambda i: (0, 0)),
            pl.BlockSpec((1, ROWS), lambda i: (0, 0)),
        ],
        out_specs=pl.BlockSpec((height, D), lambda i: (i, 0)),
        out_shape=jax.ShapeDtypeStruct((WIDTH, D), jnp.bfloat16),
        scratch_shapes=[pltpu.VMEM((ROWS, D), jnp.bfloat16)],
        compiler_params=params(),
        name="send_rows",
    )(rows, place)


def limits(counts_ref, source, core, z, group):
    device = ((source >> 1) * 2 + core) * 8 + (source & 1) * 4 + z
    ends = []
    end = jnp.int32(0)
    for k in range(CPG):
        end = end + counts_ref[device, group * CPG + k]
        ends.append(end)
    return ends


def label_of(slot, ends, empty):
    label = jnp.where(slot < ends[3], 3, empty)
    for k in (2, 1, 0):
        label = jnp.where(slot < ends[k], k, label)
    return label


def row_labels(counts_ref, first_source, sources, core, z, group):
    slot = lax.broadcasted_iota(jnp.int32, (SLOTS, 1), 0)
    return jnp.concatenate(
        [
            label_of(slot, limits(counts_ref, first_source + s, core, z, group), -1)
            for s in range(sources)
        ],
        axis=0,
    )


def column_labels(counts_ref, core, z, group):
    lane = lax.broadcasted_iota(jnp.int32, (1, WIDTH), 1)
    label = jnp.full((1, WIDTH), -2, jnp.int32)
    for s in range(GROUPS):
        ends = limits(counts_ref, jnp.int32(s), core, z, group)
        label = jnp.where(lane >= s * SLOTS, label_of(lane - s * SLOTS, ends, -2), label)
    return label


def lanes_of(best):
    return jnp.max(best.T, axis=0, keepdims=True)


SOURCES = 4
HEIGHT = SOURCES * SLOTS
CHUNK = 512


def own_kernel(where_ref, counts_ref, rows_ref, own_ref, peer_ref, best_ref, labels):
    group, core, z = where_ref[0], where_ref[1], where_ref[2]
    step = pl.program_id(0)

    @pl.when(step == 0)
    def _():
        labels[0:1, :] = column_labels(counts_ref, core, z, group)
        labels[1:2, :] = column_labels(counts_ref, 1 - core, z, group)

    mine = row_labels(counts_ref, step * SOURCES, SOURCES, core, z, group)
    index = lax.broadcasted_iota(jnp.int32, (HEIGHT, 1), 0) + step * HEIGHT
    best = jnp.full((HEIGHT, 128), FLOOR, jnp.float32)
    rows = rows_ref[...]
    for which, ref in enumerate((own_ref, peer_ref)):
        for first in range(0, WIDTH, CHUNK):
            score = lax.dot_general(
                rows, ref[first : first + CHUNK], NT, preferred_element_type=jnp.float32
            )
            match = mine == labels[which : which + 1, first : first + CHUNK]
            if which == 0:
                column = lax.broadcasted_iota(jnp.int32, (1, CHUNK), 1) + first
                match = match & (index != column)
            score = jnp.where(match, score, FLOOR)
            for k in range(0, CHUNK, 128):
                best = jnp.maximum(best, score[:, k : k + 128])
    best_ref[...] = lanes_of(best)


def own_best(where, counts, own, peer):
    return pl.pallas_call(
        own_kernel,
        grid=(WIDTH // HEIGHT,),
        in_specs=[
            pl.BlockSpec(memory_space=pltpu.SMEM),
            pl.BlockSpec(memory_space=pltpu.SMEM),
            pl.BlockSpec((HEIGHT, D), lambda i: (i, 0)),
            pl.BlockSpec((WIDTH, D), lambda i: (0, 0)),
            pl.BlockSpec((WIDTH, D), lambda i: (0, 0)),
        ],
        out_specs=pl.BlockSpec((1, HEIGHT), lambda i: (0, i)),
        out_shape=jax.ShapeDtypeStruct((1, WIDTH), jnp.float32),
        scratch_shapes=[pltpu.VMEM((8, WIDTH), jnp.int32)],
        compiler_params=params(),
        cost_estimate=pl.CostEstimate(
            flops=4 * WIDTH * WIDTH * D, bytes_accessed=6 * WIDTH * D, transcendentals=0
        ),
        name="own_best",
    )(where, counts, own, own, peer)


def far_kernel(
    where_ref, counts_ref, own_ref, peer_ref, below_ref, above_ref, best_ref, above_best_ref, labels, column_best
):
    group, core, z = where_ref[0], where_ref[1], where_ref[2]
    under, over, over_core = where_ref[3], where_ref[4], where_ref[5]
    step = pl.program_id(0)
    tiles = WIDTH // HEIGHT
    kind = step // tiles

    @pl.when(step == 0)
    def _():
        labels[0:1, :] = column_labels(counts_ref, over_core, over, group)
        column_best[...] = jnp.full(column_best.shape, FLOOR, jnp.float32)

    row_core = jnp.where(kind == 1, 1 - core, core)
    row_z = jnp.where(kind == 2, under, z)
    mine = row_labels(counts_ref, (step - kind * tiles) * SOURCES, SOURCES, row_core, row_z, group)

    def visit(rows_ref):
        rows = rows_ref[...]
        best = jnp.full((HEIGHT, 128), FLOOR, jnp.float32)
        for first in range(0, WIDTH, CHUNK):
            score = lax.dot_general(
                rows, above_ref[first : first + CHUNK], NT, preferred_element_type=jnp.float32
            )
            score = jnp.where(mine == labels[0:1, first : first + CHUNK], score, FLOOR)
            for k in range(0, CHUNK, 128):
                best = jnp.maximum(best, score[:, k : k + 128])
            column_best[:, first : first + CHUNK] = jnp.maximum(
                column_best[:, first : first + CHUNK],
                jnp.max(score.reshape(HEIGHT // 8, 8, CHUNK), axis=0),
            )
        best_ref[...] = lanes_of(best)

    pl.when(kind == 0)(lambda: visit(own_ref))
    pl.when(kind == 1)(lambda: visit(peer_ref))
    pl.when(kind == 2)(lambda: visit(below_ref))

    @pl.when(step == 3 * tiles - 1)
    def _():
        above_best_ref[...] = jnp.max(column_best[...], axis=0, keepdims=True)


def far_best(where, counts, own, peer, below, above):
    tiles = WIDTH // HEIGHT

    def block(kind):
        return pl.BlockSpec(
            (HEIGHT, D), lambda i, kind=kind: (jnp.clip(i - kind * tiles, 0, tiles - 1), 0)
        )

    return pl.pallas_call(
        far_kernel,
        grid=(3 * tiles,),
        in_specs=[
            pl.BlockSpec(memory_space=pltpu.SMEM),
            pl.BlockSpec(memory_space=pltpu.SMEM),
            block(0),
            block(1),
            block(2),
            pl.BlockSpec((WIDTH, D), lambda i: (0, 0)),
        ],
        out_specs=(
            pl.BlockSpec((1, HEIGHT), lambda i: (0, i)),
            pl.BlockSpec((1, WIDTH), lambda i: (0, 0)),
        ),
        out_shape=(
            jax.ShapeDtypeStruct((1, 3 * WIDTH), jnp.float32),
            jax.ShapeDtypeStruct((1, WIDTH), jnp.float32),
        ),
        scratch_shapes=[pltpu.VMEM((8, WIDTH), jnp.int32), pltpu.VMEM((8, WIDTH), jnp.float32)],
        compiler_params=params(),
        cost_estimate=pl.CostEstimate(
            flops=6 * WIDTH * WIDTH * D, bytes_accessed=8 * WIDTH * D, transcendentals=0
        ),
        name="far_best",
    )(where, counts, own, peer, below, above)


def join_kernel(*refs):
    best = refs[0][...]
    for ref in refs[1:-1]:
        best = jnp.maximum(best, ref[...])
    out_ref = refs[-1]
    out_ref[...] = jnp.zeros(out_ref.shape, jnp.float32)
    for s in range(GROUPS):
        out_ref[s : s + 1, :SLOTS] = best[:, s * SLOTS : (s + 1) * SLOTS]


def joined(*parts):
    return pl.pallas_call(
        join_kernel,
        out_shape=jax.ShapeDtypeStruct((GROUPS, 128), jnp.float32),
        compiler_params=params(),
        name="joined",
    )(*parts)


def pick_kernel(answers_ref, cluster_ref, place_ref, out_ref):
    group = cluster_ref[...] // CPG
    slot = place_ref[...] - group * SLOTS
    hot = (lax.broadcasted_iota(jnp.int32, (GROUPS, ROWS), 0) == group).astype(jnp.bfloat16)
    rest = answers_ref[...]
    found = jnp.zeros((128, ROWS), jnp.float32)
    for _ in range(3):
        part = rest.astype(jnp.bfloat16)
        rest = rest - part.astype(jnp.float32)
        found = found + lax.dot_general(
            part, hot, (((0,), (0,)), ((), ())), preferred_element_type=jnp.float32
        )
    here = lax.broadcasted_iota(jnp.int32, (128, ROWS), 0) == slot
    out_ref[...] = jnp.sum(jnp.where(here, found, 0.0), axis=0, keepdims=True)


def picked(answers, cluster, place):
    return pl.pallas_call(
        pick_kernel,
        out_shape=jax.ShapeDtypeStruct((1, ROWS), jnp.float32),
        compiler_params=params(),
        name="picked",
    )(answers, cluster, place)


def shards(embeddings, cluster):
    group = lax.axis_index(PLANE)
    core = lax.axis_index("c")
    z = lax.axis_index("z")
    crossed = (z == CROSSED[0]) | (z == CROSSED[1])
    where = jnp.stack(
        [group, core, z, (z + 3) % 4, (z + 1) % 4, jnp.where(crossed, 1 - core, core)]
    ).astype(jnp.int32)
    cluster = cluster.reshape(1, ROWS)
    place, counts = placed(cluster)
    counts = lax.all_gather(counts, AXES, tiled=True)
    sent = send_rows(embeddings, place)
    own = lax.all_to_all(
        sent.reshape(GROUPS, SLOTS, D), PLANE, split_axis=0, concat_axis=0, tiled=True
    ).reshape(WIDTH, D)
    below = lax.ppermute(own, RING, to_above())
    above = lax.ppermute(own, RING, to_below())
    peer = lax.ppermute(own, "c", [(0, 1), (1, 0)])
    best_own = own_best(where, counts, own, peer)
    best, best_above = far_best(where, counts, own, peer, below, above)
    best_far, best_peer, best_below = (best[:, k * WIDTH : (k + 1) * WIDTH] for k in range(3))
    answers = joined(
        best_own,
        best_far,
        lax.ppermute(best_peer, "c", [(0, 1), (1, 0)]),
        lax.ppermute(best_below, RING, reverse(to_above())),
        lax.ppermute(best_above, RING, reverse(to_below())),
    )
    answers = lax.all_to_all(
        answers.reshape(GROUPS, 1, 128), PLANE, split_axis=0, concat_axis=0, tiled=True
    ).reshape(GROUPS, 128)
    return picked(answers, cluster, place).reshape(ROWS)


def solution(mesh):
    devices = mesh.devices.reshape(tuple(SIZES[a] for a in AXES))
    inner = Mesh(devices, AXES)
    return jax.shard_map(
        shards,
        mesh=inner,
        in_specs=(P(AXES, None), P(AXES)),
        out_specs=P(AXES),
        check_vma=False,
    )
```

time: 387 us -> 410 us (1.059)
  blocking collectives: 21.7 us -> 355 us
  waiting for transfers between devices: 265 us -> 0.02 us
  matrix products: 31.5 us -> 0 us
  Pallas kernels: 0 us -> 28 us
  local copies, waits for them, and re-layouts: 29.9 us -> 2 us
  other arithmetic: 17.9 us -> 0 us
  starting transfers between devices: 19.6 us -> 24.3 us
    all_gather x0 -> x1, blocking collectives: none -> 317 us  [shards(): counts = lax.all_gather(counts, AXES, tiled=True)]
    ppermute x14 -> x6, waiting for transfers between devices: 243 us -> 0.02 us  [the longest x1 0.01 us: shards(): below = lax.ppermute(own, RING, to_above())]
    dot_general x24 -> x0, matrix products: 31.5 us -> none  [one_tile(): lax.dot_general(rows, other_rows, (((1,), (1,)), ((), ())), preferred_ele...]
    pallas_call x0 -> x6, Pallas kernels: none -> 28 us  [the longest x1 14.6 us: far_best(): pl.pallas_call(far_kernel, grid=(3 * tiles,), in_specs=[pl.BlockSpec(memo...]
    all_to_all x2 -> x0, waiting for transfers between devices: 21.5 us -> none  [the longest x1 21.5 us: shards(): lax.all_to_all(send_rows.reshape(groups, slots, unit.shape[1]), 'group',...]
    ppermute x14 -> x6, starting transfers between devices: 3.92 us -> 24.3 us  [the longest x1 16.9 us: shards(): lax.ppermute(best_peer, 'c', [(0, 1), (1, 0)])]
    all_to_all x1 -> x2, blocking collectives: 21.7 us -> 37.9 us  [the longest x1 29 us: shards(): lax.all_to_all(sent.reshape(GROUPS, SLOTS, D), PLANE, split_axis=0, conca...]
    all_to_all x2 -> x0, starting transfers between devices: 15.7 us -> none  [the longest x1 8.45 us: shards(): lax.all_to_all(send_labels.reshape(groups, slots), 'group', split_axis=0,...]
  transfers between devices with their start and end apart: 16 -> 6, of which waited for: 8 -> 0; matrix products, arithmetic and copies ran while one was open for 3% -> 0% of each run, Pallas kernels for 0% -> 2%
where the time goes in v1:
time: 410 us; the launch traced here: 409 us
  blocking collectives  355 us (87%)
  Pallas kernels  28 us (7%)
  starting transfers between devices  24.3 us (6%)
    all_gather x1, blocking collectives, shards(): counts = lax.all_gather(counts, AXES, tiled=True)  317 us
    all_to_all x1, blocking collectives, shards(): lax.all_to_all(sent.reshape(GROUPS, SLOTS, D), PLANE, split_axis=0, conca...  29 us
    ppermute x1, starting transfers between devices, shards(): lax.ppermute(best_peer, 'c', [(0, 1), (1, 0)])  16.9 us
    pallas_call x1, Pallas kernels, far_best(): pl.pallas_call(far_kernel, grid=(3 * tiles,), in_specs=[pl.BlockSpec(memo...  14.6 us
    all_to_all x1, blocking collectives, shards(): lax.all_to_all(answers.reshape(GROUPS, 1, 128), PLANE, split_axis=0, conc...  8.97 us
    pallas_call x1, Pallas kernels, own_best(): pl.pallas_call(own_kernel, grid=(WIDTH // HEIGHT,), in_specs=[pl.BlockSpe...  8.8 us
  transfers between devices with their start and end apart: 6, of which 0 were waited for; matrix products, arithmetic and copies ran while one was open for 0% of the time, Pallas kernels for 2%

profile of v1, /device:TPU:1, one launch (start us, length us, event | category | flops | bytes accessed | tf_op | source)
XLA Modules:
  0.0 409.3 jit_solution(9444203383776726809)
XLA Ops:
  0.0 0.0 copy-start.1
  0.0 0.7 copy-done.1
  0.7 0.5 placed.1
  1.2 0.0 copy-start
  1.2 1.2 copy-done
  2.4 3.0 send_rows.1
  5.4 29.0 %all_to_all.10 = bf16[16,96,512]{2,1,0:T(8,128)(2,1)S(1)} all-to-all(bf16[16,96,512]{2,1,0:T(8,128)(2,1)S(1)} %bitcast.16), channel_id=1, replica_groups=mesh['yh'=2,'x'=4,'c'=2,'yl'=2,'z'=4] {'yh','x','yl'}, dimensions={0} | all-to-all | bytes 3145728 | tf_op jit(solution)/shard_map/all_to_all | solution.py:357
  34.4 5.8 %collective-permute-start.2 = (bf16[1536,512]{1,0:T(8,128)(2,1)S(1)}, bf16[1536,512]{1,0:T(8,128)(2,1)}, u32[]{:S(2)}, u32[]{:S(2)}) collective-permute-start(bf16[1536,512]{1,0:T(8,128)(2,1)S(1)} %bitcast.17), channel_id=1, source_target_pairs={{0,11},{1,8},{2,1},{3,2},{8,3},{9,0},{10,9},{11,10},{4,15},{5,12},... | collective-permute-start | bytes 4718600 | tf_op jit(solution)/shard_map/ppermute | solution.py:361
  40.1 0.0 collective-permute-start.1
  40.1 0.0 collective-permute-start
  40.1 0.1 stack.27.where_ref
  40.2 317.0 %all-gather = s32[128,1,128]{2,1,0:T(1,128)S(1)} all-gather(s32[1,1,128]{2,1,0:T(1,128)S(1)} %bitcast.29), channel_id=1, replica_groups=mesh['yh'=2,'x'=4,'c'=2,'yl'=2,'z'=4] {'yh','x','c','yl','z'}, dimensions={0}, use_global_device_ids=true | all-gather | bytes 66048 | tf_op jit(solution)/shard_map/all_gather | solution.py:355
  357.2 0.0 collective-permute-done.2.above_ref
  357.2 0.0 collective-permute-done.1.below_ref
  357.2 0.0 collective-permute-done.peer_ref
  357.2 14.6 %far_best.1 = (f32[1,4608]{1,0:T(1,128)S(1)}, f32[1,1536]{1,0:T(1,128)S(1)}) custom-call(s32[6]{0:T(128)S(1)} %stack.27.where_ref, s32[128,128]{1,0:T(8,128)S(1)} %bitcast.23, bf16[1536,512]{1,0:T(8,128)(2,1)S(1)} %bitcast.20, bf16[1536,512]{1,0:T(8,128)(2,1)S(1)} %collective-permute-done.peer_ref, bf16[1536,512]{1,0:T(8,128)(2,1)} %collective-permute-done.1.below_ref, ...), custom_call_target="tpu_custom_call" | custom-call | flops 7247757312 | bytes 6291456 | tf_op jit(solution)/shard_map/far_best/pallas_call | solution.py:273
  371.9 0.1 collective-permute-start.4
  371.9 16.9 %collective-permute-start.3 = (f32[1,1536]{1,0:T(1,128)S(1)}, f32[1,1536]{1,0:T(1,128)S(1)}, u32[]{:S(2)}, u32[]{:S(2)}) collective-permute-start(f32[1,1536]{1,0:T(1,128)S(1)} %get-tuple-element.14), channel_id=1, source_target_pairs={{0,8},{8,0},{1,9},{9,1},{2,10},{10,2},{3,11},{11,3},{4,12},{12,4},... | collective-permute-start | bytes 18440 | tf_op jit(solution)/shard_map/ppermute | solution.py:369
  388.8 0.0 copy-start.2
  388.9 1.5 collective-permute-start.5
  390.4 8.8 %own_best.1.refs_0_ = f32[1,1536]{1,0:T(1,128)S(1)} custom-call(s32[6]{0:T(128)S(1)} %stack.27.where_ref, s32[128,128]{1,0:T(8,128)S(1)} %bitcast.24, bf16[1536,512]{1,0:T(8,128)(2,1)S(1)} %bitcast.21, bf16[1536,512]{1,0:T(8,128)(2,1)S(1)} %bitcast.22, bf16[1536,512]{1,0:T(8,128)(2,1)S(1)} %collective-permute-done.peer_ref), custom_call_target="tpu_custom_call" | custom-call | flops 4831838208 | bytes 4718592 | tf_op jit(solution)/shard_map/own_best/pallas_call | solution.py:201
  399.2 0.0 collective-permute-done.4.refs_3_
  399.2 0.0 collective-permute-done.3.refs_2_
  399.2 0.0 collective-permute-done.5.refs_4_
  399.2 0.1 joined.1
  399.3 9.0 %all_to_all.11 = f32[16,1,128]{2,1,0:T(1,128)S(1)} all-to-all(f32[16,1,128]{2,1,0:T(1,128)S(1)} %bitcast.25), channel_id=1, replica_groups=mesh['yh'=2,'x'=4,'c'=2,'yl'=2,'z'=4] {'yh','x','yl'}, dimensions={0} | all-to-all | bytes 16384 | tf_op jit(solution)/shard_map/all_to_all | solution.py:373
  408.3 0.0 copy-done.2
  408.3 1.0 picked.1
  (1 shorter events, 0.0 us)
Async XLA Ops:
  0.0 0.7 copy-start.1
  1.2 1.2 copy-start
  34.4 322.8 %collective-permute-start.2 = (bf16[1536,512]{1,0:T(8,128)(2,1)S(1)}, bf16[1536,512]{1,0:T(8,128)(2,1)}, u32[]{:S(2)}, u32[]{:S(2)}) collective-permute-start(bf16[1536,512]{1,0:T(8,128)(2,1)S(1)} %bitcast.17), channel_id=1, source_target_pairs={{0,11},{1,8},{2,1},{3,2},{8,3},{9,0},{10,9},{11,10},{4,15},{5,12},... | collective-permute-start | bytes 4718600 | tf_op jit(solution)/shard_map/ppermute | solution.py:361
  40.1 317.1 %collective-permute-start.1 = (bf16[1536,512]{1,0:T(8,128)(2,1)S(1)}, bf16[1536,512]{1,0:T(8,128)(2,1)}, u32[]{:S(2)}, u32[]{:S(2)}) collective-permute-start(bf16[1536,512]{1,0:T(8,128)(2,1)S(1)} %bitcast.18), channel_id=1, source_target_pairs={{0,1},{1,2},{2,3},{3,0},{8,9},{9,10},{10,11},{11,8},{4,5},{5,6},{6... | collective-permute-start | bytes 4718600 | tf_op jit(solution)/shard_map/ppermute | solution.py:360
  40.1 317.1 %collective-permute-start = (bf16[1536,512]{1,0:T(8,128)(2,1)S(1)}, bf16[1536,512]{1,0:T(8,128)(2,1)S(1)}, u32[]{:S(2)}, u32[]{:S(2)}) collective-permute-start(bf16[1536,512]{1,0:T(8,128)(2,1)S(1)} %bitcast.19), channel_id=1, source_target_pairs={{0,8},{8,0},{1,9},{9,1},{2,10},{10,2},{3,11},{11,3},{4,12},{12,4},... | collective-permute-start | bytes 4718600 | tf_op jit(solution)/shard_map/ppermute | solution.py:362
  371.9 27.4 %collective-permute-start.4 = (f32[1,1536]{1,0:T(1,128)S(1)}, f32[1,1536]{1,0:T(1,128)S(1)}, u32[]{:S(2)}, u32[]{:S(2)}) collective-permute-start(f32[1,1536]{1,0:T(1,128)S(1)} %get-tuple-element.13), channel_id=1, source_target_pairs={{1,0},{2,1},{3,2},{0,3},{9,8},{10,9},{11,10},{8,11},{5,4},{6,5},{7... | collective-permute-start | bytes 18440 | tf_op jit(solution)/shard_map/ppermute | solution.py:370
  371.9 27.3 %collective-permute-start.3 = (f32[1,1536]{1,0:T(1,128)S(1)}, f32[1,1536]{1,0:T(1,128)S(1)}, u32[]{:S(2)}, u32[]{:S(2)}) collective-permute-start(f32[1,1536]{1,0:T(1,128)S(1)} %get-tuple-element.14), channel_id=1, source_target_pairs={{0,8},{8,0},{1,9},{9,1},{2,10},{10,2},{3,11},{11,3},{4,12},{12,4},... | collective-permute-start | bytes 18440 | tf_op jit(solution)/shard_map/ppermute | solution.py:369
  388.8 19.4 %copy-start.2 = (s32[1024]{0:T(1024)S(1)}, s32[1024]{0:T(1024)}, u32[]{:S(2)}) copy-start(s32[1024]{0:T(1024)} %param.3) | copy-start | bytes 12292
  388.9 10.4 %collective-permute-start.5 = (f32[1,1536]{1,0:T(1,128)S(1)}, f32[1,1536]{1,0:T(1,128)S(1)}, u32[]{:S(2)}, u32[]{:S(2)}) collective-permute-start(f32[1,1536]{1,0:T(1,128)S(1)} %get-tuple-element.12), channel_id=1, source_target_pairs={{11,0},{8,1},{1,2},{2,3},{3,8},{0,9},{9,10},{10,11},{15,4},{12,5},... | collective-permute-start | bytes 18440 | tf_op jit(solution)/shard_map/ppermute | solution.py:371

commit v2 on v1

--- a/solution.py
+++ b/solution.py
@@ -54,7 +54,6 @@
         < lax.broadcasted_iota(jnp.int32, (step, step), 1)
     ).astype(jnp.bfloat16)
     total = jnp.zeros((128, 1), jnp.float32)
-    row_total = jnp.zeros((8, 128), jnp.float32)
     hots, ranks = [], []
     for first in range(0, ROWS, step):
         hot = kinds == cluster_ref[:, first : first + step]
@@ -62,9 +61,6 @@
         hots.append(hot)
         ranks.append(jnp.dot(hot16, before, preferred_element_type=jnp.float32) + total)
         total = total + jnp.sum(hot.astype(jnp.float32), axis=1, keepdims=True)
-        row_total = row_total + lax.dot_general(
-            jnp.ones((8, step), jnp.bfloat16), hot16, NT, preferred_element_type=jnp.float32
-        )
     one = lax.broadcasted_iota(jnp.int32, (128, 128), 0)
     other = lax.broadcasted_iota(jnp.int32, (128, 128), 1)
     earlier = ((one // CPG == other // CPG) & (other < one)).astype(jnp.bfloat16)
@@ -77,7 +73,14 @@
     for k, first in enumerate(range(0, ROWS, step)):
         place = jnp.sum(jnp.where(hots[k], ranks[k] + base, 0.0), axis=0, keepdims=True)
         place_ref[:, first : first + step] = place.astype(jnp.int32)
-    counts_ref[...] = row_total[:1].astype(jnp.int32)
+    group = lax.broadcasted_iota(jnp.int32, (GROUPS, 128), 0)
+    kind = lax.broadcasted_iota(jnp.int32, (GROUPS, 128), 1)
+    counts = jnp.dot(
+        (kind // CPG == group).astype(jnp.bfloat16),
+        jnp.where(one % CPG == other, total, 0.0).astype(jnp.bfloat16),
+        preferred_element_type=jnp.float32,
+    )
+    counts_ref[...] = counts.astype(jnp.int32)
 
 
 def placed(cluster):
@@ -85,7 +88,7 @@
         place_kernel,
         out_shape=(
             jax.ShapeDtypeStruct((1, ROWS), jnp.int32),
-            jax.ShapeDtypeStruct((1, 128), jnp.int32),
+            jax.ShapeDtypeStruct((GROUPS, 128), jnp.int32),
         ),
         compiler_params=params(),
         name="placed",
@@ -123,12 +126,11 @@
     )(rows, place)
 
 
-def limits(counts_ref, source, core, z, group):
-    device = ((source >> 1) * 2 + core) * 8 + (source & 1) * 4 + z
+def limits(counts_ref, source):
     ends = []
     end = jnp.int32(0)
     for k in range(CPG):
-        end = end + counts_ref[device, group * CPG + k]
+        end = end + counts_ref[source, k]
         ends.append(end)
     return ends
 
@@ -140,22 +142,18 @@
     return label
 
 
-def row_labels(counts_ref, first_source, sources, core, z, group):
+def row_labels(counts_ref, first_source, sources):
     slot = lax.broadcasted_iota(jnp.int32, (SLOTS, 1), 0)
     return jnp.concatenate(
-        [
-            label_of(slot, limits(counts_ref, first_source + s, core, z, group), -1)
-            for s in range(sources)
-        ],
-        axis=0,
-    )
-
-
-def column_labels(counts_ref, core, z, group):
+        [label_of(slot, limits(counts_ref, first_source + s), -1) for s in range(sources)], axis=0
+    )
+
+
+def column_labels(counts_ref):
     lane = lax.broadcasted_iota(jnp.int32, (1, WIDTH), 1)
     label = jnp.full((1, WIDTH), -2, jnp.int32)
     for s in range(GROUPS):
-        ends = limits(counts_ref, jnp.int32(s), core, z, group)
+        ends = limits(counts_ref, s)
         label = jnp.where(lane >= s * SLOTS, label_of(lane - s * SLOTS, ends, -2), label)
     return label
 
@@ -169,16 +167,15 @@
 CHUNK = 512
 
 
-def own_kernel(where_ref, counts_ref, rows_ref, own_ref, peer_ref, best_ref, labels):
-    group, core, z = where_ref[0], where_ref[1], where_ref[2]
+def own_kernel(own_counts, peer_counts, rows_ref, own_ref, peer_ref, best_ref, labels):
     step = pl.program_id(0)
 
     @pl.when(step == 0)
     def _():
-        labels[0:1, :] = column_labels(counts_ref, core, z, group)
-        labels[1:2, :] = column_labels(counts_ref, 1 - core, z, group)
-
-    mine = row_labels(counts_ref, step * SOURCES, SOURCES, core, z, group)
+        labels[0:1, :] = column_labels(own_counts)
+        labels[1:2, :] = column_labels(peer_counts)
+
+    mine = row_labels(own_counts, step * SOURCES, SOURCES)
     index = lax.broadcasted_iota(jnp.int32, (HEIGHT, 1), 0) + step * HEIGHT
     best = jnp.full((HEIGHT, 128), FLOOR, jnp.float32)
     rows = rows_ref[...]
@@ -197,7 +194,7 @@
     best_ref[...] = lanes_of(best)
 
 
-def own_best(where, counts, own, peer):
+def own_best(own_counts, peer_counts, own, peer):
     return pl.pallas_call(
         own_kernel,
         grid=(WIDTH // HEIGHT,),
@@ -216,28 +213,34 @@
             flops=4 * WIDTH * WIDTH * D, bytes_accessed=6 * WIDTH * D, transcendentals=0
         ),
         name="own_best",
-    )(where, counts, own, own, peer)
+    )(own_counts, peer_counts, own, own, peer)
 
 
 def far_kernel(
-    where_ref, counts_ref, own_ref, peer_ref, below_ref, above_ref, best_ref, above_best_ref, labels, column_best
+    own_counts,
+    peer_counts,
+    below_counts,
+    above_counts,
+    own_ref,
+    peer_ref,
+    below_ref,
+    above_ref,
+    best_ref,
+    above_best_ref,
+    labels,
+    column_best,
 ):
-    group, core, z = where_ref[0], where_ref[1], where_ref[2]
-    under, over, over_core = where_ref[3], where_ref[4], where_ref[5]
     step = pl.program_id(0)
     tiles = WIDTH // HEIGHT
     kind = step // tiles
 
     @pl.when(step == 0)
     def _():
-        labels[0:1, :] = column_labels(counts_ref, over_core, over, group)
+        labels[0:1, :] = column_labels(above_counts)
         column_best[...] = jnp.full(column_best.shape, FLOOR, jnp.float32)
 
-    row_core = jnp.where(kind == 1, 1 - core, core)
-    row_z = jnp.where(kind == 2, under, z)
-    mine = row_labels(counts_ref, (step - kind * tiles) * SOURCES, SOURCES, row_core, row_z, group)
-
-    def visit(rows_ref):
+    def visit(rows_ref, counts_ref):
+        mine = row_labels(counts_ref, (step - kind * tiles) * SOURCES, SOURCES)
         rows = rows_ref[...]
         best = jnp.full((HEIGHT, 128), FLOOR, jnp.float32)
         for first in range(0, WIDTH, CHUNK):
@@ -253,16 +256,16 @@
             )
         best_ref[...] = lanes_of(best)
 
-    pl.when(kind == 0)(lambda: visit(own_ref))
-    pl.when(kind == 1)(lambda: visit(peer_ref))
-    pl.when(kind == 2)(lambda: visit(below_ref))
+    pl.when(kind == 0)(lambda: visit(own_ref, own_counts))
+    pl.when(kind == 1)(lambda: visit(peer_ref, peer_counts))
+    pl.when(kind == 2)(lambda: visit(below_ref, below_counts))
 
     @pl.when(step == 3 * tiles - 1)
     def _():
         above_best_ref[...] = jnp.max(column_best[...], axis=0, keepdims=True)
 
 
-def far_best(where, counts, own, peer, below, above):
+def far_best(counts, own, peer, below, above):
     tiles = WIDTH // HEIGHT
 
     def block(kind):
@@ -274,6 +277,8 @@
         far_kernel,
         grid=(3 * tiles,),
         in_specs=[
+            pl.BlockSpec(memory_space=pltpu.SMEM),
+            pl.BlockSpec(memory_space=pltpu.SMEM),
             pl.BlockSpec(memory_space=pltpu.SMEM),
             pl.BlockSpec(memory_space=pltpu.SMEM),
             block(0),
@@ -295,7 +300,7 @@
             flops=6 * WIDTH * WIDTH * D, bytes_accessed=8 * WIDTH * D, transcendentals=0
         ),
         name="far_best",
-    )(where, counts, own, peer, below, above)
+    )(*counts, own, peer, below, above)
 
 
 def join_kernel(*refs):
@@ -342,31 +347,36 @@
     )(answers, cluster, place)
 
 
+SWAP = [(0, 1), (1, 0)]
+
+
+def all_to_plane(block):
+    return lax.all_to_all(block, PLANE, split_axis=0, concat_axis=0, tiled=True)
+
+
 def shards(embeddings, cluster):
-    group = lax.axis_index(PLANE)
-    core = lax.axis_index("c")
-    z = lax.axis_index("z")
-    crossed = (z == CROSSED[0]) | (z == CROSSED[1])
-    where = jnp.stack(
-        [group, core, z, (z + 3) % 4, (z + 1) % 4, jnp.where(crossed, 1 - core, core)]
-    ).astype(jnp.int32)
     cluster = cluster.reshape(1, ROWS)
     place, counts = placed(cluster)
-    counts = lax.all_gather(counts, AXES, tiled=True)
     sent = send_rows(embeddings, place)
-    own = lax.all_to_all(
-        sent.reshape(GROUPS, SLOTS, D), PLANE, split_axis=0, concat_axis=0, tiled=True
-    ).reshape(WIDTH, D)
+    own = all_to_plane(sent.reshape(GROUPS, SLOTS, D)).reshape(WIDTH, D)
     below = lax.ppermute(own, RING, to_above())
     above = lax.ppermute(own, RING, to_below())
-    peer = lax.ppermute(own, "c", [(0, 1), (1, 0)])
-    best_own = own_best(where, counts, own, peer)
-    best, best_above = far_best(where, counts, own, peer, below, above)
+    peer = lax.ppermute(own, "c", SWAP)
+    counts, own = lax.optimization_barrier((counts, own))
+    counts = all_to_plane(counts.reshape(GROUPS, 1, 128)).reshape(GROUPS, 128)
+    tables = (
+        counts,
+        lax.ppermute(counts, "c", SWAP),
+        lax.ppermute(counts, RING, to_above()),
+        lax.ppermute(counts, RING, to_below()),
+    )
+    best_own = own_best(tables[0], tables[1], own, peer)
+    best, best_above = far_best(tables, own, peer, below, above)
     best_far, best_peer, best_below = (best[:, k * WIDTH : (k + 1) * WIDTH] for k in range(3))
     answers = joined(
         best_own,
         best_far,
-        lax.ppermute(best_peer, "c", [(0, 1), (1, 0)]),
+        lax.ppermute(best_peer, "c", SWAP),
         lax.ppermute(best_below, RING, reverse(to_above())),
         lax.ppermute(best_above, RING, reverse(to_below())),
     )

time: 410 us -> 112 us (0.27)
  blocking collectives: 355 us -> 48.1 us
  waiting for transfers between devices: 0.02 us -> 22.5 us
  starting transfers between devices: 24.3 us -> 12.2 us
    all_gather x1 -> x0, blocking collectives: 317 us -> none  [shards(): counts = lax.all_gather(counts, AXES, tiled=True)]
    ppermute x2 -> x5, waiting for transfers between devices: 0.01 us -> 22.5 us  [the longest x1 19.1 us: shards(): lax.ppermute(counts, RING, to_below())]
    ppermute x2 -> x5, starting transfers between devices: 16.9 us -> 5.14 us  [the longest x1 4.49 us: shards(): lax.ppermute(counts, RING, to_below())]
    all_to_all x1 -> x2, blocking collectives: 29 us -> 38.3 us  [all_to_plane(): return lax.all_to_all(block, PLANE, split_axis=0, concat_axis=0, tiled=True)]
  transfers between devices with their start and end apart: 6 -> 9, of which waited for: 0 -> 2; matrix products, arithmetic and copies ran while one was open for 0% -> 0% of each run, Pallas kernels for 2% -> 7%
where the time goes in v2:
time: 112 us
  blocking collectives  48.1 us (43%)
  Pallas kernels  25.6 us (23%)
  waiting for transfers between devices  22.5 us (20%)
  starting transfers between devices  12.2 us (11%)
  local copies, waits for them, and re-layouts  3.06 us (3%)
    all_to_all x2, blocking collectives, all_to_plane(): return lax.all_to_all(block, PLANE, split_axis=0, concat_axis=0, tiled=True)  38.3 us
    ppermute x1, waiting for transfers between devices, shards(): lax.ppermute(counts, RING, to_below())  19.1 us
    pallas_call x1, Pallas kernels, far_best(): pl.pallas_call(far_kernel, grid=(3 * tiles,), in_specs=[pl.BlockSpec(memo...  13.2 us
    all_to_all x1, blocking collectives, shards(): lax.all_to_all(answers.reshape(GROUPS, 1, 128), PLANE, split_axis=0, conc...  9.79 us
    pallas_call x1, Pallas kernels, own_best(): pl.pallas_call(own_kernel, grid=(WIDTH // HEIGHT,), in_specs=[pl.BlockSpe...  7.88 us
    ppermute x1, starting transfers between devices, shards(): above = lax.ppermute(own, RING, to_below())  5.76 us
    ppermute x1, starting transfers between devices, shards(): lax.ppermute(counts, RING, to_below())  4.49 us
    ppermute x1, waiting for transfers between devices, shards(): lax.ppermute(counts, RING, to_above())  3.39 us
  transfers between devices with their start and end apart: 9, of which 2 were waited for; matrix products, arithmetic and copies ran while one was open for 0% of the time, Pallas kernels for 7%

profile of v2, /device:TPU:1, one launch (start us, length us, event | category | flops | bytes accessed | tf_op | source)
XLA Modules:
  0.0 111.6 jit_solution(4154614849988908288)
XLA Ops:
  0.0 0.0 copy-start.1
  0.0 0.7 copy-done.1
  0.7 0.5 placed.1
  1.2 0.0 copy-start
  1.2 1.2 %copy-done = bf16[1024,512]{1,0:T(8,128)(2,1)S(1)} copy-done((bf16[1024,512]{1,0:T(8,128)(2,1)S(1)}, bf16[1024,512]{1,0:T(8,128)(2,1)}, u32[]{:S(2)}) %copy-start) | copy-done | bytes 1048600
  2.4 3.0 %send_rows.1 = bf16[1536,512]{1,0:T(8,128)(2,1)S(1)} custom-call(bf16[1024,512]{1,0:T(8,128)(2,1)S(1)} %copy-done, s32[1,1024]{1,0:T(1,128)S(1)} %get-tuple-element.12.place_ref), custom_call_target="tpu_custom_call" | custom-call | tf_op jit(solution)/shard_map/send_rows/pallas_call | solution.py:114
  5.4 29.0 %all_to_all.15 = bf16[16,96,512]{2,1,0:T(8,128)(2,1)S(1)} all-to-all(bf16[16,96,512]{2,1,0:T(8,128)(2,1)S(1)} %bitcast.12), channel_id=1, replica_groups=mesh['yh'=2,'x'=4,'c'=2,'yl'=2,'z'=4] {'yh','x','yl'}, dimensions={0} | all-to-all | bytes 3145728 | tf_op jit(solution)/shard_map/all_to_all | solution.py:354
  34.4 5.8 %collective-permute-start.5 = (bf16[1536,512]{1,0:T(8,128)(2,1)S(1)}, bf16[1536,512]{1,0:T(8,128)(2,1)S(1)}, u32[]{:S(2)}, u32[]{:S(2)}) collective-permute-start(bf16[1536,512]{1,0:T(8,128)(2,1)S(1)} %bitcast.13), channel_id=1, source_target_pairs={{0,11},{1,8},{2,1},{3,2},{8,3},{9,0},{10,9},{11,10},{4,15},{5,12},... | collective-permute-start | bytes 4718600 | tf_op jit(solution)/shard_map/ppermute | solution.py:363
  40.1 0.0 collective-permute-start.4
  40.1 0.0 collective-permute-start.1
  40.1 9.4 %all_to_all.16 = s32[16,1,128]{2,1,0:T(1,128)S(1)} all-to-all(s32[16,1,128]{2,1,0:T(1,128)S(1)} %bitcast.28), channel_id=1, replica_groups=mesh['yh'=2,'x'=4,'c'=2,'yl'=2,'z'=4] {'yh','x','yl'}, dimensions={0} | all-to-all | bytes 16384 | tf_op jit(solution)/shard_map/all_to_all | solution.py:354
  49.5 4.5 %collective-permute-start.3 = (s32[16,128]{1,0:T(8,128)S(1)}, s32[16,128]{1,0:T(8,128)S(1)}, u32[]{:S(2)}, u32[]{:S(2)}) collective-permute-start(s32[16,128]{1,0:T(8,128)S(1)} %bitcast.23), channel_id=1, source_target_pairs={{0,11},{1,8},{2,1},{3,2},{8,3},{9,0},{10,9},{11,10},{4,15},{5,12},... | collective-permute-start | bytes 24584 | tf_op jit(solution)/shard_map/ppermute | solution.py:371
  54.0 0.0 collective-permute-start.2
  54.0 19.1 %collective-permute-done.3.above_counts = s32[16,128]{1,0:T(8,128)S(1)} collective-permute-done((s32[16,128]{1,0:T(8,128)S(1)}, s32[16,128]{1,0:T(8,128)S(1)}, u32[]{:S(2)}, u32[]{:S(2)}) %collective-permute-start.3) | collective-permute-done | bytes 8224 | tf_op jit(solution)/shard_map/ppermute | solution.py:371
  73.1 0.0 collective-permute-start
  73.1 3.4 %collective-permute-done.2.below_counts = s32[16,128]{1,0:T(8,128)S(1)} collective-permute-done((s32[16,128]{1,0:T(8,128)S(1)}, s32[16,128]{1,0:T(8,128)S(1)}, u32[]{:S(2)}, u32[]{:S(2)}) %collective-permute-start.2) | collective-permute-done | bytes 8224 | tf_op jit(solution)/shard_map/ppermute | solution.py:370
  76.5 0.0 collective-permute-done.peer_counts
  76.5 0.0 collective-permute-done.5.above_ref
  76.5 0.0 copy-start.3
  76.5 0.0 collective-permute-done.4.below_ref
  76.5 0.0 collective-permute-done.1.peer_ref
  76.5 1.1 %copy-done.3 = bf16[1536,512]{1,0:T(8,128)(2,1)} copy-done((bf16[1536,512]{1,0:T(8,128)(2,1)}, bf16[1536,512]{1,0:T(8,128)(2,1)S(1)}, u32[]{:S(2)}) %copy-start.3) | copy-done | bytes 1572888
  77.7 13.2 %far_best.1 = (f32[1,4608]{1,0:T(1,128)S(1)}, f32[1,1536]{1,0:T(1,128)S(1)}) custom-call(s32[16,128]{1,0:T(8,128)S(1)} %bitcast.26, s32[16,128]{1,0:T(8,128)S(1)} %collective-permute-done.peer_counts, s32[16,128]{1,0:T(8,128)S(1)} %collective-permute-done.2.below_counts, s32[16,128]{1,0:T(8,128)S(1)} %collective-permute-done.3.above_counts, ...), custom_call_target="tpu_custom_call" | custom-call | flops 7247757312 | bytes 6291456 | tf_op jit(solution)/shard_map/far_best/pallas_call | solution.py:276
  90.9 1.3 %collective-permute-start.7 = (f32[1,1536]{1,0:T(1,128)S(1)}, f32[1,1536]{1,0:T(1,128)S(1)}, u32[]{:S(2)}, u32[]{:S(2)}) collective-permute-start(f32[1,1536]{1,0:T(1,128)S(1)} %get-tuple-element.17), channel_id=1, source_target_pairs={{1,0},{2,1},{3,2},{0,3},{9,8},{10,9},{11,10},{8,11},{5,4},{6,5},{7... | collective-permute-start | bytes 18440 | tf_op jit(solution)/shard_map/ppermute | solution.py:380
  92.2 0.6 collective-permute-start.6
  92.8 0.0 copy-start.2
  92.8 0.0 collective-permute-start.8
  92.8 7.9 %own_best.1.refs_0_ = f32[1,1536]{1,0:T(1,128)S(1)} custom-call(s32[16,128]{1,0:T(8,128)S(1)} %bitcast.27, s32[16,128]{1,0:T(8,128)S(1)} %collective-permute-done.peer_counts, bf16[1536,512]{1,0:T(8,128)(2,1)S(1)} %bitcast.17, bf16[1536,512]{1,0:T(8,128)(2,1)S(1)} %bitcast.18, bf16[1536,512]{1,0:T(8,128)(2,1)S(1)} %collective-permute-done.1.peer_ref), custom_call_target="tpu_custom_call" | custom-call | flops 4831838208 | bytes 4718592 | tf_op jit(solution)/shard_map/own_best/pallas_call | solution.py:198
  100.7 0.0 collective-permute-done.7.refs_3_
  100.7 0.0 collective-permute-done.6.refs_2_
  100.7 0.0 collective-permute-done.8.refs_4_
  100.7 0.1 joined.1
  100.8 9.8 %all_to_all.17 = f32[16,1,128]{2,1,0:T(1,128)S(1)} all-to-all(f32[16,1,128]{2,1,0:T(1,128)S(1)} %bitcast.19), channel_id=1, replica_groups=mesh['yh'=2,'x'=4,'c'=2,'yl'=2,'z'=4] {'yh','x','yl'}, dimensions={0} | all-to-all | bytes 16384 | tf_op jit(solution)/shard_map/all_to_all | solution.py:383
  110.6 0.0 copy-done.2
  110.6 1.0 picked.1
  (1 shorter events, 0.0 us)
Async XLA Ops:
  0.0 0.7 copy-start.1
  1.2 1.2 %copy-start = (bf16[1024,512]{1,0:T(8,128)(2,1)S(1)}, bf16[1024,512]{1,0:T(8,128)(2,1)}, u32[]{:S(2)}) copy-start(bf16[1024,512]{1,0:T(8,128)(2,1)} %rows_ref.1) | copy-start | bytes 3145732
  34.4 42.1 %collective-permute-start.5 = (bf16[1536,512]{1,0:T(8,128)(2,1)S(1)}, bf16[1536,512]{1,0:T(8,128)(2,1)S(1)}, u32[]{:S(2)}, u32[]{:S(2)}) collective-permute-start(bf16[1536,512]{1,0:T(8,128)(2,1)S(1)} %bitcast.13), channel_id=1, source_target_pairs={{0,11},{1,8},{2,1},{3,2},{8,3},{9,0},{10,9},{11,10},{4,15},{5,12},... | collective-permute-start | bytes 4718600 | tf_op jit(solution)/shard_map/ppermute | solution.py:363
  40.1 36.4 %collective-permute-start.4 = (bf16[1536,512]{1,0:T(8,128)(2,1)S(1)}, bf16[1536,512]{1,0:T(8,128)(2,1)S(1)}, u32[]{:S(2)}, u32[]{:S(2)}) collective-permute-start(bf16[1536,512]{1,0:T(8,128)(2,1)S(1)} %bitcast.14), channel_id=1, source_target_pairs={{0,1},{1,2},{2,3},{3,0},{8,9},{9,10},{10,11},{11,8},{4,5},{5,6},{6... | collective-permute-start | bytes 4718600 | tf_op jit(solution)/shard_map/ppermute | solution.py:362
  40.1 36.4 %collective-permute-start.1 = (bf16[1536,512]{1,0:T(8,128)(2,1)S(1)}, bf16[1536,512]{1,0:T(8,128)(2,1)S(1)}, u32[]{:S(2)}, u32[]{:S(2)}) collective-permute-start(bf16[1536,512]{1,0:T(8,128)(2,1)S(1)} %bitcast.15), channel_id=1, source_target_pairs={{0,8},{8,0},{1,9},{9,1},{2,10},{10,2},{3,11},{11,3},{4,12},{12,4},... | collective-permute-start | bytes 4718600 | tf_op jit(solution)/shard_map/ppermute | solution.py:364
  49.5 23.6 %collective-permute-start.3 = (s32[16,128]{1,0:T(8,128)S(1)}, s32[16,128]{1,0:T(8,128)S(1)}, u32[]{:S(2)}, u32[]{:S(2)}) collective-permute-start(s32[16,128]{1,0:T(8,128)S(1)} %bitcast.23), channel_id=1, source_target_pairs={{0,11},{1,8},{2,1},{3,2},{8,3},{9,0},{10,9},{11,10},{4,15},{5,12},... | collective-permute-start | bytes 24584 | tf_op jit(solution)/shard_map/ppermute | solution.py:371
  54.0 22.5 %collective-permute-start.2 = (s32[16,128]{1,0:T(8,128)S(1)}, s32[16,128]{1,0:T(8,128)S(1)}, u32[]{:S(2)}, u32[]{:S(2)}) collective-permute-start(s32[16,128]{1,0:T(8,128)S(1)} %bitcast.24), channel_id=1, source_target_pairs={{0,1},{1,2},{2,3},{3,0},{8,9},{9,10},{10,11},{11,8},{4,5},{5,6},{6... | collective-permute-start | bytes 24584 | tf_op jit(solution)/shard_map/ppermute | solution.py:370
  73.1 3.4 %collective-permute-start = (s32[16,128]{1,0:T(8,128)S(1)}, s32[16,128]{1,0:T(8,128)S(1)}, u32[]{:S(2)}, u32[]{:S(2)}) collective-permute-start(s32[16,128]{1,0:T(8,128)S(1)} %bitcast.25), channel_id=1, source_target_pairs={{0,8},{8,0},{1,9},{9,1},{2,10},{10,2},{3,11},{11,3},{4,12},{12,4},... | collective-permute-start | bytes 24584 | tf_op jit(solution)/shard_map/ppermute | solution.py:369
  76.5 1.2 %copy-start.3 = (bf16[1536,512]{1,0:T(8,128)(2,1)}, bf16[1536,512]{1,0:T(8,128)(2,1)S(1)}, u32[]{:S(2)}) copy-start(bf16[1536,512]{1,0:T(8,128)(2,1)S(1)} %collective-permute-done.5.above_ref) | copy-start | bytes 4718596
  90.9 9.8 %collective-permute-start.7 = (f32[1,1536]{1,0:T(1,128)S(1)}, f32[1,1536]{1,0:T(1,128)S(1)}, u32[]{:S(2)}, u32[]{:S(2)}) collective-permute-start(f32[1,1536]{1,0:T(1,128)S(1)} %get-tuple-element.17), channel_id=1, source_target_pairs={{1,0},{2,1},{3,2},{0,3},{9,8},{10,9},{11,10},{8,11},{5,4},{6,5},{7... | collective-permute-start | bytes 18440 | tf_op jit(solution)/shard_map/ppermute | solution.py:380
  92.2 8.5 %collective-permute-start.6 = (f32[1,1536]{1,0:T(1,128)S(1)}, f32[1,1536]{1,0:T(1,128)S(1)}, u32[]{:S(2)}, u32[]{:S(2)}) collective-permute-start(f32[1,1536]{1,0:T(1,128)S(1)} %get-tuple-element.18), channel_id=1, source_target_pairs={{0,8},{8,0},{1,9},{9,1},{2,10},{10,2},{3,11},{11,3},{4,12},{12,4},... | collective-permute-start | bytes 18440 | tf_op jit(solution)/shard_map/ppermute | solution.py:379
  92.8 17.8 %copy-start.2 = (s32[1024]{0:T(1024)S(1)}, s32[1024]{0:T(1024)}, u32[]{:S(2)}) copy-start(s32[1024]{0:T(1024)} %param.3) | copy-start | bytes 12292
  92.8 7.9 %collective-permute-start.8 = (f32[1,1536]{1,0:T(1,128)S(1)}, f32[1,1536]{1,0:T(1,128)S(1)}, u32[]{:S(2)}, u32[]{:S(2)}) collective-permute-start(f32[1,1536]{1,0:T(1,128)S(1)} %get-tuple-element.16), channel_id=1, source_target_pairs={{11,0},{8,1},{1,2},{2,3},{3,8},{0,9},{9,10},{10,11},{15,4},{12,5},... | collective-permute-start | bytes 18440 | tf_op jit(solution)/shard_map/ppermute | solution.py:381

commit v3 on v2

v3 whole, which is shorter than its diff:
```python
import math

import jax
import jax.numpy as jnp
from jax import lax
from jax.experimental import pallas as pl
from jax.experimental.pallas import tpu as pltpu
from jax.sharding import Mesh, PartitionSpec as P

CPG = 4
GROUPS = 16
SLOTS = 96
ROWS = 1024
D = 512
LANES = 128
FEATURE_PARTS = D // LANES
PIECES = 3
SHARE = SLOTS // PIECES
PIECE = FEATURE_PARTS * SHARE
TAIL = 16
BLOCK = PIECES * PIECE + TAIL
EARLY = (PIECES - 1) * PIECE
EARLY_BLOCK = PIECE + TAIL
HEIGHT = GROUPS * SHARE
WIDTH = GROUPS * SLOTS
FLOOR = -4.0

SIZES = {"yh": 2, "x": 4, "c": 2, "yl": 2, "z": 4}
AXES = ("yh", "x", "c", "yl", "z")
PLANE = ("yh", "x", "yl")
RING = ("c", "z")
NT = (((1,), (1,)), ((), ()))
VMEM_LIMIT = 48 * 1024 * 1024

CROSSED = (0, 3)


def to_above():
    return [(c * 4 + z, c * 4 + (z + 1) % 4) for c in range(2) for z in range(4)]


def to_below():
    pairs = []
    for c in range(2):
        for z in range(4):
            lands = (z - 1) % 4
            pairs.append((c * 4 + z, (c ^ 1 if lands in CROSSED else c) * 4 + lands))
    return pairs


def reverse(pairs):
    return [(b, a) for a, b in pairs]


def params():
    return pltpu.CompilerParams(vmem_limit_bytes=VMEM_LIMIT)


def place_kernel(cluster_ref, place_ref, ends_ref):
    step = 256
    kinds = lax.broadcasted_iota(jnp.int32, (128, step), 0)
    before = (
        lax.broadcasted_iota(jnp.int32, (step, step), 0)
        < lax.broadcasted_iota(jnp.int32, (step, step), 1)
    ).astype(jnp.bfloat16)
    total = jnp.zeros((128, 1), jnp.float32)
    hots, ranks = [], []
    for first in range(0, ROWS, step):
        hot = kinds == cluster_ref[:, first : first + step]
        hot16 = hot.astype(jnp.bfloat16)
        hots.append(hot)
        ranks.append(jnp.dot(hot16, before, preferred_element_type=jnp.float32) + total)
        total = total + jnp.sum(hot.astype(jnp.float32), axis=1, keepdims=True)
    one = lax.broadcasted_iota(jnp.int32, (128, 128), 0)
    other = lax.broadcasted_iota(jnp.int32, (128, 128), 1)
    earlier = ((one // CPG == other // CPG) & (other < one)).astype(jnp.bfloat16)
    base = jnp.dot(
        earlier,
        jnp.broadcast_to(total, (128, 128)).astype(jnp.bfloat16),
        preferred_element_type=jnp.float32,
    )[:, :1]
    base = base + (lax.broadcasted_iota(jnp.int32, (128, 1), 0) // CPG * SLOTS).astype(jnp.float32)
    for k, first in enumerate(range(0, ROWS, step)):
        place = jnp.sum(jnp.where(hots[k], ranks[k] + base, 0.0), axis=0, keepdims=True)
        place_ref[:, first : first + step] = place.astype(jnp.int32)
    group = lax.broadcasted_iota(jnp.int32, (GROUPS, 128), 0)
    kind = lax.broadcasted_iota(jnp.int32, (GROUPS, 128), 1)
    ends = jnp.dot(
        (kind // CPG == group).astype(jnp.bfloat16),
        jnp.where(one % CPG <= other, total, 0.0).astype(jnp.bfloat16),
        preferred_element_type=jnp.float32,
    )
    ends = jnp.where(kind < CPG, ends, 512.0)
    ends_ref[...] = jnp.broadcast_to(ends[:, None, :], ends_ref.shape).astype(jnp.bfloat16)


def placed(cluster):
    return pl.pallas_call(
        place_kernel,
        out_shape=(
            jax.ShapeDtypeStruct((1, ROWS), jnp.int32),
            jax.ShapeDtypeStruct((GROUPS, TAIL, LANES), jnp.bfloat16),
        ),
        compiler_params=params(),
        name="placed",
    )(cluster)


def send_kernel(rows_ref, place_ref, ends_ref, out_ref, early_ref, unit):
    step = pl.program_id(0)

    @pl.when(step == 0)
    def _():
        values = rows_ref[...].astype(jnp.float32)
        mean = jnp.mean(values * values, axis=1, keepdims=True)
        scale = lax.rsqrt(mean + 1e-06) / math.sqrt(D)
        unit[...] = (values * scale).astype(jnp.bfloat16)

    number = out_ref.shape[0]
    height = number * SLOTS
    slot = lax.broadcasted_iota(jnp.int32, (height, ROWS), 0) + step * height
    hot = (slot == place_ref[...]).astype(jnp.bfloat16)
    rows = jnp.dot(hot, unit[...], preferred_element_type=jnp.float32).astype(jnp.bfloat16)
    rows = rows.reshape(number, SLOTS, D)
    for k in range(PIECES):
        for part in range(FEATURE_PARTS):
            first = k * PIECE + part * SHARE
            out_ref[:, first : first + SHARE] = rows[
                :, k * SHARE : (k + 1) * SHARE, part * LANES : (part + 1) * LANES
            ]
    out_ref[:, PIECES * PIECE :] = ends_ref[...]
    early_ref[...] = out_ref[:, EARLY:]


def send_rows(rows, place, ends):
    number = 4
    return pl.pallas_call(
        send_kernel,
        grid=(GROUPS // number,),
        in_specs=[
            pl.BlockSpec((ROWS, D), lambda i: (0, 0)),
            pl.BlockSpec((1, ROWS), lambda i: (0, 0)),
            pl.BlockSpec((number, TAIL, LANES), lambda i: (i, 0, 0)),
        ],
        out_specs=(
            pl.BlockSpec((number, BLOCK, LANES), lambda i: (i, 0, 0)),
            pl.BlockSpec((number, EARLY_BLOCK, LANES), lambda i: (i, 0, 0)),
        ),
        out_shape=(
            jax.ShapeDtypeStruct((GROUPS, BLOCK, LANES), jnp.bfloat16),
            jax.ShapeDtypeStruct((GROUPS, EARLY_BLOCK, LANES), jnp.bfloat16),
        ),
        scratch_shapes=[pltpu.VMEM((ROWS, D), jnp.bfloat16)],
        compiler_params=params(),
        name="send_rows",
    )(rows, place, ends)


def labels_of(ends, number, empty):
    slot = lax.broadcasted_iota(jnp.int32, (GROUPS, SHARE, LANES), 1) + number * SHARE
    past = jnp.where(slot.astype(jnp.float32) >= ends[:, :1].astype(jnp.float32), 1.0, 0.0)
    label = jnp.sum(past, axis=2, keepdims=True).reshape(HEIGHT, 1)
    return jnp.where(label >= CPG, empty, label)


def row_labels(ends, number):
    return labels_of(ends, number, 5.0)


def column_labels(ends, number):
    label = labels_of(ends, number, 6.0)
    return jnp.broadcast_to(label, (HEIGHT, LANES)).T[:1]


def piece_of(ref, first):
    return jnp.concatenate(
        [
            ref[:, pl.ds(first + part * SHARE, SHARE)].reshape(HEIGHT, LANES)
            for part in range(FEATURE_PARTS)
        ],
        axis=1,
    )


def lanes_of(best):
    return jnp.max(best.T, axis=0, keepdims=True)


def span(number):
    return slice(number * HEIGHT, (number + 1) * HEIGHT)


def scored(rows, mine, columns, labels, numbers, column_best, index=None):
    best = jnp.full((HEIGHT, LANES), FLOOR, jnp.float32)
    for number in numbers:
        score = lax.dot_general(rows, columns[number], NT, preferred_element_type=jnp.float32)
        match = mine == labels[:, span(number)]
        if index is not None:
            column = lax.broadcasted_iota(jnp.int32, (1, HEIGHT), 1) + number * HEIGHT
            match = match & (index != column)
        score = jnp.where(match, score, FLOOR)
        for k in range(0, HEIGHT, LANES):
            best = jnp.maximum(best, score[:, k : k + LANES])
        if column_best is not None:
            column_best[:, span(number)] = jnp.maximum(
                column_best[:, span(number)],
                jnp.max(score.reshape(HEIGHT // 8, 8, HEIGHT), axis=0),
            )
    return best


def own_kernel(own_ref, peer_ref, best_ref, columns, labels):
    own_ends = own_ref[:, PIECES * PIECE :]
    peer_ends = peer_ref[:, PIECES * PIECE :]
    for number in range(PIECES):
        columns[0, number] = piece_of(own_ref, number * PIECE)
        columns[1, number] = piece_of(peer_ref, number * PIECE)
        labels[0:1, span(number)] = column_labels(own_ends, number)
        labels[1:2, span(number)] = column_labels(peer_ends, number)

    def visit(number, _):
        rows = columns[0, number]
        mine = row_labels(own_ends, number)
        index = lax.broadcasted_iota(jnp.int32, (HEIGHT, 1), 0) + number * HEIGHT
        best = jnp.maximum(
            scored(rows, mine, columns.at[0], labels.at[0:1], range(PIECES), None, index),
            scored(rows, mine, columns.at[1], labels.at[1:2], range(PIECES), None),
        )
        best_ref[number] = lanes_of(best)
        return 0

    lax.fori_loop(0, PIECES, visit, 0)


def estimate(pairs):
    return pl.CostEstimate(
        flops=2 * pairs * HEIGHT * HEIGHT * D, bytes_accessed=8 * WIDTH * D, transcendentals=0
    )


BEST = jax.ShapeDtypeStruct((PIECES, 1, HEIGHT), jnp.float32)


def own_best(own, peer):
    return pl.pallas_call(
        own_kernel,
        out_shape=BEST,
        scratch_shapes=[
            pltpu.VMEM((2, PIECES, HEIGHT, D), jnp.bfloat16),
            pltpu.VMEM((8, WIDTH), jnp.float32),
        ],
        compiler_params=params(),
        cost_estimate=estimate(18),
        name="own_best",
    )(own, peer)


def near_kernel(
    own_ref,
    peer_ref,
    below_ref,
    above_ref,
    early_ref,
    old_ref,
    best_ref,
    peer_best_ref,
    below_best_ref,
    above_best_ref,
    columns,
    labels,
    column_best,
):
    above_ends = early_ref[:, EARLY_BLOCK + PIECE :]
    below_ends = early_ref[:, PIECE:EARLY_BLOCK]
    columns[0] = piece_of(above_ref, 0)
    columns[2] = piece_of(early_ref, EARLY_BLOCK)
    for number in (0, 2):
        labels[0:1, span(number)] = column_labels(above_ends, number)
    column_best[...] = jnp.full(column_best.shape, FLOOR, jnp.float32)

    def visit(rows, ends, number):
        mine = row_labels(ends, number)
        return lanes_of(scored(rows, mine, columns, labels.at[0:1], (0, 2), column_best))

    def one(number, _):
        first = pl.multiple_of(number * PIECE, PIECE)
        found = visit(piece_of(own_ref, first), own_ref[:, PIECES * PIECE :], number)
        best_ref[number] = jnp.maximum(found, old_ref[number])
        found = visit(piece_of(peer_ref, first), peer_ref[:, PIECES * PIECE :], number)
        peer_best_ref[number] = found
        return 0

    lax.fori_loop(0, PIECES, one, 0)
    below_best_ref[0] = visit(piece_of(below_ref, 0), below_ends, 0)
    below_best_ref[1] = jnp.full((1, HEIGHT), FLOOR, jnp.float32)
    below_best_ref[2] = visit(piece_of(early_ref, 0), below_ends, 2)
    for number in range(PIECES):
        above_best_ref[number] = jnp.max(column_best[:, span(number)], axis=0, keepdims=True)


def near_best(own, peer, below, above, early, old):
    return pl.pallas_call(
        near_kernel,
        out_shape=(BEST,) * 4,
        scratch_shapes=[
            pltpu.VMEM((PIECES, HEIGHT, D), jnp.bfloat16),
            pltpu.VMEM((8, WIDTH), jnp.float32),
            pltpu.VMEM((8, WIDTH), jnp.float32),
        ],
        compiler_params=params(),
        cost_estimate=estimate(16),
        name="near_best",
    )(own, peer, below, above, early, old)


def last_kernel(
    own_ref,
    peer_ref,
    below_ref,
    above_ref,
    below_late_ref,
    above_late_ref,
    early_ref,
    old_ref,
    old_peer_ref,
    old_below_ref,
    old_above_ref,
    best_ref,
    peer_best_ref,
    below_best_ref,
    above_best_ref,
    columns,
    labels,
    column_best,
):
    above_ends = early_ref[:, EARLY_BLOCK + PIECE :]
    below_ends = early_ref[:, PIECE:EARLY_BLOCK]
    columns[0] = piece_of(above_ref, 0)
    columns[1] = piece_of(above_late_ref, 0)
    columns[2] = piece_of(early_ref, EARLY_BLOCK)
    for number in range(PIECES):
        labels[0:1, span(number)] = column_labels(above_ends, number)
    column_best[...] = jnp.full(column_best.shape, FLOOR, jnp.float32)

    def visit(rows, ends, number, numbers=(1,)):
        mine = row_labels(ends, number)
        return lanes_of(scored(rows, mine, columns, labels.at[0:1], numbers, column_best))

    def one(number, _):
        first = pl.multiple_of(number * PIECE, PIECE)
        found = visit(piece_of(own_ref, first), own_ref[:, PIECES * PIECE :], number)
        best_ref[number] = jnp.maximum(found, old_ref[number])
        found = visit(piece_of(peer_ref, first), peer_ref[:, PIECES * PIECE :], number)
        peer_best_ref[number] = jnp.maximum(found, old_peer_ref[number])
        return 0

    lax.fori_loop(0, PIECES, one, 0)
    found = visit(piece_of(below_ref, 0), below_ends, 0)
    below_best_ref[0] = jnp.maximum(found, old_below_ref[0])
    below_best_ref[1] = visit(piece_of(below_late_ref, 0), below_ends, 1, range(PIECES))
    found = visit(piece_of(early_ref, 0), below_ends, 2)
    below_best_ref[2] = jnp.maximum(found, old_below_ref[2])
    for number in range(PIECES):
        found = jnp.max(column_best[:, span(number)], axis=0, keepdims=True)
        above_best_ref[number] = jnp.maximum(found, old_above_ref[number])


def last_best(*arrays):
    return pl.pallas_call(
        last_kernel,
        out_shape=(BEST,) * 4,
        scratch_shapes=[
            pltpu.VMEM((PIECES, HEIGHT, D), jnp.bfloat16),
            pltpu.VMEM((8, WIDTH), jnp.float32),
            pltpu.VMEM((8, WIDTH), jnp.float32),
        ],
        compiler_params=params(),
        cost_estimate=estimate(11),
        name="last_best",
    )(*arrays)


def join_kernel(*refs):
    best = refs[0][...]
    for ref in refs[1:-1]:
        best = jnp.maximum(best, ref[...])
    out_ref = refs[-1]
    out_ref[...] = jnp.zeros(out_ref.shape, jnp.float32)
    for k in range(PIECES):
        for s in range(GROUPS):
            out_ref[s : s + 1, k * SHARE : (k + 1) * SHARE] = best[k, :, s * SHARE : (s + 1) * SHARE]


def joined(*parts):
    return pl.pallas_call(
        join_kernel,
        out_shape=jax.ShapeDtypeStruct((GROUPS, 128), jnp.float32),
        compiler_params=params(),
        name="joined",
    )(*parts)


def pick_kernel(answers_ref, cluster_ref, place_ref, out_ref):
    group = cluster_ref[...] // CPG
    slot = place_ref[...] - group * SLOTS
    hot = (lax.broadcasted_iota(jnp.int32, (GROUPS, ROWS), 0) == group).astype(jnp.bfloat16)
    rest = answers_ref[...]
    found = jnp.zeros((128, ROWS), jnp.float32)
    for _ in range(3):
        part = rest.astype(jnp.bfloat16)
        rest = rest - part.astype(jnp.float32)
        found = found + lax.dot_general(
            part, hot, (((0,), (0,)), ((), ())), preferred_element_type=jnp.float32
        )
    here = lax.broadcasted_iota(jnp.int32, (128, ROWS), 0) == slot
    out_ref[...] = jnp.sum(jnp.where(here, found, 0.0), axis=0, keepdims=True)


def picked(answers, cluster, place):
    return pl.pallas_call(
        pick_kernel,
        out_shape=jax.ShapeDtypeStruct((1, ROWS), jnp.float32),
        compiler_params=params(),
        name="picked",
    )(answers, cluster, place)


SWAP = [(0, 1), (1, 0)]


def all_to_plane(block):
    return lax.all_to_all(block, PLANE, split_axis=0, concat_axis=0, tiled=True)


def shards(embeddings, cluster):
    cluster = cluster.reshape(1, ROWS)
    place, ends = placed(cluster)
    sent, early = send_rows(embeddings, place, ends)
    early = jnp.concatenate(
        [lax.ppermute(early, RING, to_above()), lax.ppermute(early, RING, to_below())], axis=1
    )
    own = all_to_plane(sent)
    late = [own[:, k * PIECE : (k + 1) * PIECE] for k in range(PIECES - 1)]
    below = [lax.ppermute(block, RING, to_above()) for block in late]
    above = [lax.ppermute(block, RING, to_below()) for block in late]
    early, own = lax.optimization_barrier((early, own))
    peer = lax.ppermute(own, "c", SWAP)
    early = all_to_plane(early)
    best = own_best(own, peer)
    bests = near_best(own, peer, below[0], above[0], early, best)
    best, best_peer, best_below, best_above = last_best(
        own, peer, below[0], above[0], below[1], above[1], early, *bests
    )
    answers = joined(
        best,
        lax.ppermute(best_peer, "c", SWAP),
        lax.ppermute(best_below, RING, reverse(to_above())),
        lax.ppermute(best_above, RING, reverse(to_below())),
    )
    answers = lax.all_to_all(
        answers.reshape(GROUPS, 1, 128), PLANE, split_axis=0, concat_axis=0, tiled=True
    ).reshape(GROUPS, 128)
    return picked(answers, cluster, place).reshape(ROWS)


def solution(mesh):
    devices = mesh.devices.reshape(tuple(SIZES[a] for a in AXES))
    inner = Mesh(devices, AXES)
    return jax.shard_map(
        shards,
        mesh=inner,
        in_specs=(P(AXES, None), P(AXES)),
        out_specs=P(AXES),
        check_vma=False,
    )
```

time: 112 us -> 101 us (0.902)
  blocking collectives: 48.1 us -> 11 us
  starting transfers between devices: 12.2 us -> 27.7 us
  waiting for transfers between devices: 22.5 us -> 27.1 us
  Pallas kernels: 25.6 us -> 28.8 us
  local copies, waits for them, and re-layouts: 3.06 us -> 4.71 us
    all_to_all x2 -> x0, blocking collectives: 38.3 us -> none  [all_to_plane(): return lax.all_to_all(block, PLANE, split_axis=0, concat_axis=0, tiled=True)]
    all_to_all x0 -> x2, starting transfers between devices: none -> 11.3 us  [all_to_plane(): return lax.all_to_all(block, PLANE, split_axis=0, concat_axis=0, tiled=True)]
    ppermute x1, waiting for transfers between devices: 0.01 us -> 3.49 us  [shards(): lax.ppermute(best_above, RING, reverse(to_below()))]
    all_to_all x0 -> x2, waiting for transfers between devices: none -> 3.47 us  [all_to_plane(): return lax.all_to_all(block, PLANE, split_axis=0, concat_axis=0, tiled=True)]
    ppermute x5 -> x6, waiting for transfers between devices: 22.5 us -> 19.4 us  [the longest x1 12.9 us: shards(): lax.ppermute(early, RING, to_below())]
    pallas_call x3 -> x4, Pallas kernels: 24.1 us -> 27.2 us  [the longest x1 9.27 us: own_best(): pl.pallas_call(own_kernel, out_shape=BEST, scratch_shapes=[pltpu.VMEM((2,...]
    ppermute x5 -> x6, starting transfers between devices: 10.3 us -> 11.6 us  [the longest x2 6.97 us: shards(): above = [lax.ppermute(block, RING, to_below()) for block in late]]
    all_to_all x1, blocking collectives: 9.79 us -> 11 us  [shards(): lax.all_to_all(answers.reshape(GROUPS, 1, 128), PLANE, split_axis=0, conc...]
  transfers between devices with their start and end apart: 9 -> 12, of which waited for: 2 -> 8; matrix products, arithmetic and copies ran while one was open for 0% -> 2% of each run, Pallas kernels for 7% -> 17%
where the time goes in v3:
time: 101 us; the launch traced here: 100 us
  Pallas kernels  28.8 us (29%)
  starting transfers between devices  27.7 us (27%)
  waiting for transfers between devices  27.1 us (27%)
  blocking collectives  11 us (11%)
  local copies, waits for them, and re-layouts  4.71 us (5%)
  other arithmetic  1.11 us (1%)
    ppermute x1, waiting for transfers between devices, shards(): lax.ppermute(early, RING, to_below())  12.9 us
    all_to_all x2, starting transfers between devices, all_to_plane(): return lax.all_to_all(block, PLANE, split_axis=0, concat_axis=0, tiled=True)  11.3 us
    all_to_all x1, blocking collectives, shards(): lax.all_to_all(answers.reshape(GROUPS, 1, 128), PLANE, split_axis=0, conc...  11 us
    pallas_call x1, Pallas kernels, own_best(): pl.pallas_call(own_kernel, out_shape=BEST, scratch_shapes=[pltpu.VMEM((2,...  9.27 us
    pallas_call x1, Pallas kernels, near_best(): pl.pallas_call(near_kernel, out_shape=(BEST,) * 4, scratch_shapes=[pltpu....  7.73 us
    ppermute x2, starting transfers between devices, shards(): above = [lax.ppermute(block, RING, to_below()) for block in late]  6.97 us
    pallas_call x1, Pallas kernels, last_best(): pl.pallas_call(last_kernel, out_shape=(BEST,) * 4, scratch_shapes=[pltpu....  6.54 us
    ppermute x1, starting transfers between devices, shards(): lax.ppermute(early, RING, to_below())  4.66 us
  transfers between devices with their start and end apart: 12, of which 8 were waited for; matrix products, arithmetic and copies ran while one was open for 2% of the time, Pallas kernels for 17%

profile of v3, /device:TPU:1, one launch (start us, length us, event | category | flops | bytes accessed | tf_op | source)
XLA Modules:
  0.0 100.4 jit_solution(4159690575320693715)
XLA Ops:
  0.0 0.0 copy-start.1
  0.0 0.7 copy-done.1
  0.7 0.5 placed.1
  1.2 0.0 copy-start
  1.2 1.2 %copy-done = bf16[1024,512]{1,0:T(8,128)(2,1)S(1)} copy-done((bf16[1024,512]{1,0:T(8,128)(2,1)S(1)}, bf16[1024,512]{1,0:T(8,128)(2,1)}, u32[]{:S(2)}) %copy-start) | copy-done | bytes 1048600
  2.4 3.6 %send_rows.1 = (bf16[16,400,128]{2,1,0:T(8,128)(2,1)}, bf16[16,144,128]{2,1,0:T(8,128)(2,1)S(1)}) custom-call(bf16[1024,512]{1,0:T(8,128)(2,1)S(1)} %copy-done, s32[1,1024]{1,0:T(1,128)S(1)} %get-tuple-element.19.place_ref, bf16[16,16,128]{2,1,0:T(8,128)(2,1)S(1)} %get-tuple-element.20.ends_ref), custom_call_target="tpu_custom_call" | custom-call | tf_op jit(solution)/shard_map/send_rows/pallas_call | solution.py:137
  6.0 7.6 %all-to-all-start = ((bf16[16,400,128]{2,1,0:T(8,128)(2,1)}), bf16[16,400,128]{2,1,0:T(8,128)(2,1)S(1)}, u32[]{:S(2)}, u32[]{:S(2)}) async-start(bf16[16,400,128]{2,1,0:T(8,128)(2,1)} %get-tuple-element.22), calls=%async_computation | async-start | bytes 3276800 | tf_op jit(solution)/shard_map/all_to_all | solution.py:432
  13.6 4.7 %collective-permute-start.1 = (bf16[16,144,128]{2,1,0:T(8,128)(2,1)S(1)}, bf16[16,144,128]{2,1,0:T(8,128)(2,1)S(1)}, u32[]{:S(2)}, u32[]{:S(2)}) collective-permute-start(bf16[16,144,128]{2,1,0:T(8,128)(2,1)S(1)} %get-tuple-element.21), channel_id=1, source_target_pairs={{0,11},{1,8},{2,1},{3,2},{8,3},{9,0},{10,9},{11,10},{4,15},{5,12},... | collective-permute-start | bytes 1769480 | tf_op jit(solution)/shard_map/ppermute | solution.py:440
  18.3 0.0 collective-permute-start
  18.3 12.9 %collective-permute-done.1 = bf16[16,144,128]{2,1,0:T(8,128)(2,1)S(1)} collective-permute-done((bf16[16,144,128]{2,1,0:T(8,128)(2,1)S(1)}, bf16[16,144,128]{2,1,0:T(8,128)(2,1)S(1)}, u32[]{:S(2)}, u32[]{:S(2)}) %collective-permute-start.1) | collective-permute-done | bytes 589856 | tf_op jit(solution)/shard_map/ppermute | solution.py:440
  31.2 3.7 %collective-permute-done = bf16[16,144,128]{2,1,0:T(8,128)(2,1)S(1)} collective-permute-done((bf16[16,144,128]{2,1,0:T(8,128)(2,1)S(1)}, bf16[16,144,128]{2,1,0:T(8,128)(2,1)S(1)}, u32[]{:S(2)}, u32[]{:S(2)}) %collective-permute-start) | collective-permute-done | bytes 589856 | tf_op jit(solution)/shard_map/ppermute | solution.py:440
  34.8 1.1 %pad_maximum_fusion = bf16[16,288,128]{2,1,0:T(8,128)(2,1)} fusion(bf16[16,144,128]{2,1,0:T(8,128)(2,1)S(1)} %collective-permute-done.1, bf16[16,144,128]{2,1,0:T(8,128)(2,1)S(1)} %collective-permute-done), kind=kLoop, calls=%fused_computation | loop fusion | flops 2359296 | bytes 2359296 | tf_op jit(solution)/shard_map/concatenate | solution.py:439
  35.9 3.0 %all-to-all-done.own_ref = bf16[16,400,128]{2,1,0:T(8,128)(2,1)S(1)} async-done(((bf16[16,400,128]{2,1,0:T(8,128)(2,1)}), bf16[16,400,128]{2,1,0:T(8,128)(2,1)S(1)}, u32[]{:S(2)}, u32[]{:S(2)}) %all-to-all-start) | async-done | bytes 1638432 | tf_op jit(solution)/shard_map/all_to_all | solution.py:432
  39.0 1.1 %collective-permute-start.2 = (bf16[16,400,128]{2,1,0:T(8,128)(2,1)S(1)}, bf16[16,400,128]{2,1,0:T(8,128)(2,1)}, u32[]{:S(2)}, u32[]{:S(2)}) collective-permute-start(bf16[16,400,128]{2,1,0:T(8,128)(2,1)S(1)} %all-to-all-done.own_ref), channel_id=1, source_target_pairs={{0,8},{8,0},{1,9},{9,1},{2,10},{10,2},{3,11},{11,3},{4,12},{12,4},... | collective-permute-start | bytes 4915208 | tf_op jit(solution)/shard_map/ppermute | solution.py:447
  40.1 3.7 %all-to-all-start.1 = ((bf16[16,288,128]{2,1,0:T(8,128)(2,1)}), bf16[16,288,128]{2,1,0:T(8,128)(2,1)S(1)}, u32[]{:S(2)}, u32[]{:S(2)}) async-start(bf16[16,288,128]{2,1,0:T(8,128)(2,1)} %pad_maximum_fusion), calls=%async_computation.1 | async-start | bytes 2359296 | tf_op jit(solution)/shard_map/all_to_all | solution.py:432
  43.8 0.9 fusion
  44.8 3.6 %collective-permute-start.4 = (bf16[16,128,128]{2,1,0:T(8,128)(2,1)S(1)}, bf16[16,128,128]{2,1,0:T(8,128)(2,1)S(1)}, u32[]{:S(2)}, u32[]{:S(2)}) collective-permute-start(bf16[16,128,128]{2,1,0:T(8,128)(2,1)S(1)} %get-tuple-element.34), channel_id=1, source_target_pairs={{0,11},{1,8},{2,1},{3,2},{8,3},{9,0},{10,9},{11,10},{4,15},{5,12},... | collective-permute-start | bytes 1572872 | tf_op jit(solution)/shard_map/ppermute | solution.py:445
  48.4 0.0 collective-permute-start.3
  48.4 3.3 %collective-permute-start.6 = (bf16[16,128,128]{2,1,0:T(8,128)(2,1)}, bf16[16,128,128]{2,1,0:T(8,128)(2,1)}, u32[]{:S(2)}, u32[]{:S(2)}) collective-permute-start(bf16[16,128,128]{2,1,0:T(8,128)(2,1)} %get-tuple-element.33), channel_id=1, source_target_pairs={{0,11},{1,8},{2,1},{3,2},{8,3},{9,0},{10,9},{11,10},{4,15},{5,12},... | collective-permute-start | bytes 1572872 | tf_op jit(solution)/shard_map/ppermute | solution.py:445
  51.7 0.0 collective-permute-start.5
  51.7 0.0 collective-permute-done.2.peer_ref
  51.8 9.3 %own_best.1.old_ref = f32[3,1,512]{2,1,0:T(1,128)S(1)} custom-call(bf16[16,400,128]{2,1,0:T(8,128)(2,1)S(1)} %all-to-all-done.own_ref, bf16[16,400,128]{2,1,0:T(8,128)(2,1)} %collective-permute-done.2.peer_ref), custom_call_target="tpu_custom_call" | custom-call | flops 4831838208 | bytes 6291456 | tf_op jit(solution)/shard_map/own_best/pallas_call | solution.py:245
  61.0 0.0 collective-permute-done.4.above_ref
  61.0 1.5 %collective-permute-done.3.below_ref = bf16[16,128,128]{2,1,0:T(8,128)(2,1)S(1)} collective-permute-done((bf16[16,128,128]{2,1,0:T(8,128)(2,1)S(1)}, bf16[16,128,128]{2,1,0:T(8,128)(2,1)S(1)}, u32[]{:S(2)}, u32[]{:S(2)}) %collective-permute-start.3) | collective-permute-done | bytes 524320 | tf_op jit(solution)/shard_map/ppermute | solution.py:444
  62.6 0.0 copy-start.3
  62.6 0.8 copy-done.3
  63.4 0.4 all-to-all-done.1.early_ref
  63.8 0.0 copy-start.4
  63.8 1.0 %copy-done.4 = bf16[16,128,128]{2,1,0:T(8,128)(2,1)S(1)} copy-done((bf16[16,128,128]{2,1,0:T(8,128)(2,1)S(1)}, bf16[16,128,128]{2,1,0:T(8,128)(2,1)}, u32[]{:S(2)}) %copy-start.4) | copy-done | bytes 524312
  64.9 0.0 copy-start.5
  64.9 7.7 %near_best.1 = (f32[3,1,512]{2,1,0:T(1,128)S(1)}, f32[3,1,512]{2,1,0:T(1,128)S(1)}, f32[3,1,512]{2,1,0:T(1,128)S(1)}, f32[3,1,512]{2,1,0:T(1,128)S(1)}) custom-call(bf16[16,400,128]{2,1,0:T(8,128)(2,1)S(1)} %all-to-all-done.own_ref, bf16[16,400,128]{2,1,0:T(8,128)(2,1)} %collective-permute-done.2.peer_ref, bf16[16,128,128]{2,1,0:T(8,128)(2,1)S(1)} %copy-done.4, ...), custom_call_target="tpu_custom_call" | custom-call | flops 4294967296 | bytes 6291456 | tf_op jit(solution)/shard_map/near_best/pallas_call | solution.py:302
  72.6 0.0 collective-permute-done.6.above_late_ref
  72.6 1.3 %collective-permute-done.5.below_late_ref = bf16[16,128,128]{2,1,0:T(8,128)(2,1)} collective-permute-done((bf16[16,128,128]{2,1,0:T(8,128)(2,1)}, bf16[16,128,128]{2,1,0:T(8,128)(2,1)}, u32[]{:S(2)}, u32[]{:S(2)}) %collective-permute-start.5) | collective-permute-done | bytes 524320 | tf_op jit(solution)/shard_map/ppermute | solution.py:444
  73.9 0.0 copy-done.5
  73.9 0.0 copy-start.2
  73.9 6.5 %last_best.1 = (f32[3,1,512]{2,1,0:T(1,128)S(1)}, f32[3,1,512]{2,1,0:T(1,128)S(1)}, f32[3,1,512]{2,1,0:T(1,128)S(1)}, f32[3,1,512]{2,1,0:T(1,128)S(1)}) custom-call(bf16[16,400,128]{2,1,0:T(8,128)(2,1)S(1)} %all-to-all-done.own_ref, bf16[16,400,128]{2,1,0:T(8,128)(2,1)} %collective-permute-done.2.peer_ref, bf16[16,128,128]{2,1,0:T(8,128)(2,1)S(1)} %copy-done.5, ...), custom_call_target="tpu_custom_call" | custom-call | flops 2952790016 | bytes 6291456 | tf_op jit(solution)/shard_map/last_best/pallas_call | solution.py:369
  80.5 1.4 %collective-permute-start.7 = (f32[3,1,512]{2,1,0:T(1,128)S(1)}, f32[3,1,512]{2,1,0:T(1,128)S(1)}, u32[]{:S(2)}, u32[]{:S(2)}) collective-permute-start(f32[3,1,512]{2,1,0:T(1,128)S(1)} %get-tuple-element.30), channel_id=1, source_target_pairs={{0,8},{8,0},{1,9},{9,1},{2,10},{10,2},{3,11},{11,3},{4,12},{12,4},... | collective-permute-start | bytes 18440 | tf_op jit(solution)/shard_map/ppermute | solution.py:456
  81.9 2.1 %collective-permute-start.8 = (f32[3,1,512]{2,1,0:T(1,128)S(1)}, f32[3,1,512]{2,1,0:T(1,128)S(1)}, u32[]{:S(2)}, u32[]{:S(2)}) collective-permute-start(f32[3,1,512]{2,1,0:T(1,128)S(1)} %get-tuple-element.31), channel_id=1, source_target_pairs={{1,0},{2,1},{3,2},{0,3},{9,8},{10,9},{11,10},{8,11},{5,4},{6,5},{7... | collective-permute-start | bytes 18440 | tf_op jit(solution)/shard_map/ppermute | solution.py:457
  84.0 0.0 collective-permute-start.9
  84.0 0.0 collective-permute-done.7.refs_1_
  84.0 0.8 collective-permute-done.8.refs_2_
  84.8 3.5 %collective-permute-done.9.refs_3_ = f32[3,1,512]{2,1,0:T(1,128)S(1)} collective-permute-done((f32[3,1,512]{2,1,0:T(1,128)S(1)}, f32[3,1,512]{2,1,0:T(1,128)S(1)}, u32[]{:S(2)}, u32[]{:S(2)}) %collective-permute-start.9) | collective-permute-done | bytes 6176 | tf_op jit(solution)/shard_map/ppermute | solution.py:458
  88.3 0.2 joined.1
  88.5 11.0 %all_to_all.15 = f32[16,1,128]{2,1,0:T(1,128)S(1)} all-to-all(f32[16,1,128]{2,1,0:T(1,128)S(1)} %bitcast.7), channel_id=1, replica_groups=mesh['yh'=2,'x'=4,'c'=2,'yl'=2,'z'=4] {'yh','x','yl'}, dimensions={0} | all-to-all | bytes 16384 | tf_op jit(solution)/shard_map/all_to_all | solution.py:460
  99.4 0.0 copy-done.2
  99.4 1.0 picked.1
Async XLA Ops:
  0.0 0.7 copy-start.1
  1.2 1.2 %copy-start = (bf16[1024,512]{1,0:T(8,128)(2,1)S(1)}, bf16[1024,512]{1,0:T(8,128)(2,1)}, u32[]{:S(2)}) copy-start(bf16[1024,512]{1,0:T(8,128)(2,1)} %rows_ref.1) | copy-start | bytes 3145732
  6.0 33.0 %all-to-all-start = ((bf16[16,400,128]{2,1,0:T(8,128)(2,1)}), bf16[16,400,128]{2,1,0:T(8,128)(2,1)S(1)}, u32[]{:S(2)}, u32[]{:S(2)}) async-start(bf16[16,400,128]{2,1,0:T(8,128)(2,1)} %get-tuple-element.22), calls=%async_computation | async-start | bytes 3276800 | tf_op jit(solution)/shard_map/all_to_all | solution.py:432
  13.6 17.5 %collective-permute-start.1 = (bf16[16,144,128]{2,1,0:T(8,128)(2,1)S(1)}, bf16[16,144,128]{2,1,0:T(8,128)(2,1)S(1)}, u32[]{:S(2)}, u32[]{:S(2)}) collective-permute-start(bf16[16,144,128]{2,1,0:T(8,128)(2,1)S(1)} %get-tuple-element.21), channel_id=1, source_target_pairs={{0,11},{1,8},{2,1},{3,2},{8,3},{9,0},{10,9},{11,10},{4,15},{5,12},... | collective-permute-start | bytes 1769480 | tf_op jit(solution)/shard_map/ppermute | solution.py:440
  18.3 16.5 %collective-permute-start = (bf16[16,144,128]{2,1,0:T(8,128)(2,1)S(1)}, bf16[16,144,128]{2,1,0:T(8,128)(2,1)S(1)}, u32[]{:S(2)}, u32[]{:S(2)}) collective-permute-start(bf16[16,144,128]{2,1,0:T(8,128)(2,1)S(1)} %get-tuple-element.21), channel_id=1, source_target_pairs={{0,1},{1,2},{2,3},{3,0},{8,9},{9,10},{10,11},{11,8},{4,5},{5,6},{6... | collective-permute-start | bytes 1769480 | tf_op jit(solution)/shard_map/ppermute | solution.py:440
  39.0 12.8 %collective-permute-start.2 = (bf16[16,400,128]{2,1,0:T(8,128)(2,1)S(1)}, bf16[16,400,128]{2,1,0:T(8,128)(2,1)}, u32[]{:S(2)}, u32[]{:S(2)}) collective-permute-start(bf16[16,400,128]{2,1,0:T(8,128)(2,1)S(1)} %all-to-all-done.own_ref), channel_id=1, source_target_pairs={{0,8},{8,0},{1,9},{9,1},{2,10},{10,2},{3,11},{11,3},{4,12},{12,4},... | collective-permute-start | bytes 4915208 | tf_op jit(solution)/shard_map/ppermute | solution.py:447
  40.1 23.7 %all-to-all-start.1 = ((bf16[16,288,128]{2,1,0:T(8,128)(2,1)}), bf16[16,288,128]{2,1,0:T(8,128)(2,1)S(1)}, u32[]{:S(2)}, u32[]{:S(2)}) async-start(bf16[16,288,128]{2,1,0:T(8,128)(2,1)} %pad_maximum_fusion), calls=%async_computation.1 | async-start | bytes 2359296 | tf_op jit(solution)/shard_map/all_to_all | solution.py:432
  44.8 16.3 %collective-permute-start.4 = (bf16[16,128,128]{2,1,0:T(8,128)(2,1)S(1)}, bf16[16,128,128]{2,1,0:T(8,128)(2,1)S(1)}, u32[]{:S(2)}, u32[]{:S(2)}) collective-permute-start(bf16[16,128,128]{2,1,0:T(8,128)(2,1)S(1)} %get-tuple-element.34), channel_id=1, source_target_pairs={{0,11},{1,8},{2,1},{3,2},{8,3},{9,0},{10,9},{11,10},{4,15},{5,12},... | collective-permute-start | bytes 1572872 | tf_op jit(solution)/shard_map/ppermute | solution.py:445
  48.4 14.2 %collective-permute-start.3 = (bf16[16,128,128]{2,1,0:T(8,128)(2,1)S(1)}, bf16[16,128,128]{2,1,0:T(8,128)(2,1)S(1)}, u32[]{:S(2)}, u32[]{:S(2)}) collective-permute-start(bf16[16,128,128]{2,1,0:T(8,128)(2,1)S(1)} %get-tuple-element.34), channel_id=1, source_target_pairs={{0,1},{1,2},{2,3},{3,0},{8,9},{9,10},{10,11},{11,8},{4,5},{5,6},{6... | collective-permute-start | bytes 1572872 | tf_op jit(solution)/shard_map/ppermute | solution.py:444
  48.4 24.2 %collective-permute-start.6 = (bf16[16,128,128]{2,1,0:T(8,128)(2,1)}, bf16[16,128,128]{2,1,0:T(8,128)(2,1)}, u32[]{:S(2)}, u32[]{:S(2)}) collective-permute-start(bf16[16,128,128]{2,1,0:T(8,128)(2,1)} %get-tuple-element.33), channel_id=1, source_target_pairs={{0,11},{1,8},{2,1},{3,2},{8,3},{9,0},{10,9},{11,10},{4,15},{5,12},... | collective-permute-start | bytes 1572872 | tf_op jit(solution)/shard_map/ppermute | solution.py:445
  51.7 22.2 %collective-permute-start.5 = (bf16[16,128,128]{2,1,0:T(8,128)(2,1)}, bf16[16,128,128]{2,1,0:T(8,128)(2,1)}, u32[]{:S(2)}, u32[]{:S(2)}) collective-permute-start(bf16[16,128,128]{2,1,0:T(8,128)(2,1)} %get-tuple-element.33), channel_id=1, source_target_pairs={{0,1},{1,2},{2,3},{3,0},{8,9},{9,10},{10,11},{11,8},{4,5},{5,6},{6... | collective-permute-start | bytes 1572872 | tf_op jit(solution)/shard_map/ppermute | solution.py:444
  62.6 0.8 copy-start.3
  63.8 1.0 %copy-start.4 = (bf16[16,128,128]{2,1,0:T(8,128)(2,1)S(1)}, bf16[16,128,128]{2,1,0:T(8,128)(2,1)}, u32[]{:S(2)}) copy-start(bf16[16,128,128]{2,1,0:T(8,128)(2,1)} %copy-done.3) | copy-start | bytes 1572868
  64.9 9.0 %copy-start.5 = (bf16[16,128,128]{2,1,0:T(8,128)(2,1)S(1)}, bf16[16,128,128]{2,1,0:T(8,128)(2,1)}, u32[]{:S(2)}) copy-start(bf16[16,128,128]{2,1,0:T(8,128)(2,1)} %copy-done.3) | copy-start | bytes 1572868
  73.9 25.5 %copy-start.2 = (s32[1024]{0:T(1024)S(1)}, s32[1024]{0:T(1024)}, u32[]{:S(2)}) copy-start(s32[1024]{0:T(1024)} %param.3) | copy-start | bytes 12292
  80.5 3.6 %collective-permute-start.7 = (f32[3,1,512]{2,1,0:T(1,128)S(1)}, f32[3,1,512]{2,1,0:T(1,128)S(1)}, u32[]{:S(2)}, u32[]{:S(2)}) collective-permute-start(f32[3,1,512]{2,1,0:T(1,128)S(1)} %get-tuple-element.30), channel_id=1, source_target_pairs={{0,8},{8,0},{1,9},{9,1},{2,10},{10,2},{3,11},{11,3},{4,12},{12,4},... | collective-permute-start | bytes 18440 | tf_op jit(solution)/shard_map/ppermute | solution.py:456
  81.9 2.9 %collective-permute-start.8 = (f32[3,1,512]{2,1,0:T(1,128)S(1)}, f32[3,1,512]{2,1,0:T(1,128)S(1)}, u32[]{:S(2)}, u32[]{:S(2)}) collective-permute-start(f32[3,1,512]{2,1,0:T(1,128)S(1)} %get-tuple-element.31), channel_id=1, source_target_pairs={{1,0},{2,1},{3,2},{0,3},{9,8},{10,9},{11,10},{8,11},{5,4},{6,5},{7... | collective-permute-start | bytes 18440 | tf_op jit(solution)/shard_map/ppermute | solution.py:457
  84.0 4.3 %collective-permute-start.9 = (f32[3,1,512]{2,1,0:T(1,128)S(1)}, f32[3,1,512]{2,1,0:T(1,128)S(1)}, u32[]{:S(2)}, u32[]{:S(2)}) collective-permute-start(f32[3,1,512]{2,1,0:T(1,128)S(1)} %get-tuple-element.32), channel_id=1, source_target_pairs={{11,0},{8,1},{1,2},{2,3},{3,8},{0,9},{9,10},{10,11},{15,4},{12,5},... | collective-permute-start | bytes 18440 | tf_op jit(solution)/shard_map/ppermute | solution.py:458

commit v4 on v3

--- a/solution.py
+++ b/solution.py
@@ -29,8 +29,10 @@
 AXES = ("yh", "x", "c", "yl", "z")
 PLANE = ("yh", "x", "yl")
 RING = ("c", "z")
+EVERYWHERE = ("z", "c") + PLANE
+RING_SIZE = 8
 NT = (((1,), (1,)), ((), ()))
-VMEM_LIMIT = 48 * 1024 * 1024
+VMEM_LIMIT = 32 * 1024 * 1024
 
 CROSSED = (0, 3)
 
@@ -48,15 +50,22 @@
     return pairs
 
 
-def reverse(pairs):
-    return [(b, a) for a, b in pairs]
-
-
 def params():
     return pltpu.CompilerParams(vmem_limit_bytes=VMEM_LIMIT)
 
 
-def place_kernel(cluster_ref, place_ref, ends_ref):
+CHUNK = 4
+
+
+def send_kernel(
+    cluster_hbm, rows_hbm, place_ref, early_ref, out_hbm, rows, unit, out, row_sem, out_sems, cluster_ref, cl_sem
+):
+    cl = pltpu.make_async_copy(cluster_hbm, cluster_ref, cl_sem)
+    cl.start()
+    fetch = pltpu.make_async_copy(rows_hbm, rows, row_sem)
+    fetch.start()
+    cl.wait()
+
     step = 256
     kinds = lax.broadcasted_iota(jnp.int32, (128, step), 0)
     before = (
@@ -67,9 +76,9 @@
     hots, ranks = [], []
     for first in range(0, ROWS, step):
         hot = kinds == cluster_ref[:, first : first + step]
-        hot16 = hot.astype(jnp.bfloat16)
         hots.append(hot)
-        ranks.append(jnp.dot(hot16, before, preferred_element_type=jnp.float32) + total)
+        rank = jnp.dot(hot.astype(jnp.bfloat16), before, preferred_element_type=jnp.float32)
+        ranks.append(rank + total)
         total = total + jnp.sum(hot.astype(jnp.float32), axis=1, keepdims=True)
     one = lax.broadcasted_iota(jnp.int32, (128, 128), 0)
     other = lax.broadcasted_iota(jnp.int32, (128, 128), 1)
@@ -83,6 +92,7 @@
     for k, first in enumerate(range(0, ROWS, step)):
         place = jnp.sum(jnp.where(hots[k], ranks[k] + base, 0.0), axis=0, keepdims=True)
         place_ref[:, first : first + step] = place.astype(jnp.int32)
+
     group = lax.broadcasted_iota(jnp.int32, (GROUPS, 128), 0)
     kind = lax.broadcasted_iota(jnp.int32, (GROUPS, 128), 1)
     ends = jnp.dot(
@@ -91,69 +101,64 @@
         preferred_element_type=jnp.float32,
     )
     ends = jnp.where(kind < CPG, ends, 512.0)
-    ends_ref[...] = jnp.broadcast_to(ends[:, None, :], ends_ref.shape).astype(jnp.bfloat16)
-
-
-def placed(cluster):
+    ends = jnp.broadcast_to(ends[:, None, :], (GROUPS, TAIL, LANES)).astype(jnp.bfloat16)
+    out[:, PIECES * PIECE :] = ends
+    early_ref[:, PIECE:] = ends
+
+    fetch.wait()
+    values = rows[...].astype(jnp.float32)
+    mean = jnp.mean(values * values, axis=1, keepdims=True)
+    scale = lax.rsqrt(mean + 1e-06) / math.sqrt(D)
+    unit[...] = (values * scale).astype(jnp.bfloat16)
+
+    height = CHUNK * SLOTS
+    copies = []
+    for chunk in range(GROUPS // CHUNK):
+        groups = slice(chunk * CHUNK, (chunk + 1) * CHUNK)
+        slot = lax.broadcasted_iota(jnp.int32, (height, ROWS), 0) + chunk * height
+        hot = (slot == place_ref[...]).astype(jnp.bfloat16)
+        sent = jnp.dot(hot, unit[...], preferred_element_type=jnp.float32).astype(jnp.bfloat16)
+        sent = sent.reshape(CHUNK, SLOTS, D)
+        for k in range(PIECES):
+            for part in range(FEATURE_PARTS):
+                first = k * PIECE + part * SHARE
+                piece = sent[:, k * SHARE : (k + 1) * SHARE, part * LANES : (part + 1) * LANES]
+                out[groups, first : first + SHARE] = piece
+                if k == PIECES - 1:
+                    early_ref[groups, part * SHARE : (part + 1) * SHARE] = piece
+        copy = pltpu.make_async_copy(out.at[groups], out_hbm.at[groups], out_sems.at[chunk])
+        copy.start()
+        copies.append(copy)
+    for copy in copies:
+        copy.wait()
+
+
+VMEM = pl.BlockSpec(memory_space=pltpu.VMEM)
+ANY = pl.BlockSpec(memory_space=pltpu.HBM)
+
+
+def send_rows(cluster, rows):
     return pl.pallas_call(
-        place_kernel,
+        send_kernel,
+        in_specs=[ANY, ANY],
+        out_specs=(VMEM, VMEM, ANY),
         out_shape=(
             jax.ShapeDtypeStruct((1, ROWS), jnp.int32),
-            jax.ShapeDtypeStruct((GROUPS, TAIL, LANES), jnp.bfloat16),
+            jax.ShapeDtypeStruct((GROUPS, EARLY_BLOCK, LANES), jnp.bfloat16),
+            jax.ShapeDtypeStruct((GROUPS, BLOCK, LANES), jnp.bfloat16),
         ),
-        compiler_params=params(),
-        name="placed",
-    )(cluster)
-
-
-def send_kernel(rows_ref, place_ref, ends_ref, out_ref, early_ref, unit):
-    step = pl.program_id(0)
-
-    @pl.when(step == 0)
-    def _():
-        values = rows_ref[...].astype(jnp.float32)
-        mean = jnp.mean(values * values, axis=1, keepdims=True)
-        scale = lax.rsqrt(mean + 1e-06) / math.sqrt(D)
-        unit[...] = (values * scale).astype(jnp.bfloat16)
-
-    number = out_ref.shape[0]
-    height = number * SLOTS
-    slot = lax.broadcasted_iota(jnp.int32, (height, ROWS), 0) + step * height
-    hot = (slot == place_ref[...]).astype(jnp.bfloat16)
-    rows = jnp.dot(hot, unit[...], preferred_element_type=jnp.float32).astype(jnp.bfloat16)
-    rows = rows.reshape(number, SLOTS, D)
-    for k in range(PIECES):
-        for part in range(FEATURE_PARTS):
-            first = k * PIECE + part * SHARE
-            out_ref[:, first : first + SHARE] = rows[
-                :, k * SHARE : (k + 1) * SHARE, part * LANES : (part + 1) * LANES
-            ]
-    out_ref[:, PIECES * PIECE :] = ends_ref[...]
-    early_ref[...] = out_ref[:, EARLY:]
-
-
-def send_rows(rows, place, ends):
-    number = 4
-    return pl.pallas_call(
-        send_kernel,
-        grid=(GROUPS // number,),
-        in_specs=[
-            pl.BlockSpec((ROWS, D), lambda i: (0, 0)),
-            pl.BlockSpec((1, ROWS), lambda i: (0, 0)),
-            pl.BlockSpec((number, TAIL, LANES), lambda i: (i, 0, 0)),
+        scratch_shapes=[
+            pltpu.VMEM((ROWS, D), jnp.bfloat16),
+            pltpu.VMEM((ROWS, D), jnp.bfloat16),
+            pltpu.VMEM((GROUPS, BLOCK, LANES), jnp.bfloat16),
+            pltpu.SemaphoreType.DMA,
+            pltpu.SemaphoreType.DMA((GROUPS // CHUNK,)),
+            pltpu.VMEM((1, ROWS), jnp.int32),
+            pltpu.SemaphoreType.DMA,
         ],
-        out_specs=(
-            pl.BlockSpec((number, BLOCK, LANES), lambda i: (i, 0, 0)),
-            pl.BlockSpec((number, EARLY_BLOCK, LANES), lambda i: (i, 0, 0)),
-        ),
-        out_shape=(
-            jax.ShapeDtypeStruct((GROUPS, BLOCK, LANES), jnp.bfloat16),
-            jax.ShapeDtypeStruct((GROUPS, EARLY_BLOCK, LANES), jnp.bfloat16),
-        ),
-        scratch_shapes=[pltpu.VMEM((ROWS, D), jnp.bfloat16)],
-        compiler_params=params(),
+        compiler_params=pltpu.CompilerParams(vmem_limit_bytes=63 * 1024 * 1024),
         name="send_rows",
-    )(rows, place, ends)
+    )(cluster, rows)
 
 
 def labels_of(ends, number, empty):
@@ -313,7 +318,13 @@
     )(own, peer, below, above, early, old)
 
 
+def spread(table, number, row):
+    for s in range(GROUPS):
+        table[s : s + 1, number * SHARE : (number + 1) * SHARE] = row[:, s * SHARE : (s + 1) * SHARE]
+
+
 def last_kernel(
+    slabs_ref,
     own_ref,
     peer_ref,
     below_ref,
@@ -325,10 +336,7 @@
     old_peer_ref,
     old_below_ref,
     old_above_ref,
-    best_ref,
-    peer_best_ref,
-    below_best_ref,
-    above_best_ref,
+    out_ref,
     columns,
     labels,
     column_best,
@@ -346,29 +354,30 @@
         mine = row_labels(ends, number)
         return lanes_of(scored(rows, mine, columns, labels.at[0:1], numbers, column_best))
 
-    def one(number, _):
-        first = pl.multiple_of(number * PIECE, PIECE)
-        found = visit(piece_of(own_ref, first), own_ref[:, PIECES * PIECE :], number)
-        best_ref[number] = jnp.maximum(found, old_ref[number])
-        found = visit(piece_of(peer_ref, first), peer_ref[:, PIECES * PIECE :], number)
-        peer_best_ref[number] = jnp.maximum(found, old_peer_ref[number])
-        return 0
-
-    lax.fori_loop(0, PIECES, one, 0)
+    out_ref[...] = jnp.full(out_ref.shape, FLOOR, jnp.float32)
+    tables = [out_ref.at[slabs_ref[k]] for k in range(4)]
+    for number in range(PIECES):
+        found = visit(piece_of(own_ref, number * PIECE), own_ref[:, PIECES * PIECE :], number)
+        spread(tables[0], number, jnp.maximum(found, old_ref[number]))
+    for number in range(PIECES):
+        found = visit(piece_of(peer_ref, number * PIECE), peer_ref[:, PIECES * PIECE :], number)
+        spread(tables[1], number, jnp.maximum(found, old_peer_ref[number]))
     found = visit(piece_of(below_ref, 0), below_ends, 0)
-    below_best_ref[0] = jnp.maximum(found, old_below_ref[0])
-    below_best_ref[1] = visit(piece_of(below_late_ref, 0), below_ends, 1, range(PIECES))
+    spread(tables[2], 0, jnp.maximum(found, old_below_ref[0]))
     found = visit(piece_of(early_ref, 0), below_ends, 2)
-    below_best_ref[2] = jnp.maximum(found, old_below_ref[2])
+    spread(tables[2], 2, jnp.maximum(found, old_below_ref[2]))
+    found = visit(piece_of(below_late_ref, 0), below_ends, 1, range(PIECES))
+    spread(tables[2], 1, found)
     for number in range(PIECES):
         found = jnp.max(column_best[:, span(number)], axis=0, keepdims=True)
-        above_best_ref[number] = jnp.maximum(found, old_above_ref[number])
+        spread(tables[3], number, jnp.maximum(found, old_above_ref[number]))
 
 
 def last_best(*arrays):
     return pl.pallas_call(
         last_kernel,
-        out_shape=(BEST,) * 4,
+        in_specs=[pl.BlockSpec(memory_space=pltpu.SMEM)] + [VMEM] * 11,
+        out_shape=jax.ShapeDtypeStruct((RING_SIZE, GROUPS, LANES), jnp.float32),
         scratch_shapes=[
             pltpu.VMEM((PIECES, HEIGHT, D), jnp.bfloat16),
             pltpu.VMEM((8, WIDTH), jnp.float32),
@@ -380,31 +389,11 @@
     )(*arrays)
 
 
-def join_kernel(*refs):
-    best = refs[0][...]
-    for ref in refs[1:-1]:
-        best = jnp.maximum(best, ref[...])
-    out_ref = refs[-1]
-    out_ref[...] = jnp.zeros(out_ref.shape, jnp.float32)
-    for k in range(PIECES):
-        for s in range(GROUPS):
-            out_ref[s : s + 1, k * SHARE : (k + 1) * SHARE] = best[k, :, s * SHARE : (s + 1) * SHARE]
-
-
-def joined(*parts):
-    return pl.pallas_call(
-        join_kernel,
-        out_shape=jax.ShapeDtypeStruct((GROUPS, 128), jnp.float32),
-        compiler_params=params(),
-        name="joined",
-    )(*parts)
-
-
 def pick_kernel(answers_ref, cluster_ref, place_ref, out_ref):
     group = cluster_ref[...] // CPG
     slot = place_ref[...] - group * SLOTS
     hot = (lax.broadcasted_iota(jnp.int32, (GROUPS, ROWS), 0) == group).astype(jnp.bfloat16)
-    rest = answers_ref[...]
+    rest = jnp.max(answers_ref[...], axis=0)
     found = jnp.zeros((128, ROWS), jnp.float32)
     for _ in range(3):
         part = rest.astype(jnp.bfloat16)
@@ -434,8 +423,7 @@
 
 def shards(embeddings, cluster):
     cluster = cluster.reshape(1, ROWS)
-    place, ends = placed(cluster)
-    sent, early = send_rows(embeddings, place, ends)
+    place, early, sent = send_rows(cluster, embeddings)
     early = jnp.concatenate(
         [lax.ppermute(early, RING, to_above()), lax.ppermute(early, RING, to_below())], axis=1
     )
@@ -448,18 +436,27 @@
     early = all_to_plane(early)
     best = own_best(own, peer)
     bests = near_best(own, peer, below[0], above[0], early, best)
-    best, best_peer, best_below, best_above = last_best(
-        own, peer, below[0], above[0], below[1], above[1], early, *bests
-    )
-    answers = joined(
-        best,
-        lax.ppermute(best_peer, "c", SWAP),
-        lax.ppermute(best_below, RING, reverse(to_above())),
-        lax.ppermute(best_above, RING, reverse(to_below())),
+    z = lax.axis_index("z")
+    core = lax.axis_index("c")
+    crossed = (z == CROSSED[0]) | (z == CROSSED[1])
+    slabs = jnp.stack(
+        [
+            z * 2 + core,
+            z * 2 + 1 - core,
+            (z + 3) % 4 * 2 + core,
+            (z + 1) % 4 * 2 + jnp.where(crossed, 1 - core, core),
+        ]
+    ).astype(jnp.int32)
+    answers = last_best(
+        slabs, own, peer, below[0], above[0], below[1], above[1], early, *bests
     )
     answers = lax.all_to_all(
-        answers.reshape(GROUPS, 1, 128), PLANE, split_axis=0, concat_axis=0, tiled=True
-    ).reshape(GROUPS, 128)
+        answers.reshape(RING_SIZE * GROUPS, 1, LANES),
+        EVERYWHERE,
+        split_axis=0,
+        concat_axis=0,
+        tiled=True,
+    ).reshape(RING_SIZE, GROUPS, LANES)
     return picked(answers, cluster, place).reshape(ROWS)
 
 

time: 101 us -> 98 us (0.970)
  blocking collectives: 11 us -> 17.4 us
  waiting for transfers between devices: 27.1 us -> 23 us
  starting transfers between devices: 27.7 us -> 24.3 us
  local copies, waits for them, and re-layouts: 4.71 us -> 2.79 us
    all_to_all x1, blocking collectives: 11 us -> 17.4 us  [shards(): lax.all_to_all(answers.reshape(RING_SIZE * GROUPS, 1, LANES), EVERYWHERE,...]
    ppermute x3 -> x0, waiting for transfers between devices: 4.26 us -> none  [the longest x1 3.49 us: shards(): lax.ppermute(best_above, RING, reverse(to_below()))]
    ppermute x3 -> x0, starting transfers between devices: 3.57 us -> none  [the longest x1 2.14 us: shards(): lax.ppermute(best_below, RING, reverse(to_above()))]
    unnamed x12, local copies, waits for them, and re-layouts: 3.77 us -> 1.87 us
    pallas_call x4 -> x2, Pallas kernels: 10.8 us -> 11 us  [the longest x1 6.22 us: last_best(): pl.pallas_call(last_kernel, in_specs=[pl.BlockSpec(memory_space=pltpu.SME...]
  transfers between devices with their start and end apart: 12 -> 9, of which waited for: 8 -> 6; matrix products, arithmetic and copies ran while one was open for 2% -> 2% of each run, Pallas kernels for 17% -> 17%
where the time goes in v4:
time: 98 us; the launch traced here: 97.6 us
  Pallas kernels  28.8 us (29%)
  starting transfers between devices  24.3 us (25%)
  waiting for transfers between devices  23 us (23%)
  blocking collectives  17.4 us (18%)
  local copies, waits for them, and re-layouts  2.79 us (3%)
  other arithmetic  1.18 us (1%)
    all_to_all x1, blocking collectives, shards(): lax.all_to_all(answers.reshape(RING_SIZE * GROUPS, 1, LANES), EVERYWHERE,...  17.4 us
    ppermute x1, waiting for transfers between devices, shards(): lax.ppermute(early, RING, to_below())  12.9 us
    all_to_all x2, starting transfers between devices, all_to_plane(): return lax.all_to_all(block, PLANE, split_axis=0, concat_axis=0, tiled=True)  11.4 us
    pallas_call x1, Pallas kernels, own_best(): pl.pallas_call(own_kernel, out_shape=BEST, scratch_shapes=[pltpu.VMEM((2,...  9.14 us
    pallas_call x1, Pallas kernels, near_best(): pl.pallas_call(near_kernel, out_shape=(BEST,) * 4, scratch_shapes=[pltpu....  7.61 us
    ppermute x2, starting transfers between devices, shards(): above = [lax.ppermute(block, RING, to_below()) for block in late]  7.02 us
    pallas_call x1, Pallas kernels, last_best(): pl.pallas_call(last_kernel, in_specs=[pl.BlockSpec(memory_space=pltpu.SME...  6.22 us
    pallas_call x1, Pallas kernels, send_rows(): pl.pallas_call(send_kernel, in_specs=[ANY, ANY], out_specs=(VMEM, VMEM, A...  4.82 us
  transfers between devices with their start and end apart: 9, of which 6 were waited for; matrix products, arithmetic and copies ran while one was open for 2% of the time, Pallas kernels for 17%

profile of v4, /device:TPU:1, one launch (start us, length us, event | category | flops | bytes accessed | tf_op | source)
XLA Modules:
  0.0 97.6 jit_solution(9116490795206089684)
XLA Ops:
  0.0 4.8 %send_rows.1 = (s32[1,1024]{1,0:T(1,128)}, bf16[16,144,128]{2,1,0:T(8,128)(2,1)}, bf16[16,400,128]{2,1,0:T(8,128)(2,1)}) custom-call(s32[1,1024]{1,0:T(1,128)} %bitcast.12, bf16[1024,512]{1,0:T(8,128)(2,1)} %rows_hbm.1), custom_call_target="tpu_custom_call" | custom-call | tf_op jit(solution)/shard_map/send_rows/pallas_call | solution.py:141
  4.8 0.0 copy-start.5
  4.8 7.7 %all-to-all-start = ((bf16[16,400,128]{2,1,0:T(8,128)(2,1)}), bf16[16,400,128]{2,1,0:T(8,128)(2,1)S(1)}, u32[]{:S(2)}, u32[]{:S(2)}) async-start(bf16[16,400,128]{2,1,0:T(8,128)(2,1)} %get-tuple-element.15), calls=%async_computation | async-start | bytes 3276800 | tf_op jit(solution)/shard_map/all_to_all | solution.py:421
  12.6 0.0 copy-done.5
  12.6 4.7 %collective-permute-start.1 = (bf16[16,144,128]{2,1,0:T(8,128)(2,1)S(1)}, bf16[16,144,128]{2,1,0:T(8,128)(2,1)S(1)}, u32[]{:S(2)}, u32[]{:S(2)}) collective-permute-start(bf16[16,144,128]{2,1,0:T(8,128)(2,1)S(1)} %copy-done.5), channel_id=1, source_target_pairs={{0,11},{1,8},{2,1},{3,2},{8,3},{9,0},{10,9},{11,10},{4,15},{5,12},... | collective-permute-start | bytes 1769480 | tf_op jit(solution)/shard_map/ppermute | solution.py:428
  17.3 0.0 collective-permute-start
  17.3 12.9 %collective-permute-done.1 = bf16[16,144,128]{2,1,0:T(8,128)(2,1)S(1)} collective-permute-done((bf16[16,144,128]{2,1,0:T(8,128)(2,1)S(1)}, bf16[16,144,128]{2,1,0:T(8,128)(2,1)S(1)}, u32[]{:S(2)}, u32[]{:S(2)}) %collective-permute-start.1) | collective-permute-done | bytes 589856 | tf_op jit(solution)/shard_map/ppermute | solution.py:428
  30.1 3.7 %collective-permute-done = bf16[16,144,128]{2,1,0:T(8,128)(2,1)S(1)} collective-permute-done((bf16[16,144,128]{2,1,0:T(8,128)(2,1)S(1)}, bf16[16,144,128]{2,1,0:T(8,128)(2,1)S(1)}, u32[]{:S(2)}, u32[]{:S(2)}) %collective-permute-start) | collective-permute-done | bytes 589856 | tf_op jit(solution)/shard_map/ppermute | solution.py:428
  33.8 1.1 %pad_maximum_fusion = bf16[16,288,128]{2,1,0:T(8,128)(2,1)} fusion(bf16[16,144,128]{2,1,0:T(8,128)(2,1)S(1)} %collective-permute-done.1, bf16[16,144,128]{2,1,0:T(8,128)(2,1)S(1)} %collective-permute-done), kind=kLoop, calls=%fused_computation | loop fusion | flops 2359296 | bytes 2359296 | tf_op jit(solution)/shard_map/concatenate | solution.py:427
  34.9 3.0 %all-to-all-done.own_ref = bf16[16,400,128]{2,1,0:T(8,128)(2,1)S(1)} async-done(((bf16[16,400,128]{2,1,0:T(8,128)(2,1)}), bf16[16,400,128]{2,1,0:T(8,128)(2,1)S(1)}, u32[]{:S(2)}, u32[]{:S(2)}) %all-to-all-start) | async-done | bytes 1638432 | tf_op jit(solution)/shard_map/all_to_all | solution.py:421
  37.9 1.1 %collective-permute-start.2 = (bf16[16,400,128]{2,1,0:T(8,128)(2,1)S(1)}, bf16[16,400,128]{2,1,0:T(8,128)(2,1)}, u32[]{:S(2)}, u32[]{:S(2)}) collective-permute-start(bf16[16,400,128]{2,1,0:T(8,128)(2,1)S(1)} %all-to-all-done.own_ref), channel_id=1, source_target_pairs={{0,8},{8,0},{1,9},{9,1},{2,10},{10,2},{3,11},{11,3},{4,12},{12,4},... | collective-permute-start | bytes 4915208 | tf_op jit(solution)/shard_map/ppermute | solution.py:435
  39.0 3.7 %all-to-all-start.1 = ((bf16[16,288,128]{2,1,0:T(8,128)(2,1)}), bf16[16,288,128]{2,1,0:T(8,128)(2,1)S(1)}, u32[]{:S(2)}, u32[]{:S(2)}) async-start(bf16[16,288,128]{2,1,0:T(8,128)(2,1)} %pad_maximum_fusion), calls=%async_computation.1 | async-start | bytes 2359296 | tf_op jit(solution)/shard_map/all_to_all | solution.py:421
  42.8 0.9 fusion
  43.7 3.7 %collective-permute-start.4 = (bf16[16,128,128]{2,1,0:T(8,128)(2,1)S(1)}, bf16[16,128,128]{2,1,0:T(8,128)(2,1)S(1)}, u32[]{:S(2)}, u32[]{:S(2)}) collective-permute-start(bf16[16,128,128]{2,1,0:T(8,128)(2,1)S(1)} %get-tuple-element.24), channel_id=1, source_target_pairs={{0,11},{1,8},{2,1},{3,2},{8,3},{9,0},{10,9},{11,10},{4,15},{5,12},... | collective-permute-start | bytes 1572872 | tf_op jit(solution)/shard_map/ppermute | solution.py:433
  47.4 0.0 collective-permute-start.3
  47.4 0.1 pad_add_fusion.slabs_ref
  47.4 3.4 %collective-permute-start.6 = (bf16[16,128,128]{2,1,0:T(8,128)(2,1)}, bf16[16,128,128]{2,1,0:T(8,128)(2,1)}, u32[]{:S(2)}, u32[]{:S(2)}) collective-permute-start(bf16[16,128,128]{2,1,0:T(8,128)(2,1)} %get-tuple-element.23), channel_id=1, source_target_pairs={{0,11},{1,8},{2,1},{3,2},{8,3},{9,0},{10,9},{11,10},{4,15},{5,12},... | collective-permute-start | bytes 1572872 | tf_op jit(solution)/shard_map/ppermute | solution.py:433
  50.8 0.0 collective-permute-start.5
  50.8 0.0 collective-permute-done.2.peer_ref
  50.8 9.1 %own_best.1.old_ref = f32[3,1,512]{2,1,0:T(1,128)S(1)} custom-call(bf16[16,400,128]{2,1,0:T(8,128)(2,1)S(1)} %all-to-all-done.own_ref, bf16[16,400,128]{2,1,0:T(8,128)(2,1)} %collective-permute-done.2.peer_ref), custom_call_target="tpu_custom_call" | custom-call | flops 4831838208 | bytes 6291456 | tf_op jit(solution)/shard_map/own_best/pallas_call | solution.py:250
  60.0 0.0 collective-permute-done.4.above_ref
  60.0 1.6 %collective-permute-done.3.below_ref = bf16[16,128,128]{2,1,0:T(8,128)(2,1)S(1)} collective-permute-done((bf16[16,128,128]{2,1,0:T(8,128)(2,1)S(1)}, bf16[16,128,128]{2,1,0:T(8,128)(2,1)S(1)}, u32[]{:S(2)}, u32[]{:S(2)}) %collective-permute-start.3) | collective-permute-done | bytes 524320 | tf_op jit(solution)/shard_map/ppermute | solution.py:432
  61.6 0.0 copy-start.2
  61.6 0.8 copy-done.2
  62.4 0.4 all-to-all-done.1.early_ref
  62.8 0.0 copy-start.3
  62.8 1.0 %copy-done.3 = bf16[16,128,128]{2,1,0:T(8,128)(2,1)S(1)} copy-done((bf16[16,128,128]{2,1,0:T(8,128)(2,1)S(1)}, bf16[16,128,128]{2,1,0:T(8,128)(2,1)}, u32[]{:S(2)}) %copy-start.3) | copy-done | bytes 524312
  63.8 0.0 copy-start.4
  63.8 7.6 %near_best.1 = (f32[3,1,512]{2,1,0:T(1,128)S(1)}, f32[3,1,512]{2,1,0:T(1,128)S(1)}, f32[3,1,512]{2,1,0:T(1,128)S(1)}, f32[3,1,512]{2,1,0:T(1,128)S(1)}) custom-call(bf16[16,400,128]{2,1,0:T(8,128)(2,1)S(1)} %all-to-all-done.own_ref, bf16[16,400,128]{2,1,0:T(8,128)(2,1)} %collective-permute-done.2.peer_ref, bf16[16,128,128]{2,1,0:T(8,128)(2,1)S(1)} %copy-done.3, ...), custom_call_target="tpu_custom_call" | custom-call | flops 4294967296 | bytes 6291456 | tf_op jit(solution)/shard_map/near_best/pallas_call | solution.py:307
  71.4 0.0 collective-permute-done.6.above_late_ref
  71.4 1.5 %collective-permute-done.5.below_late_ref = bf16[16,128,128]{2,1,0:T(8,128)(2,1)} collective-permute-done((bf16[16,128,128]{2,1,0:T(8,128)(2,1)}, bf16[16,128,128]{2,1,0:T(8,128)(2,1)}, u32[]{:S(2)}, u32[]{:S(2)}) %collective-permute-start.5) | collective-permute-done | bytes 524320 | tf_op jit(solution)/shard_map/ppermute | solution.py:432
  72.9 0.0 copy-done.4
  72.9 0.0 copy-start
  72.9 0.0 copy-start.1
  72.9 6.2 %last_best.1 = f32[8,16,128]{2,1,0:T(8,128)S(1)} custom-call(s32[4]{0:T(128)S(1)} %pad_add_fusion.slabs_ref, bf16[16,400,128]{2,1,0:T(8,128)(2,1)S(1)} %all-to-all-done.own_ref, bf16[16,400,128]{2,1,0:T(8,128)(2,1)} %collective-permute-done.2.peer_ref, bf16[16,128,128]{2,1,0:T(8,128)(2,1)S(1)} %copy-done.4, ...), custom_call_target="tpu_custom_call" | custom-call | flops 2952790016 | bytes 6291456 | tf_op jit(solution)/shard_map/last_best/pallas_call | solution.py:377
  79.1 17.4 %all_to_all.15 = f32[128,1,128]{2,1,0:T(1,128)S(1)} all-to-all(f32[128,1,128]{2,1,0:T(1,128)S(1)} %bitcast.11), channel_id=1, replica_groups=mesh['yh'=2,'x'=4,'c'=2,'yl'=2,'z'=4] {'z','c','yh','x','yl'}, dimensions={0} | all-to-all | bytes 131072 | tf_op jit(solution)/shard_map/all_to_all | solution.py:453
  96.6 0.0 copy-done
  96.6 0.0 copy-done.1
  96.6 1.0 %picked.1 = f32[1,1024]{1,0:T(1,128)} custom-call(f32[8,16,128]{2,1,0:T(8,128)S(1)} %bitcast.10, s32[1,1024]{1,0:T(1,128)S(1)} %bitcast.13, s32[1,1024]{1,0:T(1,128)S(1)} %copy-done.1), custom_call_target="tpu_custom_call" | custom-call | tf_op jit(solution)/shard_map/picked/pallas_call | solution.py:409
Async XLA Ops:
  4.8 7.7 %copy-start.5 = (bf16[16,144,128]{2,1,0:T(8,128)(2,1)S(1)}, bf16[16,144,128]{2,1,0:T(8,128)(2,1)}, u32[]{:S(2)}) copy-start(bf16[16,144,128]{2,1,0:T(8,128)(2,1)} %get-tuple-element.14) | copy-start | bytes 1769476
  4.8 33.1 %all-to-all-start = ((bf16[16,400,128]{2,1,0:T(8,128)(2,1)}), bf16[16,400,128]{2,1,0:T(8,128)(2,1)S(1)}, u32[]{:S(2)}, u32[]{:S(2)}) async-start(bf16[16,400,128]{2,1,0:T(8,128)(2,1)} %get-tuple-element.15), calls=%async_computation | async-start | bytes 3276800 | tf_op jit(solution)/shard_map/all_to_all | solution.py:421
  12.6 17.6 %collective-permute-start.1 = (bf16[16,144,128]{2,1,0:T(8,128)(2,1)S(1)}, bf16[16,144,128]{2,1,0:T(8,128)(2,1)S(1)}, u32[]{:S(2)}, u32[]{:S(2)}) collective-permute-start(bf16[16,144,128]{2,1,0:T(8,128)(2,1)S(1)} %copy-done.5), channel_id=1, source_target_pairs={{0,11},{1,8},{2,1},{3,2},{8,3},{9,0},{10,9},{11,10},{4,15},{5,12},... | collective-permute-start | bytes 1769480 | tf_op jit(solution)/shard_map/ppermute | solution.py:428
  17.3 16.5 %collective-permute-start = (bf16[16,144,128]{2,1,0:T(8,128)(2,1)S(1)}, bf16[16,144,128]{2,1,0:T(8,128)(2,1)S(1)}, u32[]{:S(2)}, u32[]{:S(2)}) collective-permute-start(bf16[16,144,128]{2,1,0:T(8,128)(2,1)S(1)} %copy-done.5), channel_id=1, source_target_pairs={{0,1},{1,2},{2,3},{3,0},{8,9},{9,10},{10,11},{11,8},{4,5},{5,6},{6... | collective-permute-start | bytes 1769480 | tf_op jit(solution)/shard_map/ppermute | solution.py:428
  37.9 12.9 %collective-permute-start.2 = (bf16[16,400,128]{2,1,0:T(8,128)(2,1)S(1)}, bf16[16,400,128]{2,1,0:T(8,128)(2,1)}, u32[]{:S(2)}, u32[]{:S(2)}) collective-permute-start(bf16[16,400,128]{2,1,0:T(8,128)(2,1)S(1)} %all-to-all-done.own_ref), channel_id=1, source_target_pairs={{0,8},{8,0},{1,9},{9,1},{2,10},{10,2},{3,11},{11,3},{4,12},{12,4},... | collective-permute-start | bytes 4915208 | tf_op jit(solution)/shard_map/ppermute | solution.py:435
  39.0 23.7 %all-to-all-start.1 = ((bf16[16,288,128]{2,1,0:T(8,128)(2,1)}), bf16[16,288,128]{2,1,0:T(8,128)(2,1)S(1)}, u32[]{:S(2)}, u32[]{:S(2)}) async-start(bf16[16,288,128]{2,1,0:T(8,128)(2,1)} %pad_maximum_fusion), calls=%async_computation.1 | async-start | bytes 2359296 | tf_op jit(solution)/shard_map/all_to_all | solution.py:421
  43.7 16.3 %collective-permute-start.4 = (bf16[16,128,128]{2,1,0:T(8,128)(2,1)S(1)}, bf16[16,128,128]{2,1,0:T(8,128)(2,1)S(1)}, u32[]{:S(2)}, u32[]{:S(2)}) collective-permute-start(bf16[16,128,128]{2,1,0:T(8,128)(2,1)S(1)} %get-tuple-element.24), channel_id=1, source_target_pairs={{0,11},{1,8},{2,1},{3,2},{8,3},{9,0},{10,9},{11,10},{4,15},{5,12},... | collective-permute-start | bytes 1572872 | tf_op jit(solution)/shard_map/ppermute | solution.py:433
  47.4 14.2 %collective-permute-start.3 = (bf16[16,128,128]{2,1,0:T(8,128)(2,1)S(1)}, bf16[16,128,128]{2,1,0:T(8,128)(2,1)S(1)}, u32[]{:S(2)}, u32[]{:S(2)}) collective-permute-start(bf16[16,128,128]{2,1,0:T(8,128)(2,1)S(1)} %get-tuple-element.24), channel_id=1, source_target_pairs={{0,1},{1,2},{2,3},{3,0},{8,9},{9,10},{10,11},{11,8},{4,5},{5,6},{6... | collective-permute-start | bytes 1572872 | tf_op jit(solution)/shard_map/ppermute | solution.py:432
  47.4 24.0 %collective-permute-start.6 = (bf16[16,128,128]{2,1,0:T(8,128)(2,1)}, bf16[16,128,128]{2,1,0:T(8,128)(2,1)}, u32[]{:S(2)}, u32[]{:S(2)}) collective-permute-start(bf16[16,128,128]{2,1,0:T(8,128)(2,1)} %get-tuple-element.23), channel_id=1, source_target_pairs={{0,11},{1,8},{2,1},{3,2},{8,3},{9,0},{10,9},{11,10},{4,15},{5,12},... | collective-permute-start | bytes 1572872 | tf_op jit(solution)/shard_map/ppermute | solution.py:433
  50.8 22.1 %collective-permute-start.5 = (bf16[16,128,128]{2,1,0:T(8,128)(2,1)}, bf16[16,128,128]{2,1,0:T(8,128)(2,1)}, u32[]{:S(2)}, u32[]{:S(2)}) collective-permute-start(bf16[16,128,128]{2,1,0:T(8,128)(2,1)} %get-tuple-element.23), channel_id=1, source_target_pairs={{0,1},{1,2},{2,3},{3,0},{8,9},{9,10},{10,11},{11,8},{4,5},{5,6},{6... | collective-permute-start | bytes 1572872 | tf_op jit(solution)/shard_map/ppermute | solution.py:432
  61.6 0.8 copy-start.2
  62.8 1.0 %copy-start.3 = (bf16[16,128,128]{2,1,0:T(8,128)(2,1)S(1)}, bf16[16,128,128]{2,1,0:T(8,128)(2,1)}, u32[]{:S(2)}) copy-start(bf16[16,128,128]{2,1,0:T(8,128)(2,1)} %copy-done.2) | copy-start | bytes 1572868
  63.8 9.1 %copy-start.4 = (bf16[16,128,128]{2,1,0:T(8,128)(2,1)S(1)}, bf16[16,128,128]{2,1,0:T(8,128)(2,1)}, u32[]{:S(2)}) copy-start(bf16[16,128,128]{2,1,0:T(8,128)(2,1)} %copy-done.2) | copy-start | bytes 1572868
  72.9 23.7 %copy-start = (s32[1024]{0:T(1024)S(1)}, s32[1024]{0:T(1024)}, u32[]{:S(2)}) copy-start(s32[1024]{0:T(1024)} %param.3) | copy-start | bytes 12292
  72.9 23.7 %copy-start.1 = (s32[1,1024]{1,0:T(1,128)S(1)}, s32[1,1024]{1,0:T(1,128)}, u32[]{:S(2)}) copy-start(s32[1,1024]{1,0:T(1,128)} %get-tuple-element.22.place_ref) | copy-start | bytes 12292

commit v5 on v4

--- a/solution.py
+++ b/solution.py
@@ -50,8 +50,8 @@
     return pairs
 
 
-def params():
-    return pltpu.CompilerParams(vmem_limit_bytes=VMEM_LIMIT)
+def params(limit=VMEM_LIMIT):
+    return pltpu.CompilerParams(vmem_limit_bytes=limit)
 
 
 CHUNK = 4
@@ -156,7 +156,7 @@
             pltpu.VMEM((1, ROWS), jnp.int32),
             pltpu.SemaphoreType.DMA,
         ],
-        compiler_params=pltpu.CompilerParams(vmem_limit_bytes=63 * 1024 * 1024),
+        compiler_params=params(63 * 1024 * 1024),
         name="send_rows",
     )(cluster, rows)
 
@@ -168,8 +168,8 @@
     return jnp.where(label >= CPG, empty, label)
 
 
-def row_labels(ends, number):
-    return labels_of(ends, number, 5.0)
+def row_labels(ends, numbers):
+    return jnp.concatenate([labels_of(ends, number, 5.0) for number in numbers], axis=0)
 
 
 def column_labels(ends, number):
@@ -177,64 +177,69 @@
     return jnp.broadcast_to(label, (HEIGHT, LANES)).T[:1]
 
 
-def piece_of(ref, first):
-    return jnp.concatenate(
-        [
-            ref[:, pl.ds(first + part * SHARE, SHARE)].reshape(HEIGHT, LANES)
+class Fetch:
+    def __init__(self, sems):
+        self.sems = sems
+        self.number = 0
+
+    def __call__(self, pairs):
+        copies = []
+        for source, target in pairs:
+            copy = pltpu.make_async_copy(source, target, self.sems.at[self.number])
+            copy.start()
+            copies.append(copy)
+            self.number += 1
+        return copies
+
+    def piece(self, source, first, target):
+        return self(
+            (
+                source.at[:, pl.ds(first + part * SHARE, SHARE)],
+                target.at[:, :, pl.ds(part * LANES, LANES)],
+            )
             for part in range(FEATURE_PARTS)
-        ],
-        axis=1,
-    )
-
-
-def lanes_of(best):
-    return jnp.max(best.T, axis=0, keepdims=True)
+        )
+
+    def block(self, source, target):
+        return [c for k in range(PIECES) for c in self.piece(source, k * PIECE, target.at[k])]
+
+    def ends(self, source, first, target):
+        return self([(source.at[:, pl.ds(first, TAIL)], target)])
+
+
+def wait(copies):
+    for copy in copies:
+        copy.wait()
 
 
 def span(number):
     return slice(number * HEIGHT, (number + 1) * HEIGHT)
 
 
-def scored(rows, mine, columns, labels, numbers, column_best, index=None):
-    best = jnp.full((HEIGHT, LANES), FLOOR, jnp.float32)
-    for number in numbers:
-        score = lax.dot_general(rows, columns[number], NT, preferred_element_type=jnp.float32)
-        match = mine == labels[:, span(number)]
+def rows_of(ref):
+    return ref[...].reshape(-1, D)
+
+
+def lanes_of(best):
+    found = jnp.max(best.T, axis=0, keepdims=True)
+    return [found[:, k : k + HEIGHT] for k in range(0, found.shape[1], HEIGHT)]
+
+
+def scored(rows, mine, columns, labels, column_best=None, index=None):
+    best = jnp.full((rows.shape[0], LANES), FLOOR, jnp.float32)
+    for k, piece in enumerate(columns):
+        score = lax.dot_general(rows, rows_of(piece), NT, preferred_element_type=jnp.float32)
+        match = mine == labels[k]
         if index is not None:
-            column = lax.broadcasted_iota(jnp.int32, (1, HEIGHT), 1) + number * HEIGHT
+            column = lax.broadcasted_iota(jnp.int32, (1, HEIGHT), 1) + k * HEIGHT
             match = match & (index != column)
         score = jnp.where(match, score, FLOOR)
-        for k in range(0, HEIGHT, LANES):
-            best = jnp.maximum(best, score[:, k : k + LANES])
+        for first in range(0, HEIGHT, LANES):
+            best = jnp.maximum(best, score[:, first : first + LANES])
         if column_best is not None:
-            column_best[:, span(number)] = jnp.maximum(
-                column_best[:, span(number)],
-                jnp.max(score.reshape(HEIGHT // 8, 8, HEIGHT), axis=0),
-            )
+            found = jnp.max(score.reshape(-1, 8, HEIGHT), axis=0)
+            column_best[k] = jnp.maximum(column_best[k], found)
     return best
-
-
-def own_kernel(own_ref, peer_ref, best_ref, columns, labels):
-    own_ends = own_ref[:, PIECES * PIECE :]
-    peer_ends = peer_ref[:, PIECES * PIECE :]
-    for number in range(PIECES):
-        columns[0, number] = piece_of(own_ref, number * PIECE)
-        columns[1, number] = piece_of(peer_ref, number * PIECE)
-        labels[0:1, span(number)] = column_labels(own_ends, number)
-        labels[1:2, span(number)] = column_labels(peer_ends, number)
-
-    def visit(number, _):
-        rows = columns[0, number]
-        mine = row_labels(own_ends, number)
-        index = lax.broadcasted_iota(jnp.int32, (HEIGHT, 1), 0) + number * HEIGHT
-        best = jnp.maximum(
-            scored(rows, mine, columns.at[0], labels.at[0:1], range(PIECES), None, index),
-            scored(rows, mine, columns.at[1], labels.at[1:2], range(PIECES), None),
-        )
-        best_ref[number] = lanes_of(best)
-        return 0
-
-    lax.fori_loop(0, PIECES, visit, 0)
 
 
 def estimate(pairs):
@@ -243,79 +248,148 @@
     )
 
 
-BEST = jax.ShapeDtypeStruct((PIECES, 1, HEIGHT), jnp.float32)
+def best_shape(pieces=PIECES):
+    return jax.ShapeDtypeStruct((pieces, 1, HEIGHT), jnp.float32)
+
+
+def rows_scratch(pieces):
+    return pltpu.VMEM((pieces, GROUPS, SHARE, D), jnp.bfloat16)
+
+
+def ends_scratch(number):
+    return pltpu.VMEM((number, GROUPS, TAIL, LANES), jnp.bfloat16)
+
+
+def column_scratch(pieces):
+    return pltpu.VMEM((pieces, 8, HEIGHT), jnp.float32)
+
+
+def kernel_call(kernel, name, pairs, in_specs, out_shape, scratch_shapes, copies):
+    return pl.pallas_call(
+        kernel,
+        in_specs=in_specs,
+        out_specs=(VMEM,) * len(out_shape),
+        out_shape=out_shape,
+        scratch_shapes=[*scratch_shapes, pltpu.SemaphoreType.DMA((copies,))],
+        compiler_params=params(),
+        cost_estimate=estimate(pairs),
+        name=name,
+    )
+
+
+def own_kernel(own_hbm, peer_hbm, best_ref, own, peer, ends, sems):
+    fetch = Fetch(sems)
+    own_ends = fetch.ends(own_hbm, PIECES * PIECE, ends.at[0])
+    peer_ends = fetch.ends(peer_hbm, PIECES * PIECE, ends.at[1])
+    own_copies = fetch.block(own_hbm, own)
+    peer_copies = fetch.block(peer_hbm, peer)
+    wait(own_ends)
+    wait(peer_ends)
+    own_labels = [column_labels(ends[0], k) for k in range(PIECES)]
+    peer_labels = [column_labels(ends[1], k) for k in range(PIECES)]
+    mine = row_labels(ends[0], range(PIECES))
+    index = lax.broadcasted_iota(jnp.int32, (WIDTH, 1), 0)
+    wait(own_copies)
+    best = scored(rows_of(own), mine, [own.at[k] for k in range(PIECES)], own_labels, None, index)
+    wait(peer_copies)
+    found = scored(rows_of(own), mine, [peer.at[k] for k in range(PIECES)], peer_labels)
+    for k, found in enumerate(lanes_of(jnp.maximum(best, found))):
+        best_ref[k] = found
 
 
 def own_best(own, peer):
-    return pl.pallas_call(
+    return kernel_call(
         own_kernel,
-        out_shape=BEST,
-        scratch_shapes=[
-            pltpu.VMEM((2, PIECES, HEIGHT, D), jnp.bfloat16),
-            pltpu.VMEM((8, WIDTH), jnp.float32),
-        ],
-        compiler_params=params(),
-        cost_estimate=estimate(18),
-        name="own_best",
-    )(own, peer)
+        "own_best",
+        18,
+        [ANY, ANY],
+        (best_shape(),),
+        [rows_scratch(PIECES), rows_scratch(PIECES), ends_scratch(2)],
+        2 + 2 * PIECES * FEATURE_PARTS,
+    )(own, peer)[0]
 
 
 def near_kernel(
-    own_ref,
-    peer_ref,
-    below_ref,
-    above_ref,
-    early_ref,
+    own_hbm,
+    peer_hbm,
+    above_hbm,
+    early_hbm,
     old_ref,
     best_ref,
     peer_best_ref,
     below_best_ref,
     above_best_ref,
-    columns,
-    labels,
+    rows,
+    mine_ref,
+    above,
+    labels_ref,
+    below_mine_ref,
+    ends,
     column_best,
+    sems,
 ):
-    above_ends = early_ref[:, EARLY_BLOCK + PIECE :]
-    below_ends = early_ref[:, PIECE:EARLY_BLOCK]
-    columns[0] = piece_of(above_ref, 0)
-    columns[2] = piece_of(early_ref, EARLY_BLOCK)
-    for number in (0, 2):
-        labels[0:1, span(number)] = column_labels(above_ends, number)
+    fetch = Fetch(sems)
+    all_ends = fetch.ends(early_hbm, EARLY_BLOCK + PIECE, ends.at[0])
+    all_ends += fetch.ends(own_hbm, PIECES * PIECE, ends.at[1])
+    all_ends += fetch.ends(peer_hbm, PIECES * PIECE, ends.at[2])
+    all_ends += fetch.ends(early_hbm, PIECE, ends.at[3])
+    above_copies = fetch.piece(above_hbm, 0, above.at[0])
+    above_copies += fetch.piece(early_hbm, EARLY_BLOCK, above.at[1])
+    own_copies = fetch.block(own_hbm, rows.at[pl.ds(0, PIECES)])
+    peer_copies = fetch.block(peer_hbm, rows.at[pl.ds(PIECES, PIECES)])
+    below_copies = fetch.piece(early_hbm, 0, rows.at[2 * PIECES])
     column_best[...] = jnp.full(column_best.shape, FLOOR, jnp.float32)
-
-    def visit(rows, ends, number):
-        mine = row_labels(ends, number)
-        return lanes_of(scored(rows, mine, columns, labels.at[0:1], (0, 2), column_best))
-
-    def one(number, _):
-        first = pl.multiple_of(number * PIECE, PIECE)
-        found = visit(piece_of(own_ref, first), own_ref[:, PIECES * PIECE :], number)
-        best_ref[number] = jnp.maximum(found, old_ref[number])
-        found = visit(piece_of(peer_ref, first), peer_ref[:, PIECES * PIECE :], number)
-        peer_best_ref[number] = found
-        return 0
-
-    lax.fori_loop(0, PIECES, one, 0)
-    below_best_ref[0] = visit(piece_of(below_ref, 0), below_ends, 0)
-    below_best_ref[1] = jnp.full((1, HEIGHT), FLOOR, jnp.float32)
-    below_best_ref[2] = visit(piece_of(early_ref, 0), below_ends, 2)
-    for number in range(PIECES):
-        above_best_ref[number] = jnp.max(column_best[:, span(number)], axis=0, keepdims=True)
-
-
-def near_best(own, peer, below, above, early, old):
-    return pl.pallas_call(
+    wait(all_ends)
+    for k in range(PIECES):
+        labels_ref[0:1, span(k)] = column_labels(ends[0], k)
+    labels = [labels_ref[0:1, span(k)] for k in (0, 2)]
+    columns = [above.at[k] for k in range(2)]
+
+    def visit(first, ends, numbers):
+        mine = row_labels(ends, numbers)
+        mine_ref[first * HEIGHT : (first + len(numbers)) * HEIGHT] = jnp.broadcast_to(
+            mine, (len(numbers) * HEIGHT, LANES)
+        )
+        found = rows_of(rows.at[pl.ds(first, len(numbers))])
+        return lanes_of(scored(found, mine, columns, labels, column_best))
+
+    wait(above_copies)
+    wait(own_copies)
+    for k, found in enumerate(visit(0, ends[1], range(PIECES))):
+        best_ref[k] = jnp.maximum(found, old_ref[k])
+    wait(peer_copies)
+    for k, found in enumerate(visit(PIECES, ends[2], range(PIECES))):
+        peer_best_ref[k] = found
+    wait(below_copies)
+    below_best_ref[0] = visit(2 * PIECES, ends[3], (2,))[0]
+    for k in range(2):
+        above_best_ref[k] = jnp.max(column_best[k], axis=0, keepdims=True)
+    below_mine_ref[...] = jnp.broadcast_to(row_labels(ends[3], range(2)), (2 * HEIGHT, LANES))
+
+
+def near_best(*arrays):
+    return kernel_call(
         near_kernel,
-        out_shape=(BEST,) * 4,
-        scratch_shapes=[
-            pltpu.VMEM((PIECES, HEIGHT, D), jnp.bfloat16),
-            pltpu.VMEM((8, WIDTH), jnp.float32),
-            pltpu.VMEM((8, WIDTH), jnp.float32),
-        ],
-        compiler_params=params(),
-        cost_estimate=estimate(16),
-        name="near_best",
-    )(own, peer, below, above, early, old)
+        "near_best",
+        14,
+        [ANY] * 4 + [VMEM],
+        (
+            best_shape(),
+            best_shape(),
+            best_shape(1),
+            best_shape(2),
+            jax.ShapeDtypeStruct((2 * PIECES + 1, GROUPS, SHARE, D), jnp.bfloat16),
+            jax.ShapeDtypeStruct(((2 * PIECES + 1) * HEIGHT, LANES), jnp.float32),
+            jax.ShapeDtypeStruct((2, GROUPS, SHARE, D), jnp.bfloat16),
+            jax.ShapeDtypeStruct((8, WIDTH), jnp.float32),
+            jax.ShapeDtypeStruct((2 * HEIGHT, LANES), jnp.float32),
+        ),
+        [ends_scratch(4), column_scratch(2)],
+        4 + (2 * PIECES + 3) * FEATURE_PARTS,
+    )(*arrays)
+
+
+TABLE = jax.ShapeDtypeStruct((GROUPS, LANES), jnp.float32)
 
 
 def spread(table, number, row):
@@ -323,70 +397,106 @@
         table[s : s + 1, number * SHARE : (number + 1) * SHARE] = row[:, s * SHARE : (s + 1) * SHARE]
 
 
+def middle_kernel(
+    below_hbm,
+    above,
+    labels_ref,
+    mine_ref,
+    old_above_ref,
+    below_best_ref,
+    above_best_ref,
+    below,
+    kept_mine_ref,
+    column_best,
+    sems,
+):
+    fetch = Fetch(sems)
+    copies = fetch.piece(below_hbm, 0, below.at[0])
+    copies += fetch.piece(below_hbm, PIECE, below.at[1])
+    column_best[...] = jnp.full(column_best.shape, FLOOR, jnp.float32)
+    labels = [labels_ref[0:1, span(k)] for k in (0, 2)]
+    mine = mine_ref[...]
+    kept_mine_ref[...] = mine
+    wait(copies)
+    columns = [above.at[k] for k in range(2)]
+    found = lanes_of(scored(rows_of(below), mine[:, :1], columns, labels, column_best))
+    for k in range(2):
+        below_best_ref[k] = found[k]
+        found_above = jnp.max(column_best[k], axis=0, keepdims=True)
+        above_best_ref[k] = jnp.maximum(found_above, old_above_ref[k])
+
+
+def middle_best(*arrays):
+    return kernel_call(
+        middle_kernel,
+        "middle_best",
+        4,
+        [ANY] + [VMEM] * 4,
+        (
+            best_shape(2),
+            best_shape(2),
+            jax.ShapeDtypeStruct((2, GROUPS, SHARE, D), jnp.bfloat16),
+            jax.ShapeDtypeStruct((2 * HEIGHT, LANES), jnp.float32),
+        ),
+        [column_scratch(2)],
+        2 * FEATURE_PARTS,
+    )(*arrays)
+
+
 def last_kernel(
     slabs_ref,
-    own_ref,
-    peer_ref,
-    below_ref,
-    above_ref,
-    below_late_ref,
-    above_late_ref,
-    early_ref,
+    late_hbm,
+    rows,
+    mine_ref,
+    labels_ref,
+    below,
+    below_mine_ref,
     old_ref,
     old_peer_ref,
+    old_early_ref,
     old_below_ref,
     old_above_ref,
     out_ref,
-    columns,
-    labels,
+    late,
     column_best,
+    sems,
 ):
-    above_ends = early_ref[:, EARLY_BLOCK + PIECE :]
-    below_ends = early_ref[:, PIECE:EARLY_BLOCK]
-    columns[0] = piece_of(above_ref, 0)
-    columns[1] = piece_of(above_late_ref, 0)
-    columns[2] = piece_of(early_ref, EARLY_BLOCK)
-    for number in range(PIECES):
-        labels[0:1, span(number)] = column_labels(above_ends, number)
+    copies = Fetch(sems).piece(late_hbm, 0, late.at[0])
     column_best[...] = jnp.full(column_best.shape, FLOOR, jnp.float32)
-
-    def visit(rows, ends, number, numbers=(1,)):
-        mine = row_labels(ends, number)
-        return lanes_of(scored(rows, mine, columns, labels.at[0:1], numbers, column_best))
-
     out_ref[...] = jnp.full(out_ref.shape, FLOOR, jnp.float32)
+    labels = [labels_ref[0:1, span(1)]]
     tables = [out_ref.at[slabs_ref[k]] for k in range(4)]
-    for number in range(PIECES):
-        found = visit(piece_of(own_ref, number * PIECE), own_ref[:, PIECES * PIECE :], number)
-        spread(tables[0], number, jnp.maximum(found, old_ref[number]))
-    for number in range(PIECES):
-        found = visit(piece_of(peer_ref, number * PIECE), peer_ref[:, PIECES * PIECE :], number)
-        spread(tables[1], number, jnp.maximum(found, old_peer_ref[number]))
-    found = visit(piece_of(below_ref, 0), below_ends, 0)
-    spread(tables[2], 0, jnp.maximum(found, old_below_ref[0]))
-    found = visit(piece_of(early_ref, 0), below_ends, 2)
-    spread(tables[2], 2, jnp.maximum(found, old_below_ref[2]))
-    found = visit(piece_of(below_late_ref, 0), below_ends, 1, range(PIECES))
-    spread(tables[2], 1, found)
-    for number in range(PIECES):
-        found = jnp.max(column_best[:, span(number)], axis=0, keepdims=True)
-        spread(tables[3], number, jnp.maximum(found, old_above_ref[number]))
+    for k in range(2):
+        spread(tables[3], 2 * k, old_above_ref[k])
+
+    def visit(rows, mine):
+        return lanes_of(scored(rows_of(rows), mine[:, :1], [late.at[0]], labels, column_best))
+
+    def part(first, number):
+        mine = mine_ref[first * HEIGHT : (first + number) * HEIGHT]
+        return visit(rows.at[pl.ds(first, number)], mine)
+
+    wait(copies)
+    for k, found in enumerate(part(0, PIECES)):
+        spread(tables[0], k, jnp.maximum(found, old_ref[k]))
+    for k, found in enumerate(part(PIECES, PIECES)):
+        spread(tables[1], k, jnp.maximum(found, old_peer_ref[k]))
+    spread(tables[2], 2, jnp.maximum(part(2 * PIECES, 1)[0], old_early_ref[0]))
+    for k, found in enumerate(visit(below, below_mine_ref[...])):
+        spread(tables[2], k, jnp.maximum(found, old_below_ref[k]))
+    spread(tables[3], 1, jnp.max(column_best[0], axis=0, keepdims=True))
 
 
 def last_best(*arrays):
-    return pl.pallas_call(
+    return kernel_call(
         last_kernel,
-        in_specs=[pl.BlockSpec(memory_space=pltpu.SMEM)] + [VMEM] * 11,
-        out_shape=jax.ShapeDtypeStruct((RING_SIZE, GROUPS, LANES), jnp.float32),
-        scratch_shapes=[
-            pltpu.VMEM((PIECES, HEIGHT, D), jnp.bfloat16),
-            pltpu.VMEM((8, WIDTH), jnp.float32),
-            pltpu.VMEM((8, WIDTH), jnp.float32),
-        ],
-        compiler_params=params(),
-        cost_estimate=estimate(11),
-        name="last_best",
-    )(*arrays)
+        "last_best",
+        9,
+        [pl.BlockSpec(memory_space=pltpu.SMEM), ANY] + [VMEM] * 10,
+        (jax.ShapeDtypeStruct((RING_SIZE, GROUPS, LANES), jnp.float32),),
+        [rows_scratch(1), column_scratch(1)],
+        FEATURE_PARTS,
+    )(*arrays)[0]
 
 
 def pick_kernel(answers_ref, cluster_ref, place_ref, out_ref):
@@ -429,13 +539,15 @@
     )
     own = all_to_plane(sent)
     late = [own[:, k * PIECE : (k + 1) * PIECE] for k in range(PIECES - 1)]
-    below = [lax.ppermute(block, RING, to_above()) for block in late]
     above = [lax.ppermute(block, RING, to_below()) for block in late]
-    early, own = lax.optimization_barrier((early, own))
+    below = lax.ppermute(own[:, :EARLY], RING, to_above())
+    _, own = lax.optimization_barrier((early, own))
     peer = lax.ppermute(own, "c", SWAP)
     early = all_to_plane(early)
     best = own_best(own, peer)
-    bests = near_best(own, peer, below[0], above[0], early, best)
+    best, best_peer, best_early, best_above, rows, mine, columns, labels, below_mine = near_best(
+        own, peer, above[0], early, best
+    )
     z = lax.axis_index("z")
     core = lax.axis_index("c")
     crossed = (z == CROSSED[0]) | (z == CROSSED[1])
@@ -447,8 +559,22 @@
             (z + 1) % 4 * 2 + jnp.where(crossed, 1 - core, core),
         ]
     ).astype(jnp.int32)
+    best_below, best_above, below, below_mine = middle_best(
+        below, columns, labels, below_mine, best_above
+    )
     answers = last_best(
-        slabs, own, peer, below[0], above[0], below[1], above[1], early, *bests
+        slabs,
+        above[1],
+        rows,
+        mine,
+        labels,
+        below,
+        below_mine,
+        best,
+        best_peer,
+        best_early,
+        best_below,
+        best_above,
     )
     answers = lax.all_to_all(
         answers.reshape(RING_SIZE * GROUPS, 1, LANES),

time: 98 us -> 97 us (0.990)
  Pallas kernels: 28.8 us -> 26.6 us
  waiting for transfers between devices: 23 us -> 25.1 us
  local copies, waits for them, and re-layouts: 2.79 us -> 4.1 us
  starting transfers between devices: 24.3 us -> 23 us
  other arithmetic: 1.18 us -> 0.08 us
    ppermute x1, waiting for transfers between devices: 12.9 us -> 0.67 us  [shards(): lax.ppermute(early, RING, to_below())]
    ppermute x1, waiting for transfers between devices: 3.66 us -> 11.8 us  [shards(): lax.ppermute(early, RING, to_above())]
    all_to_all x2, waiting for transfers between devices: 3.4 us -> 10.8 us  [all_to_plane(): return lax.all_to_all(block, PLANE, split_axis=0, concat_axis=0, tiled=True)]
    ppermute x2, starting transfers between devices: 7.02 us -> 4.06 us  [shards(): above = [lax.ppermute(block, RING, to_below()) for block in late]]
    pallas_call x3 -> x4, Pallas kernels: 23 us -> 20.7 us  [the longest x1 7.41 us: own_best(): kernel_call(own_kernel, 'own_best', 18, [ANY, ANY], (best_shape(),), [row...]
    ppermute x1, starting transfers between devices: 0.01 us -> 1.71 us  [shards(): lax.ppermute(early, RING, to_above())]
    ppermute x2 -> x1, starting transfers between devices: 0.01 us -> 1.64 us  [shards(): below = lax.ppermute(own[:, :EARLY], RING, to_above())]
    ppermute x1, starting transfers between devices: 4.68 us -> 3.05 us  [shards(): lax.ppermute(early, RING, to_below())]
  transfers between devices with their start and end apart: 9 -> 8, of which waited for: 6 -> 5; matrix products, arithmetic and copies ran while one was open for 2% -> 4% of each run, Pallas kernels for 17% -> 18%
where the time goes in v5:
time: 97 us; the launch traced here: 96.6 us
  Pallas kernels  26.6 us (27%)
  waiting for transfers between devices  25.1 us (26%)
  starting transfers between devices  23 us (24%)
  blocking collectives  17.6 us (18%)
  local copies, waits for them, and re-layouts  4.1 us (4%)
    all_to_all x1, blocking collectives, shards(): lax.all_to_all(answers.reshape(RING_SIZE * GROUPS, 1, LANES), EVERYWHERE,...  17.6 us
    ppermute x1, waiting for transfers between devices, shards(): lax.ppermute(early, RING, to_above())  11.8 us
    all_to_all x2, starting transfers between devices, all_to_plane(): return lax.all_to_all(block, PLANE, split_axis=0, concat_axis=0, tiled=True)  11.4 us
    all_to_all x2, waiting for transfers between devices, all_to_plane(): return lax.all_to_all(block, PLANE, split_axis=0, concat_axis=0, tiled=True)  10.8 us
    pallas_call x1, Pallas kernels, own_best(): kernel_call(own_kernel, 'own_best', 18, [ANY, ANY], (best_shape(),), [row...  7.41 us
    pallas_call x1, Pallas kernels, near_best(): kernel_call(near_kernel, 'near_best', 14, [ANY] * 4 + [VMEM], (best_shape...  6.84 us
    pallas_call x1, Pallas kernels, send_rows(): pl.pallas_call(send_kernel, in_specs=[ANY, ANY], out_specs=(VMEM, VMEM, A...  4.84 us
    ppermute x2, starting transfers between devices, shards(): above = [lax.ppermute(block, RING, to_below()) for block in late]  4.06 us
  transfers between devices with their start and end apart: 8, of which 5 were waited for; matrix products, arithmetic and copies ran while one was open for 4% of the time, Pallas kernels for 18%

profile of v5, /device:TPU:1, one launch (start us, length us, event | category | flops | bytes accessed | tf_op | source)
XLA Modules:
  0.0 96.6 jit_solution(2037957302237886969)
XLA Ops:
  0.0 4.8 %send_rows.1 = (s32[1,1024]{1,0:T(1,128)}, bf16[16,144,128]{2,1,0:T(8,128)(2,1)}, bf16[16,400,128]{2,1,0:T(8,128)(2,1)}) custom-call(s32[1,1024]{1,0:T(1,128)} %bitcast.12, bf16[1024,512]{1,0:T(8,128)(2,1)} %rows_hbm.1), custom_call_target="tpu_custom_call" | custom-call | tf_op jit(solution)/shard_map/send_rows/pallas_call | solution.py:141
  4.8 0.0 copy-start.2
  4.9 7.7 %all-to-all-start = ((bf16[16,400,128]{2,1,0:T(8,128)(2,1)}), bf16[16,400,128]{2,1,0:T(8,128)(2,1)S(1)}, u32[]{:S(2)}, u32[]{:S(2)}) async-start(bf16[16,400,128]{2,1,0:T(8,128)(2,1)} %get-tuple-element.22), calls=%async_computation | async-start | bytes 3276800 | tf_op jit(solution)/shard_map/all_to_all | solution.py:531
  12.6 0.0 copy-done.2
  12.6 1.7 %collective-permute-start.1 = (bf16[16,144,128]{2,1,0:T(8,128)(2,1)S(1)}, bf16[16,144,128]{2,1,0:T(8,128)(2,1)S(1)}, u32[]{:S(2)}, u32[]{:S(2)}) collective-permute-start(bf16[16,144,128]{2,1,0:T(8,128)(2,1)S(1)} %copy-done.2), channel_id=1, source_target_pairs={{0,1},{1,2},{2,3},{3,0},{8,9},{9,10},{10,11},{11,8},{4,5},{5,6},{6... | collective-permute-start | bytes 1769480 | tf_op jit(solution)/shard_map/ppermute | solution.py:538
  14.3 3.1 %collective-permute-start.2 = (bf16[16,144,128]{2,1,0:T(8,128)(2,1)S(1)}, bf16[16,144,128]{2,1,0:T(8,128)(2,1)S(1)}, u32[]{:S(2)}, u32[]{:S(2)}) collective-permute-start(bf16[16,144,128]{2,1,0:T(8,128)(2,1)S(1)} %copy-done.2), channel_id=1, source_target_pairs={{0,11},{1,8},{2,1},{3,2},{8,3},{9,0},{10,9},{11,10},{4,15},{5,12},... | collective-permute-start | bytes 1769480 | tf_op jit(solution)/shard_map/ppermute | solution.py:538
  17.4 11.8 %collective-permute-done.1 = bf16[16,144,128]{2,1,0:T(8,128)(2,1)S(1)} collective-permute-done((bf16[16,144,128]{2,1,0:T(8,128)(2,1)S(1)}, bf16[16,144,128]{2,1,0:T(8,128)(2,1)S(1)}, u32[]{:S(2)}, u32[]{:S(2)}) %collective-permute-start.1) | collective-permute-done | bytes 589856 | tf_op jit(solution)/shard_map/ppermute | solution.py:538
  29.2 0.9 constant_dynamic-update-slice_fusion.1
  30.1 0.7 collective-permute-done.2
  30.8 1.0 constant_dynamic-update-slice_fusion
  31.7 6.2 %all-to-all-done.own_hbm = bf16[16,400,128]{2,1,0:T(8,128)(2,1)S(1)} async-done(((bf16[16,400,128]{2,1,0:T(8,128)(2,1)}), bf16[16,400,128]{2,1,0:T(8,128)(2,1)S(1)}, u32[]{:S(2)}, u32[]{:S(2)}) %all-to-all-start) | async-done | bytes 1638432 | tf_op jit(solution)/shard_map/all_to_all | solution.py:531
  37.9 1.1 %collective-permute-start.3 = (bf16[16,400,128]{2,1,0:T(8,128)(2,1)S(1)}, bf16[16,400,128]{2,1,0:T(8,128)(2,1)}, u32[]{:S(2)}, u32[]{:S(2)}) collective-permute-start(bf16[16,400,128]{2,1,0:T(8,128)(2,1)S(1)} %all-to-all-done.own_hbm), channel_id=1, source_target_pairs={{0,8},{8,0},{1,9},{9,1},{2,10},{10,2},{3,11},{11,3},{4,12},{12,4},... | collective-permute-start | bytes 4915208 | tf_op jit(solution)/shard_map/ppermute | solution.py:545
  39.1 3.7 %all-to-all-start.1 = ((bf16[16,288,128]{2,1,0:T(8,128)(2,1)}), bf16[16,288,128]{2,1,0:T(8,128)(2,1)S(1)}, u32[]{:S(2)}, u32[]{:S(2)}) async-start(bf16[16,288,128]{2,1,0:T(8,128)(2,1)} %constant_dynamic-update-slice_fusion), calls=%async_computation.1 | async-start | bytes 2359296 | tf_op jit(solution)/shard_map/all_to_all | solution.py:531
  42.8 1.1 %slice.14 = bf16[16,256,128]{2,1,0:T(8,128)(2,1)} slice(bf16[16,400,128]{2,1,0:T(8,128)(2,1)S(1)} %all-to-all-done.own_hbm), slice={[0:16], [0:256], [0:128]} | slice | bytes 2097152 | tf_op jit(solution)/shard_map/slice | solution.py:543
  43.9 1.6 %collective-permute-start.5 = (bf16[16,256,128]{2,1,0:T(8,128)(2,1)}, bf16[16,256,128]{2,1,0:T(8,128)(2,1)}, u32[]{:S(2)}, u32[]{:S(2)}) collective-permute-start(bf16[16,256,128]{2,1,0:T(8,128)(2,1)} %slice.14), channel_id=1, source_target_pairs={{0,1},{1,2},{2,3},{3,0},{8,9},{9,10},{10,11},{11,8},{4,5},{5,6},{6... | collective-permute-start | bytes 3145736 | tf_op jit(solution)/shard_map/ppermute | solution.py:543
  45.5 1.1 %fusion = (bf16[16,128,128]{2,1,0:T(8,128)(2,1)}, bf16[16,128,128]{2,1,0:T(8,128)(2,1)}) fusion(bf16[16,400,128]{2,1,0:T(8,128)(2,1)S(1)} %all-to-all-done.own_hbm), kind=kLoop, calls=%fused_computation.3 | loop fusion | bytes 2097152 | tf_op jit(solution)/shard_map/slice | solution.py:541
  46.6 2.0 %collective-permute-start.4 = (bf16[16,128,128]{2,1,0:T(8,128)(2,1)}, bf16[16,128,128]{2,1,0:T(8,128)(2,1)}, u32[]{:S(2)}, u32[]{:S(2)}) collective-permute-start(bf16[16,128,128]{2,1,0:T(8,128)(2,1)} %get-tuple-element.39), channel_id=1, source_target_pairs={{0,11},{1,8},{2,1},{3,2},{8,3},{9,0},{10,9},{11,10},{4,15},{5,12},... | collective-permute-start | bytes 1572872 | tf_op jit(solution)/shard_map/ppermute | solution.py:542
  48.7 0.1 pad_add_fusion.slabs_ref
  48.7 2.0 %collective-permute-start = (bf16[16,128,128]{2,1,0:T(8,128)(2,1)}, bf16[16,128,128]{2,1,0:T(8,128)(2,1)S(1)}, u32[]{:S(2)}, u32[]{:S(2)}) collective-permute-start(bf16[16,128,128]{2,1,0:T(8,128)(2,1)} %get-tuple-element.40), channel_id=1, source_target_pairs={{0,11},{1,8},{2,1},{3,2},{8,3},{9,0},{10,9},{11,10},{4,15},{5,12},... | collective-permute-start | bytes 1572872 | tf_op jit(solution)/shard_map/ppermute | solution.py:542
  50.8 0.0 collective-permute-done.3.peer_hbm
  50.8 7.4 %own_best.1.old_ref = f32[3,1,512]{2,1,0:T(1,128)S(1)} custom-call(bf16[16,400,128]{2,1,0:T(8,128)(2,1)S(1)} %all-to-all-done.own_hbm, bf16[16,400,128]{2,1,0:T(8,128)(2,1)} %collective-permute-done.3.peer_hbm), custom_call_target="tpu_custom_call" | custom-call | flops 4831838208 | bytes 6291456 | tf_op jit(solution)/shard_map/own_best/pallas_call | solution.py:301
  58.2 4.6 %all-to-all-done.1.early_hbm = bf16[16,288,128]{2,1,0:T(8,128)(2,1)S(1)} async-done(((bf16[16,288,128]{2,1,0:T(8,128)(2,1)}), bf16[16,288,128]{2,1,0:T(8,128)(2,1)S(1)}, u32[]{:S(2)}, u32[]{:S(2)}) %all-to-all-start.1) | async-done | bytes 1179680 | tf_op jit(solution)/shard_map/all_to_all | solution.py:531
  62.8 0.0 collective-permute-done.4.above_hbm
  62.8 6.8 %near_best.1 = (f32[3,1,512]{2,1,0:T(1,128)S(1)}, f32[3,1,512]{2,1,0:T(1,128)S(1)}, f32[1,1,512]{2,1,0:T(1,128)S(1)}, f32[2,1,512]{2,1,0:T(1,128)S(1)}, bf16[7,1...) custom-call(bf16[16,400,128]{2,1,0:T(8,128)(2,1)S(1)} %all-to-all-do, ...), custom_call_target="tpu_custom_call" | custom-call | flops 3758096384 | bytes 6291456 | tf_op jit(solution)/shard_map/near_best/pallas_call | solution.py:371
  69.6 1.9 %collective-permute-done.5.below_hbm = bf16[16,256,128]{2,1,0:T(8,128)(2,1)} collective-permute-done((bf16[16,256,128]{2,1,0:T(8,128)(2,1)}, bf16[16,256,128]{2,1,0:T(8,128)(2,1)}, u32[]{:S(2)}, u32[]{:S(2)}) %collective-permute-start.5) | collective-permute-done | bytes 1048608 | tf_op jit(solution)/shard_map/ppermute | solution.py:543
  71.5 2.8 %middle_best.1 = (f32[2,1,512]{2,1,0:T(1,128)S(1)}, f32[2,1,512]{2,1,0:T(1,128)S(1)}, bf16[2,16,32,512]{3,2,1,0:T(8,128)(2,1)S(1)}, f32[1024,128]{1,0:T(8,128)S(1)}) custom-call(bf16[16,256,128]{2,1,0:T(8,128)(2,1)} %collective-permute-done.5.below_hbm, bf16[2,16,32,512]{3,2,1,0:T(8,128)(2,1)S(1)} %get-tuple-element.28.above, ...), custom_call_target="tpu_custom_call" | custom-call | flops 1073741824 | bytes 6291456 | tf_op jit(solution)/shard_map/middle_best/pallas_call | solution.py:430
  74.3 0.0 collective-permute-done.late_hbm
  74.3 0.0 copy-start
  74.3 0.0 copy-start.1
  74.3 3.7 %last_best.1 = f32[8,16,128]{2,1,0:T(8,128)S(1)} custom-call(s32[4]{0:T(128)S(1)} %pad_add_fusion.slabs_ref, bf16[16,128,128]{2,1,0:T(8,128)(2,1)S(1)} %collective-permute-done.late_hbm, bf16[7,16,32,512]{3,2,1,0:T(8,128)(2,1)S(1)} %get-tuple-element.25.rows, f32[3584,128]{1,0:T(8,128)S(1)} %get-tuple-element.26.mine_ref, ...), custom_call_target="tpu_custom_call" | custom-call | flops 2415919104 | bytes 6291456 | tf_op jit(solution)/shard_map/last_best/pallas_call | solution.py:491
  78.0 17.6 %all_to_all.15 = f32[128,1,128]{2,1,0:T(1,128)S(1)} all-to-all(f32[128,1,128]{2,1,0:T(1,128)S(1)} %bitcast.11), channel_id=1, replica_groups=mesh['yh'=2,'x'=4,'c'=2,'yl'=2,'z'=4] {'z','c','yh','x','yl'}, dimensions={0} | all-to-all | bytes 131072 | tf_op jit(solution)/shard_map/all_to_all | solution.py:579
  95.6 0.0 copy-done
  95.6 0.0 copy-done.1
  95.6 1.0 %picked.1 = f32[1,1024]{1,0:T(1,128)} custom-call(f32[8,16,128]{2,1,0:T(8,128)S(1)} %bitcast.10, s32[1,1024]{1,0:T(1,128)S(1)} %bitcast.13, s32[1,1024]{1,0:T(1,128)S(1)} %copy-done.1), custom_call_target="tpu_custom_call" | custom-call | tf_op jit(solution)/shard_map/picked/pallas_call | solution.py:519
Async XLA Ops:
  4.8 7.7 %copy-start.2 = (bf16[16,144,128]{2,1,0:T(8,128)(2,1)S(1)}, bf16[16,144,128]{2,1,0:T(8,128)(2,1)}, u32[]{:S(2)}) copy-start(bf16[16,144,128]{2,1,0:T(8,128)(2,1)} %get-tuple-element.23) | copy-start | bytes 1769476
  4.9 33.1 %all-to-all-start = ((bf16[16,400,128]{2,1,0:T(8,128)(2,1)}), bf16[16,400,128]{2,1,0:T(8,128)(2,1)S(1)}, u32[]{:S(2)}, u32[]{:S(2)}) async-start(bf16[16,400,128]{2,1,0:T(8,128)(2,1)} %get-tuple-element.22), calls=%async_computation | async-start | bytes 3276800 | tf_op jit(solution)/shard_map/all_to_all | solution.py:531
  12.6 16.6 %collective-permute-start.1 = (bf16[16,144,128]{2,1,0:T(8,128)(2,1)S(1)}, bf16[16,144,128]{2,1,0:T(8,128)(2,1)S(1)}, u32[]{:S(2)}, u32[]{:S(2)}) collective-permute-start(bf16[16,144,128]{2,1,0:T(8,128)(2,1)S(1)} %copy-done.2), channel_id=1, source_target_pairs={{0,1},{1,2},{2,3},{3,0},{8,9},{9,10},{10,11},{11,8},{4,5},{5,6},{6... | collective-permute-start | bytes 1769480 | tf_op jit(solution)/shard_map/ppermute | solution.py:538
  14.3 16.5 %collective-permute-start.2 = (bf16[16,144,128]{2,1,0:T(8,128)(2,1)S(1)}, bf16[16,144,128]{2,1,0:T(8,128)(2,1)S(1)}, u32[]{:S(2)}, u32[]{:S(2)}) collective-permute-start(bf16[16,144,128]{2,1,0:T(8,128)(2,1)S(1)} %copy-done.2), channel_id=1, source_target_pairs={{0,11},{1,8},{2,1},{3,2},{8,3},{9,0},{10,9},{11,10},{4,15},{5,12},... | collective-permute-start | bytes 1769480 | tf_op jit(solution)/shard_map/ppermute | solution.py:538
  37.9 12.8 %collective-permute-start.3 = (bf16[16,400,128]{2,1,0:T(8,128)(2,1)S(1)}, bf16[16,400,128]{2,1,0:T(8,128)(2,1)}, u32[]{:S(2)}, u32[]{:S(2)}) collective-permute-start(bf16[16,400,128]{2,1,0:T(8,128)(2,1)S(1)} %all-to-all-done.own_hbm), channel_id=1, source_target_pairs={{0,8},{8,0},{1,9},{9,1},{2,10},{10,2},{3,11},{11,3},{4,12},{12,4},... | collective-permute-start | bytes 4915208 | tf_op jit(solution)/shard_map/ppermute | solution.py:545
  39.1 23.7 %all-to-all-start.1 = ((bf16[16,288,128]{2,1,0:T(8,128)(2,1)}), bf16[16,288,128]{2,1,0:T(8,128)(2,1)S(1)}, u32[]{:S(2)}, u32[]{:S(2)}) async-start(bf16[16,288,128]{2,1,0:T(8,128)(2,1)} %constant_dynamic-update-slice_fusion), calls=%async_computation.1 | async-start | bytes 2359296 | tf_op jit(solution)/shard_map/all_to_all | solution.py:531
  43.9 27.6 %collective-permute-start.5 = (bf16[16,256,128]{2,1,0:T(8,128)(2,1)}, bf16[16,256,128]{2,1,0:T(8,128)(2,1)}, u32[]{:S(2)}, u32[]{:S(2)}) collective-permute-start(bf16[16,256,128]{2,1,0:T(8,128)(2,1)} %slice.14), channel_id=1, source_target_pairs={{0,1},{1,2},{2,3},{3,0},{8,9},{9,10},{10,11},{11,8},{4,5},{5,6},{6... | collective-permute-start | bytes 3145736 | tf_op jit(solution)/shard_map/ppermute | solution.py:543
  46.6 16.2 %collective-permute-start.4 = (bf16[16,128,128]{2,1,0:T(8,128)(2,1)}, bf16[16,128,128]{2,1,0:T(8,128)(2,1)}, u32[]{:S(2)}, u32[]{:S(2)}) collective-permute-start(bf16[16,128,128]{2,1,0:T(8,128)(2,1)} %get-tuple-element.39), channel_id=1, source_target_pairs={{0,11},{1,8},{2,1},{3,2},{8,3},{9,0},{10,9},{11,10},{4,15},{5,12},... | collective-permute-start | bytes 1572872 | tf_op jit(solution)/shard_map/ppermute | solution.py:542
  48.7 25.5 %collective-permute-start = (bf16[16,128,128]{2,1,0:T(8,128)(2,1)}, bf16[16,128,128]{2,1,0:T(8,128)(2,1)S(1)}, u32[]{:S(2)}, u32[]{:S(2)}) collective-permute-start(bf16[16,128,128]{2,1,0:T(8,128)(2,1)} %get-tuple-element.40), channel_id=1, source_target_pairs={{0,11},{1,8},{2,1},{3,2},{8,3},{9,0},{10,9},{11,10},{4,15},{5,12},... | collective-permute-start | bytes 1572872 | tf_op jit(solution)/shard_map/ppermute | solution.py:542
  74.3 21.3 %copy-start = (s32[1024]{0:T(1024)S(1)}, s32[1024]{0:T(1024)}, u32[]{:S(2)}) copy-start(s32[1024]{0:T(1024)} %param.3) | copy-start | bytes 12292
  74.3 21.3 %copy-start.1 = (s32[1,1024]{1,0:T(1,128)S(1)}, s32[1,1024]{1,0:T(1,128)}, u32[]{:S(2)}) copy-start(s32[1,1024]{1,0:T(1,128)} %get-tuple-element.38.place_ref) | copy-start | bytes 12292

commit v6 on v5

--- a/solution.py
+++ b/solution.py
@@ -329,19 +329,19 @@
     sems,
 ):
     fetch = Fetch(sems)
-    all_ends = fetch.ends(early_hbm, EARLY_BLOCK + PIECE, ends.at[0])
+    all_ends = fetch.ends(early_hbm, 2 * PIECE, ends.at[0])
     all_ends += fetch.ends(own_hbm, PIECES * PIECE, ends.at[1])
     all_ends += fetch.ends(peer_hbm, PIECES * PIECE, ends.at[2])
-    all_ends += fetch.ends(early_hbm, PIECE, ends.at[3])
     above_copies = fetch.piece(above_hbm, 0, above.at[0])
-    above_copies += fetch.piece(early_hbm, EARLY_BLOCK, above.at[1])
+    above_copies += fetch.piece(early_hbm, PIECE, above.at[1])
     own_copies = fetch.block(own_hbm, rows.at[pl.ds(0, PIECES)])
     peer_copies = fetch.block(peer_hbm, rows.at[pl.ds(PIECES, PIECES)])
     below_copies = fetch.piece(early_hbm, 0, rows.at[2 * PIECES])
     column_best[...] = jnp.full(column_best.shape, FLOOR, jnp.float32)
     wait(all_ends)
+    above_ends = ends[0].astype(jnp.float32)[:, TAIL // 2 :]
     for k in range(PIECES):
-        labels_ref[0:1, span(k)] = column_labels(ends[0], k)
+        labels_ref[0:1, span(k)] = column_labels(above_ends, k)
     labels = [labels_ref[0:1, span(k)] for k in (0, 2)]
     columns = [above.at[k] for k in range(2)]
 
@@ -361,10 +361,10 @@
     for k, found in enumerate(visit(PIECES, ends[2], range(PIECES))):
         peer_best_ref[k] = found
     wait(below_copies)
-    below_best_ref[0] = visit(2 * PIECES, ends[3], (2,))[0]
+    below_best_ref[0] = visit(2 * PIECES, ends[0], (2,))[0]
     for k in range(2):
         above_best_ref[k] = jnp.max(column_best[k], axis=0, keepdims=True)
-    below_mine_ref[...] = jnp.broadcast_to(row_labels(ends[3], range(2)), (2 * HEIGHT, LANES))
+    below_mine_ref[...] = jnp.broadcast_to(row_labels(ends[0], range(2)), (2 * HEIGHT, LANES))
 
 
 def near_best(*arrays):
@@ -384,8 +384,8 @@
             jax.ShapeDtypeStruct((8, WIDTH), jnp.float32),
             jax.ShapeDtypeStruct((2 * HEIGHT, LANES), jnp.float32),
         ),
-        [ends_scratch(4), column_scratch(2)],
-        4 + (2 * PIECES + 3) * FEATURE_PARTS,
+        [ends_scratch(3), column_scratch(2)],
+        3 + (2 * PIECES + 3) * FEATURE_PARTS,
     )(*arrays)
 
 
@@ -534,8 +534,11 @@
 def shards(embeddings, cluster):
     cluster = cluster.reshape(1, ROWS)
     place, early, sent = send_rows(cluster, embeddings)
+    under = lax.ppermute(early, RING, to_above())
+    over = lax.ppermute(early, RING, to_below())
+    half = PIECE + TAIL // 2
     early = jnp.concatenate(
-        [lax.ppermute(early, RING, to_above()), lax.ppermute(early, RING, to_below())], axis=1
+        [under[:, :PIECE], over[:, :PIECE], under[:, PIECE:half], over[:, PIECE:half]], axis=1
     )
     own = all_to_plane(sent)
     late = [own[:, k * PIECE : (k + 1) * PIECE] for k in range(PIECES - 1)]

time: 97 us -> 97 us (level)
  local copies, waits for them, and re-layouts: 4.1 us -> 2.3 us
  other arithmetic: 0.08 us -> 1.16 us
    concatenate x0 -> x1, other arithmetic: none -> 1.09 us  [shards(): jnp.concatenate([under[:, :PIECE], over[:, :PIECE], under[:, PIECE:half],...]
    all_to_all x2, waiting for transfers between devices: 10.8 us -> 9.79 us  [all_to_plane(): return lax.all_to_all(block, PLANE, split_axis=0, concat_axis=0, tiled=True)]
where the time goes in v6:
time: 97 us; the launch traced here: 96.6 us
  Pallas kernels  26.7 us (28%)
  waiting for transfers between devices  25.7 us (26%)
  starting transfers between devices  23 us (24%)
  blocking collectives  17.6 us (18%)
  local copies, waits for them, and re-layouts  2.3 us (2%)
  other arithmetic  1.16 us (1%)
    all_to_all x1, blocking collectives, shards(): lax.all_to_all(answers.reshape(RING_SIZE * GROUPS, 1, LANES), EVERYWHERE,...  17.6 us
    ppermute x1, waiting for transfers between devices, shards(): under = lax.ppermute(early, RING, to_above())  11.8 us
    all_to_all x2, starting transfers between devices, all_to_plane(): return lax.all_to_all(block, PLANE, split_axis=0, concat_axis=0, tiled=True)  11.4 us
    all_to_all x2, waiting for transfers between devices, all_to_plane(): return lax.all_to_all(block, PLANE, split_axis=0, concat_axis=0, tiled=True)  9.79 us
    pallas_call x1, Pallas kernels, own_best(): kernel_call(own_kernel, 'own_best', 18, [ANY, ANY], (best_shape(),), [row...  7.41 us
    pallas_call x1, Pallas kernels, near_best(): kernel_call(near_kernel, 'near_best', 14, [ANY] * 4 + [VMEM], (best_shape...  7 us
    pallas_call x1, Pallas kernels, send_rows(): pl.pallas_call(send_kernel, in_specs=[ANY, ANY], out_specs=(VMEM, VMEM, A...  4.84 us
    ppermute x2, starting transfers between devices, shards(): above = [lax.ppermute(block, RING, to_below()) for block in late]  4.06 us
  transfers between devices with their start and end apart: 8, of which 5 were waited for; matrix products, arithmetic and copies ran while one was open for 4% of the time, Pallas kernels for 18%

profile of v6, /device:TPU:1, one launch (start us, length us, event | category | flops | bytes accessed | tf_op | source)
XLA Modules:
  0.0 96.6 jit_solution(11717226921596429291)
XLA Ops:
  0.0 4.8 %send_rows.1 = (s32[1,1024]{1,0:T(1,128)}, bf16[16,144,128]{2,1,0:T(8,128)(2,1)}, bf16[16,400,128]{2,1,0:T(8,128)(2,1)}) custom-call(s32[1,1024]{1,0:T(1,128)} %bitcast.12, bf16[1024,512]{1,0:T(8,128)(2,1)} %rows_hbm.1), custom_call_target="tpu_custom_call" | custom-call | tf_op jit(solution)/shard_map/send_rows/pallas_call | solution.py:141
  4.8 0.0 copy-start.2
  4.9 7.7 %all-to-all-start = ((bf16[16,400,128]{2,1,0:T(8,128)(2,1)}), bf16[16,400,128]{2,1,0:T(8,128)(2,1)S(1)}, u32[]{:S(2)}, u32[]{:S(2)}) async-start(bf16[16,400,128]{2,1,0:T(8,128)(2,1)} %get-tuple-element.22), calls=%async_computation | async-start | bytes 3276800 | tf_op jit(solution)/shard_map/all_to_all | solution.py:531
  12.6 0.0 copy-done.2
  12.6 1.7 %collective-permute-start.1 = (bf16[16,144,128]{2,1,0:T(8,128)(2,1)S(1)}, bf16[16,144,128]{2,1,0:T(8,128)(2,1)S(1)}, u32[]{:S(2)}, u32[]{:S(2)}) collective-permute-start(bf16[16,144,128]{2,1,0:T(8,128)(2,1)S(1)} %copy-done.2), channel_id=1, source_target_pairs={{0,1},{1,2},{2,3},{3,0},{8,9},{9,10},{10,11},{11,8},{4,5},{5,6},{6... | collective-permute-start | bytes 1769480 | tf_op jit(solution)/shard_map/ppermute | solution.py:537
  14.3 3.1 %collective-permute-start.2 = (bf16[16,144,128]{2,1,0:T(8,128)(2,1)S(1)}, bf16[16,144,128]{2,1,0:T(8,128)(2,1)S(1)}, u32[]{:S(2)}, u32[]{:S(2)}) collective-permute-start(bf16[16,144,128]{2,1,0:T(8,128)(2,1)S(1)} %copy-done.2), channel_id=1, source_target_pairs={{0,11},{1,8},{2,1},{3,2},{8,3},{9,0},{10,9},{11,10},{4,15},{5,12},... | collective-permute-start | bytes 1769480 | tf_op jit(solution)/shard_map/ppermute | solution.py:538
  17.4 11.8 %collective-permute-done.1 = bf16[16,144,128]{2,1,0:T(8,128)(2,1)S(1)} collective-permute-done((bf16[16,144,128]{2,1,0:T(8,128)(2,1)S(1)}, bf16[16,144,128]{2,1,0:T(8,128)(2,1)S(1)}, u32[]{:S(2)}, u32[]{:S(2)}) %collective-permute-start.1) | collective-permute-done | bytes 589856 | tf_op jit(solution)/shard_map/ppermute | solution.py:537
  29.2 1.6 %collective-permute-done.2 = bf16[16,144,128]{2,1,0:T(8,128)(2,1)S(1)} collective-permute-done((bf16[16,144,128]{2,1,0:T(8,128)(2,1)S(1)}, bf16[16,144,128]{2,1,0:T(8,128)(2,1)S(1)}, u32[]{:S(2)}, u32[]{:S(2)}) %collective-permute-start.2) | collective-permute-done | bytes 589856 | tf_op jit(solution)/shard_map/ppermute | solution.py:538
  30.8 1.1 %pad_maximum_fusion = bf16[16,272,128]{2,1,0:T(8,128)(2,1)} fusion(bf16[16,8,128]{2,1,0:T(8,128)(2,1)S(1)} %slice.32, bf16[16,8,128]{2,1,0:T(8,128)(2,1)S(1)} %slice.31, bf16[16,128,128]{2,1,0:T(8,128)(2,1)S(1)} %slice.30, bf16[16,128,128]{2,1,0:T(8,128)(2,1)S(1)} %slice.29), kind=kLoop, calls=%fused_computation | loop fusion | flops 4456448 | bytes 2228224 | tf_op jit(solution)/shard_map/concatenate | solution.py:540
  31.9 6.0 %all-to-all-done.own_hbm = bf16[16,400,128]{2,1,0:T(8,128)(2,1)S(1)} async-done(((bf16[16,400,128]{2,1,0:T(8,128)(2,1)}), bf16[16,400,128]{2,1,0:T(8,128)(2,1)S(1)}, u32[]{:S(2)}, u32[]{:S(2)}) %all-to-all-start) | async-done | bytes 1638432 | tf_op jit(solution)/shard_map/all_to_all | solution.py:531
  37.9 1.1 %collective-permute-start.3 = (bf16[16,400,128]{2,1,0:T(8,128)(2,1)S(1)}, bf16[16,400,128]{2,1,0:T(8,128)(2,1)}, u32[]{:S(2)}, u32[]{:S(2)}) collective-permute-start(bf16[16,400,128]{2,1,0:T(8,128)(2,1)S(1)} %all-to-all-done.own_hbm), channel_id=1, source_target_pairs={{0,8},{8,0},{1,9},{9,1},{2,10},{10,2},{3,11},{11,3},{4,12},{12,4},... | collective-permute-start | bytes 4915208 | tf_op jit(solution)/shard_map/ppermute | solution.py:548
  39.1 3.7 %all-to-all-start.1 = ((bf16[16,272,128]{2,1,0:T(8,128)(2,1)}), bf16[16,272,128]{2,1,0:T(8,128)(2,1)S(1)}, u32[]{:S(2)}, u32[]{:S(2)}) async-start(bf16[16,272,128]{2,1,0:T(8,128)(2,1)} %pad_maximum_fusion), calls=%async_computation.1 | async-start | bytes 2228224 | tf_op jit(solution)/shard_map/all_to_all | solution.py:531
  42.8 1.1 %slice.34 = bf16[16,256,128]{2,1,0:T(8,128)(2,1)} slice(bf16[16,400,128]{2,1,0:T(8,128)(2,1)S(1)} %all-to-all-done.own_hbm), slice={[0:16], [0:256], [0:128]} | slice | bytes 2097152 | tf_op jit(solution)/shard_map/slice | solution.py:546
  43.9 1.6 %collective-permute-start.5 = (bf16[16,256,128]{2,1,0:T(8,128)(2,1)}, bf16[16,256,128]{2,1,0:T(8,128)(2,1)}, u32[]{:S(2)}, u32[]{:S(2)}) collective-permute-start(bf16[16,256,128]{2,1,0:T(8,128)(2,1)} %slice.34), channel_id=1, source_target_pairs={{0,1},{1,2},{2,3},{3,0},{8,9},{9,10},{10,11},{11,8},{4,5},{5,6},{6... | collective-permute-start | bytes 3145736 | tf_op jit(solution)/shard_map/ppermute | solution.py:546
  45.5 1.1 %fusion = (bf16[16,128,128]{2,1,0:T(8,128)(2,1)}, bf16[16,128,128]{2,1,0:T(8,128)(2,1)}) fusion(bf16[16,400,128]{2,1,0:T(8,128)(2,1)S(1)} %all-to-all-done.own_hbm), kind=kLoop, calls=%fused_computation.2 | loop fusion | bytes 2097152 | tf_op jit(solution)/shard_map/slice | solution.py:544
  46.6 2.0 %collective-permute-start.4 = (bf16[16,128,128]{2,1,0:T(8,128)(2,1)}, bf16[16,128,128]{2,1,0:T(8,128)(2,1)}, u32[]{:S(2)}, u32[]{:S(2)}) collective-permute-start(bf16[16,128,128]{2,1,0:T(8,128)(2,1)} %get-tuple-element.39), channel_id=1, source_target_pairs={{0,11},{1,8},{2,1},{3,2},{8,3},{9,0},{10,9},{11,10},{4,15},{5,12},... | collective-permute-start | bytes 1572872 | tf_op jit(solution)/shard_map/ppermute | solution.py:545
  48.7 0.1 pad_add_fusion.slabs_ref
  48.7 2.0 %collective-permute-start = (bf16[16,128,128]{2,1,0:T(8,128)(2,1)}, bf16[16,128,128]{2,1,0:T(8,128)(2,1)S(1)}, u32[]{:S(2)}, u32[]{:S(2)}) collective-permute-start(bf16[16,128,128]{2,1,0:T(8,128)(2,1)} %get-tuple-element.40), channel_id=1, source_target_pairs={{0,11},{1,8},{2,1},{3,2},{8,3},{9,0},{10,9},{11,10},{4,15},{5,12},... | collective-permute-start | bytes 1572872 | tf_op jit(solution)/shard_map/ppermute | solution.py:545
  50.8 0.0 collective-permute-done.3.peer_hbm
  50.8 7.4 %own_best.1.old_ref = f32[3,1,512]{2,1,0:T(1,128)S(1)} custom-call(bf16[16,400,128]{2,1,0:T(8,128)(2,1)S(1)} %all-to-all-done.own_hbm, bf16[16,400,128]{2,1,0:T(8,128)(2,1)} %collective-permute-done.3.peer_hbm), custom_call_target="tpu_custom_call" | custom-call | flops 4831838208 | bytes 6291456 | tf_op jit(solution)/shard_map/own_best/pallas_call | solution.py:301
  58.2 3.8 %all-to-all-done.1.early_hbm = bf16[16,272,128]{2,1,0:T(8,128)(2,1)S(1)} async-done(((bf16[16,272,128]{2,1,0:T(8,128)(2,1)}), bf16[16,272,128]{2,1,0:T(8,128)(2,1)S(1)}, u32[]{:S(2)}, u32[]{:S(2)}) %all-to-all-start.1) | async-done | bytes 1114144 | tf_op jit(solution)/shard_map/all_to_all | solution.py:531
  62.0 0.0 collective-permute-done.4.above_hbm
  62.0 7.0 %near_best.1 = (f32[3,1,512]{2,1,0:T(1,128)S(1)}, f32[3,1,512]{2,1,0:T(1,128)S(1)}, f32[1,1,512]{2,1,0:T(1,128)S(1)}, f32[2,1,512]{2,1,0:T(1,128)S(1)}, bf16[7,1...) custom-call(bf16[16,400,128]{2,1,0:T(8,128)(2,1)S(1)} %all-to-all-do, ...), custom_call_target="tpu_custom_call" | custom-call | flops 3758096384 | bytes 6291456 | tf_op jit(solution)/shard_map/near_best/pallas_call | solution.py:371
  69.0 2.5 %collective-permute-done.5.below_hbm = bf16[16,256,128]{2,1,0:T(8,128)(2,1)} collective-permute-done((bf16[16,256,128]{2,1,0:T(8,128)(2,1)}, bf16[16,256,128]{2,1,0:T(8,128)(2,1)}, u32[]{:S(2)}, u32[]{:S(2)}) %collective-permute-start.5) | collective-permute-done | bytes 1048608 | tf_op jit(solution)/shard_map/ppermute | solution.py:546
  71.5 2.8 %middle_best.1 = (f32[2,1,512]{2,1,0:T(1,128)S(1)}, f32[2,1,512]{2,1,0:T(1,128)S(1)}, bf16[2,16,32,512]{3,2,1,0:T(8,128)(2,1)S(1)}, f32[1024,128]{1,0:T(8,128)S(1)}) custom-call(bf16[16,256,128]{2,1,0:T(8,128)(2,1)} %collective-permute-done.5.below_hbm, bf16[2,16,32,512]{3,2,1,0:T(8,128)(2,1)S(1)} %get-tuple-element.28.above, ...), custom_call_target="tpu_custom_call" | custom-call | flops 1073741824 | bytes 6291456 | tf_op jit(solution)/shard_map/middle_best/pallas_call | solution.py:430
  74.3 0.0 collective-permute-done.late_hbm
  74.3 0.0 copy-start
  74.3 0.0 copy-start.1
  74.3 3.7 %last_best.1 = f32[8,16,128]{2,1,0:T(8,128)S(1)} custom-call(s32[4]{0:T(128)S(1)} %pad_add_fusion.slabs_ref, bf16[16,128,128]{2,1,0:T(8,128)(2,1)S(1)} %collective-permute-done.late_hbm, bf16[7,16,32,512]{3,2,1,0:T(8,128)(2,1)S(1)} %get-tuple-element.25.rows, f32[3584,128]{1,0:T(8,128)S(1)} %get-tuple-element.26.mine_ref, ...), custom_call_target="tpu_custom_call" | custom-call | flops 2415919104 | bytes 6291456 | tf_op jit(solution)/shard_map/last_best/pallas_call | solution.py:491
  78.0 17.6 %all_to_all.15 = f32[128,1,128]{2,1,0:T(1,128)S(1)} all-to-all(f32[128,1,128]{2,1,0:T(1,128)S(1)} %bitcast.11), channel_id=1, replica_groups=mesh['yh'=2,'x'=4,'c'=2,'yl'=2,'z'=4] {'z','c','yh','x','yl'}, dimensions={0} | all-to-all | bytes 131072 | tf_op jit(solution)/shard_map/all_to_all | solution.py:582
  95.6 0.0 copy-done
  95.6 0.0 copy-done.1
  95.6 1.0 %picked.1 = f32[1,1024]{1,0:T(1,128)} custom-call(f32[8,16,128]{2,1,0:T(8,128)S(1)} %bitcast.10, s32[1,1024]{1,0:T(1,128)S(1)} %bitcast.13, s32[1,1024]{1,0:T(1,128)S(1)} %copy-done.1), custom_call_target="tpu_custom_call" | custom-call | tf_op jit(solution)/shard_map/picked/pallas_call | solution.py:519
  (4 shorter events, 0.1 us)
Async XLA Ops:
  4.8 7.7 %copy-start.2 = (bf16[16,144,128]{2,1,0:T(8,128)(2,1)S(1)}, bf16[16,144,128]{2,1,0:T(8,128)(2,1)}, u32[]{:S(2)}) copy-start(bf16[16,144,128]{2,1,0:T(8,128)(2,1)} %get-tuple-element.23) | copy-start | bytes 1769476
  4.9 33.1 %all-to-all-start = ((bf16[16,400,128]{2,1,0:T(8,128)(2,1)}), bf16[16,400,128]{2,1,0:T(8,128)(2,1)S(1)}, u32[]{:S(2)}, u32[]{:S(2)}) async-start(bf16[16,400,128]{2,1,0:T(8,128)(2,1)} %get-tuple-element.22), calls=%async_computation | async-start | bytes 3276800 | tf_op jit(solution)/shard_map/all_to_all | solution.py:531
  12.6 16.6 %collective-permute-start.1 = (bf16[16,144,128]{2,1,0:T(8,128)(2,1)S(1)}, bf16[16,144,128]{2,1,0:T(8,128)(2,1)S(1)}, u32[]{:S(2)}, u32[]{:S(2)}) collective-permute-start(bf16[16,144,128]{2,1,0:T(8,128)(2,1)S(1)} %copy-done.2), channel_id=1, source_target_pairs={{0,1},{1,2},{2,3},{3,0},{8,9},{9,10},{10,11},{11,8},{4,5},{5,6},{6... | collective-permute-start | bytes 1769480 | tf_op jit(solution)/shard_map/ppermute | solution.py:537
  14.3 16.5 %collective-permute-start.2 = (bf16[16,144,128]{2,1,0:T(8,128)(2,1)S(1)}, bf16[16,144,128]{2,1,0:T(8,128)(2,1)S(1)}, u32[]{:S(2)}, u32[]{:S(2)}) collective-permute-start(bf16[16,144,128]{2,1,0:T(8,128)(2,1)S(1)} %copy-done.2), channel_id=1, source_target_pairs={{0,11},{1,8},{2,1},{3,2},{8,3},{9,0},{10,9},{11,10},{4,15},{5,12},... | collective-permute-start | bytes 1769480 | tf_op jit(solution)/shard_map/ppermute | solution.py:538
  37.9 12.9 %collective-permute-start.3 = (bf16[16,400,128]{2,1,0:T(8,128)(2,1)S(1)}, bf16[16,400,128]{2,1,0:T(8,128)(2,1)}, u32[]{:S(2)}, u32[]{:S(2)}) collective-permute-start(bf16[16,400,128]{2,1,0:T(8,128)(2,1)S(1)} %all-to-all-done.own_hbm), channel_id=1, source_target_pairs={{0,8},{8,0},{1,9},{9,1},{2,10},{10,2},{3,11},{11,3},{4,12},{12,4},... | collective-permute-start | bytes 4915208 | tf_op jit(solution)/shard_map/ppermute | solution.py:548
  39.1 22.9 %all-to-all-start.1 = ((bf16[16,272,128]{2,1,0:T(8,128)(2,1)}), bf16[16,272,128]{2,1,0:T(8,128)(2,1)S(1)}, u32[]{:S(2)}, u32[]{:S(2)}) async-start(bf16[16,272,128]{2,1,0:T(8,128)(2,1)} %pad_maximum_fusion), calls=%async_computation.1 | async-start | bytes 2228224 | tf_op jit(solution)/shard_map/all_to_all | solution.py:531
  43.9 27.6 %collective-permute-start.5 = (bf16[16,256,128]{2,1,0:T(8,128)(2,1)}, bf16[16,256,128]{2,1,0:T(8,128)(2,1)}, u32[]{:S(2)}, u32[]{:S(2)}) collective-permute-start(bf16[16,256,128]{2,1,0:T(8,128)(2,1)} %slice.34), channel_id=1, source_target_pairs={{0,1},{1,2},{2,3},{3,0},{8,9},{9,10},{10,11},{11,8},{4,5},{5,6},{6... | collective-permute-start | bytes 3145736 | tf_op jit(solution)/shard_map/ppermute | solution.py:546
  46.6 15.4 %collective-permute-start.4 = (bf16[16,128,128]{2,1,0:T(8,128)(2,1)}, bf16[16,128,128]{2,1,0:T(8,128)(2,1)}, u32[]{:S(2)}, u32[]{:S(2)}) collective-permute-start(bf16[16,128,128]{2,1,0:T(8,128)(2,1)} %get-tuple-element.39), channel_id=1, source_target_pairs={{0,11},{1,8},{2,1},{3,2},{8,3},{9,0},{10,9},{11,10},{4,15},{5,12},... | collective-permute-start | bytes 1572872 | tf_op jit(solution)/shard_map/ppermute | solution.py:545
  48.7 25.5 %collective-permute-start = (bf16[16,128,128]{2,1,0:T(8,128)(2,1)}, bf16[16,128,128]{2,1,0:T(8,128)(2,1)S(1)}, u32[]{:S(2)}, u32[]{:S(2)}) collective-permute-start(bf16[16,128,128]{2,1,0:T(8,128)(2,1)} %get-tuple-element.40), channel_id=1, source_target_pairs={{0,11},{1,8},{2,1},{3,2},{8,3},{9,0},{10,9},{11,10},{4,15},{5,12},... | collective-permute-start | bytes 1572872 | tf_op jit(solution)/shard_map/ppermute | solution.py:545
  74.3 21.3 %copy-start = (s32[1024]{0:T(1024)S(1)}, s32[1024]{0:T(1024)}, u32[]{:S(2)}) copy-start(s32[1024]{0:T(1024)} %param.3) | copy-start | bytes 12292
  74.3 21.3 %copy-start.1 = (s32[1,1024]{1,0:T(1,128)S(1)}, s32[1,1024]{1,0:T(1,128)}, u32[]{:S(2)}) copy-start(s32[1,1024]{1,0:T(1,128)} %get-tuple-element.38.place_ref) | copy-start | bytes 12292

commit v7 on v6

--- a/solution.py
+++ b/solution.py
@@ -503,15 +503,15 @@
     group = cluster_ref[...] // CPG
     slot = place_ref[...] - group * SLOTS
     hot = (lax.broadcasted_iota(jnp.int32, (GROUPS, ROWS), 0) == group).astype(jnp.bfloat16)
-    rest = jnp.max(answers_ref[...], axis=0)
-    found = jnp.zeros((128, ROWS), jnp.float32)
+    rest = jnp.max(answers_ref[...], axis=0)[:, :SLOTS]
+    found = jnp.zeros((SLOTS, ROWS), jnp.float32)
     for _ in range(3):
         part = rest.astype(jnp.bfloat16)
         rest = rest - part.astype(jnp.float32)
         found = found + lax.dot_general(
             part, hot, (((0,), (0,)), ((), ())), preferred_element_type=jnp.float32
         )
-    here = lax.broadcasted_iota(jnp.int32, (128, ROWS), 0) == slot
+    here = lax.broadcasted_iota(jnp.int32, (SLOTS, ROWS), 0) == slot
     out_ref[...] = jnp.sum(jnp.where(here, found, 0.0), axis=0, keepdims=True)
 
 

time: 97 us -> 96.9 us (level)
  no operation moved by 1% of the time
where the time goes in v7:
time: 96.9 us; the launch traced here: 96.6 us
  Pallas kernels  26.7 us (28%)
  waiting for transfers between devices  25.7 us (27%)
  starting transfers between devices  23 us (24%)
  blocking collectives  17.6 us (18%)
  local copies, waits for them, and re-layouts  2.3 us (2%)
  other arithmetic  1.16 us (1%)
    all_to_all x1, blocking collectives, shards(): lax.all_to_all(answers.reshape(RING_SIZE * GROUPS, 1, LANES), EVERYWHERE,...  17.6 us
    ppermute x1, waiting for transfers between devices, shards(): under = lax.ppermute(early, RING, to_above())  11.8 us
    all_to_all x2, starting transfers between devices, all_to_plane(): return lax.all_to_all(block, PLANE, split_axis=0, concat_axis=0, tiled=True)  11.4 us
    all_to_all x2, waiting for transfers between devices, all_to_plane(): return lax.all_to_all(block, PLANE, split_axis=0, concat_axis=0, tiled=True)  9.79 us
    pallas_call x1, Pallas kernels, own_best(): kernel_call(own_kernel, 'own_best', 18, [ANY, ANY], (best_shape(),), [row...  7.41 us
    pallas_call x1, Pallas kernels, near_best(): kernel_call(near_kernel, 'near_best', 14, [ANY] * 4 + [VMEM], (best_shape...  7 us
    pallas_call x1, Pallas kernels, send_rows(): pl.pallas_call(send_kernel, in_specs=[ANY, ANY], out_specs=(VMEM, VMEM, A...  4.84 us
    ppermute x2, starting transfers between devices, shards(): above = [lax.ppermute(block, RING, to_below()) for block in late]  4.06 us
  transfers between devices with their start and end apart: 8, of which 5 were waited for; matrix products, arithmetic and copies ran while one was open for 4% of the time, Pallas kernels for 18%

profile of v7, /device:TPU:1, one launch (start us, length us, event | category | flops | bytes accessed | tf_op | source)
XLA Modules:
  0.0 96.6 jit_solution(12010437611952660182)
XLA Ops:
  0.0 4.8 %send_rows.1 = (s32[1,1024]{1,0:T(1,128)}, bf16[16,144,128]{2,1,0:T(8,128)(2,1)}, bf16[16,400,128]{2,1,0:T(8,128)(2,1)}) custom-call(s32[1,1024]{1,0:T(1,128)} %bitcast.12, bf16[1024,512]{1,0:T(8,128)(2,1)} %rows_hbm.1), custom_call_target="tpu_custom_call" | custom-call | tf_op jit(solution)/shard_map/send_rows/pallas_call | solution.py:141
  4.8 0.0 copy-start.2
  4.9 7.7 %all-to-all-start = ((bf16[16,400,128]{2,1,0:T(8,128)(2,1)}), bf16[16,400,128]{2,1,0:T(8,128)(2,1)S(1)}, u32[]{:S(2)}, u32[]{:S(2)}) async-start(bf16[16,400,128]{2,1,0:T(8,128)(2,1)} %get-tuple-element.22), calls=%async_computation | async-start | bytes 3276800 | tf_op jit(solution)/shard_map/all_to_all | solution.py:531
  12.6 0.0 copy-done.2
  12.6 1.7 %collective-permute-start.1 = (bf16[16,144,128]{2,1,0:T(8,128)(2,1)S(1)}, bf16[16,144,128]{2,1,0:T(8,128)(2,1)S(1)}, u32[]{:S(2)}, u32[]{:S(2)}) collective-permute-start(bf16[16,144,128]{2,1,0:T(8,128)(2,1)S(1)} %copy-done.2), channel_id=1, source_target_pairs={{0,1},{1,2},{2,3},{3,0},{8,9},{9,10},{10,11},{11,8},{4,5},{5,6},{6... | collective-permute-start | bytes 1769480 | tf_op jit(solution)/shard_map/ppermute | solution.py:537
  14.3 3.1 %collective-permute-start.2 = (bf16[16,144,128]{2,1,0:T(8,128)(2,1)S(1)}, bf16[16,144,128]{2,1,0:T(8,128)(2,1)S(1)}, u32[]{:S(2)}, u32[]{:S(2)}) collective-permute-start(bf16[16,144,128]{2,1,0:T(8,128)(2,1)S(1)} %copy-done.2), channel_id=1, source_target_pairs={{0,11},{1,8},{2,1},{3,2},{8,3},{9,0},{10,9},{11,10},{4,15},{5,12},... | collective-permute-start | bytes 1769480 | tf_op jit(solution)/shard_map/ppermute | solution.py:538
  17.4 11.8 %collective-permute-done.1 = bf16[16,144,128]{2,1,0:T(8,128)(2,1)S(1)} collective-permute-done((bf16[16,144,128]{2,1,0:T(8,128)(2,1)S(1)}, bf16[16,144,128]{2,1,0:T(8,128)(2,1)S(1)}, u32[]{:S(2)}, u32[]{:S(2)}) %collective-permute-start.1) | collective-permute-done | bytes 589856 | tf_op jit(solution)/shard_map/ppermute | solution.py:537
  29.2 1.6 %collective-permute-done.2 = bf16[16,144,128]{2,1,0:T(8,128)(2,1)S(1)} collective-permute-done((bf16[16,144,128]{2,1,0:T(8,128)(2,1)S(1)}, bf16[16,144,128]{2,1,0:T(8,128)(2,1)S(1)}, u32[]{:S(2)}, u32[]{:S(2)}) %collective-permute-start.2) | collective-permute-done | bytes 589856 | tf_op jit(solution)/shard_map/ppermute | solution.py:538
  30.8 1.1 %pad_maximum_fusion = bf16[16,272,128]{2,1,0:T(8,128)(2,1)} fusion(bf16[16,8,128]{2,1,0:T(8,128)(2,1)S(1)} %slice.32, bf16[16,8,128]{2,1,0:T(8,128)(2,1)S(1)} %slice.31, bf16[16,128,128]{2,1,0:T(8,128)(2,1)S(1)} %slice.30, bf16[16,128,128]{2,1,0:T(8,128)(2,1)S(1)} %slice.29), kind=kLoop, calls=%fused_computation | loop fusion | flops 4456448 | bytes 2228224 | tf_op jit(solution)/shard_map/concatenate | solution.py:540
  31.9 6.0 %all-to-all-done.own_hbm = bf16[16,400,128]{2,1,0:T(8,128)(2,1)S(1)} async-done(((bf16[16,400,128]{2,1,0:T(8,128)(2,1)}), bf16[16,400,128]{2,1,0:T(8,128)(2,1)S(1)}, u32[]{:S(2)}, u32[]{:S(2)}) %all-to-all-start) | async-done | bytes 1638432 | tf_op jit(solution)/shard_map/all_to_all | solution.py:531
  37.9 1.1 %collective-permute-start.3 = (bf16[16,400,128]{2,1,0:T(8,128)(2,1)S(1)}, bf16[16,400,128]{2,1,0:T(8,128)(2,1)}, u32[]{:S(2)}, u32[]{:S(2)}) collective-permute-start(bf16[16,400,128]{2,1,0:T(8,128)(2,1)S(1)} %all-to-all-done.own_hbm), channel_id=1, source_target_pairs={{0,8},{8,0},{1,9},{9,1},{2,10},{10,2},{3,11},{11,3},{4,12},{12,4},... | collective-permute-start | bytes 4915208 | tf_op jit(solution)/shard_map/ppermute | solution.py:548
  39.1 3.7 %all-to-all-start.1 = ((bf16[16,272,128]{2,1,0:T(8,128)(2,1)}), bf16[16,272,128]{2,1,0:T(8,128)(2,1)S(1)}, u32[]{:S(2)}, u32[]{:S(2)}) async-start(bf16[16,272,128]{2,1,0:T(8,128)(2,1)} %pad_maximum_fusion), calls=%async_computation.1 | async-start | bytes 2228224 | tf_op jit(solution)/shard_map/all_to_all | solution.py:531
  42.8 1.1 %slice.34 = bf16[16,256,128]{2,1,0:T(8,128)(2,1)} slice(bf16[16,400,128]{2,1,0:T(8,128)(2,1)S(1)} %all-to-all-done.own_hbm), slice={[0:16], [0:256], [0:128]} | slice | bytes 2097152 | tf_op jit(solution)/shard_map/slice | solution.py:546
  43.9 1.6 %collective-permute-start.5 = (bf16[16,256,128]{2,1,0:T(8,128)(2,1)}, bf16[16,256,128]{2,1,0:T(8,128)(2,1)}, u32[]{:S(2)}, u32[]{:S(2)}) collective-permute-start(bf16[16,256,128]{2,1,0:T(8,128)(2,1)} %slice.34), channel_id=1, source_target_pairs={{0,1},{1,2},{2,3},{3,0},{8,9},{9,10},{10,11},{11,8},{4,5},{5,6},{6... | collective-permute-start | bytes 3145736 | tf_op jit(solution)/shard_map/ppermute | solution.py:546
  45.5 1.1 %fusion = (bf16[16,128,128]{2,1,0:T(8,128)(2,1)}, bf16[16,128,128]{2,1,0:T(8,128)(2,1)}) fusion(bf16[16,400,128]{2,1,0:T(8,128)(2,1)S(1)} %all-to-all-done.own_hbm), kind=kLoop, calls=%fused_computation.2 | loop fusion | bytes 2097152 | tf_op jit(solution)/shard_map/slice | solution.py:544
  46.6 2.0 %collective-permute-start.4 = (bf16[16,128,128]{2,1,0:T(8,128)(2,1)}, bf16[16,128,128]{2,1,0:T(8,128)(2,1)}, u32[]{:S(2)}, u32[]{:S(2)}) collective-permute-start(bf16[16,128,128]{2,1,0:T(8,128)(2,1)} %get-tuple-element.39), channel_id=1, source_target_pairs={{0,11},{1,8},{2,1},{3,2},{8,3},{9,0},{10,9},{11,10},{4,15},{5,12},... | collective-permute-start | bytes 1572872 | tf_op jit(solution)/shard_map/ppermute | solution.py:545
  48.7 0.1 pad_add_fusion.slabs_ref
  48.7 2.0 %collective-permute-start = (bf16[16,128,128]{2,1,0:T(8,128)(2,1)}, bf16[16,128,128]{2,1,0:T(8,128)(2,1)S(1)}, u32[]{:S(2)}, u32[]{:S(2)}) collective-permute-start(bf16[16,128,128]{2,1,0:T(8,128)(2,1)} %get-tuple-element.40), channel_id=1, source_target_pairs={{0,11},{1,8},{2,1},{3,2},{8,3},{9,0},{10,9},{11,10},{4,15},{5,12},... | collective-permute-start | bytes 1572872 | tf_op jit(solution)/shard_map/ppermute | solution.py:545
  50.8 0.0 collective-permute-done.3.peer_hbm
  50.8 7.4 %own_best.1.old_ref = f32[3,1,512]{2,1,0:T(1,128)S(1)} custom-call(bf16[16,400,128]{2,1,0:T(8,128)(2,1)S(1)} %all-to-all-done.own_hbm, bf16[16,400,128]{2,1,0:T(8,128)(2,1)} %collective-permute-done.3.peer_hbm), custom_call_target="tpu_custom_call" | custom-call | flops 4831838208 | bytes 6291456 | tf_op jit(solution)/shard_map/own_best/pallas_call | solution.py:301
  58.2 3.8 %all-to-all-done.1.early_hbm = bf16[16,272,128]{2,1,0:T(8,128)(2,1)S(1)} async-done(((bf16[16,272,128]{2,1,0:T(8,128)(2,1)}), bf16[16,272,128]{2,1,0:T(8,128)(2,1)S(1)}, u32[]{:S(2)}, u32[]{:S(2)}) %all-to-all-start.1) | async-done | bytes 1114144 | tf_op jit(solution)/shard_map/all_to_all | solution.py:531
  62.0 0.0 collective-permute-done.4.above_hbm
  62.0 7.0 %near_best.1 = (f32[3,1,512]{2,1,0:T(1,128)S(1)}, f32[3,1,512]{2,1,0:T(1,128)S(1)}, f32[1,1,512]{2,1,0:T(1,128)S(1)}, f32[2,1,512]{2,1,0:T(1,128)S(1)}, bf16[7,1...) custom-call(bf16[16,400,128]{2,1,0:T(8,128)(2,1)S(1)} %all-to-all-do, ...), custom_call_target="tpu_custom_call" | custom-call | flops 3758096384 | bytes 6291456 | tf_op jit(solution)/shard_map/near_best/pallas_call | solution.py:371
  69.0 2.5 %collective-permute-done.5.below_hbm = bf16[16,256,128]{2,1,0:T(8,128)(2,1)} collective-permute-done((bf16[16,256,128]{2,1,0:T(8,128)(2,1)}, bf16[16,256,128]{2,1,0:T(8,128)(2,1)}, u32[]{:S(2)}, u32[]{:S(2)}) %collective-permute-start.5) | collective-permute-done | bytes 1048608 | tf_op jit(solution)/shard_map/ppermute | solution.py:546
  71.5 2.8 %middle_best.1 = (f32[2,1,512]{2,1,0:T(1,128)S(1)}, f32[2,1,512]{2,1,0:T(1,128)S(1)}, bf16[2,16,32,512]{3,2,1,0:T(8,128)(2,1)S(1)}, f32[1024,128]{1,0:T(8,128)S(1)}) custom-call(bf16[16,256,128]{2,1,0:T(8,128)(2,1)} %collective-permute-done.5.below_hbm, bf16[2,16,32,512]{3,2,1,0:T(8,128)(2,1)S(1)} %get-tuple-element.28.above, ...), custom_call_target="tpu_custom_call" | custom-call | flops 1073741824 | bytes 6291456 | tf_op jit(solution)/shard_map/middle_best/pallas_call | solution.py:430
  74.3 0.0 collective-permute-done.late_hbm
  74.3 0.0 copy-start
  74.3 0.0 copy-start.1
  74.3 3.7 %last_best.1 = f32[8,16,128]{2,1,0:T(8,128)S(1)} custom-call(s32[4]{0:T(128)S(1)} %pad_add_fusion.slabs_ref, bf16[16,128,128]{2,1,0:T(8,128)(2,1)S(1)} %collective-permute-done.late_hbm, bf16[7,16,32,512]{3,2,1,0:T(8,128)(2,1)S(1)} %get-tuple-element.25.rows, f32[3584,128]{1,0:T(8,128)S(1)} %get-tuple-element.26.mine_ref, ...), custom_call_target="tpu_custom_call" | custom-call | flops 2415919104 | bytes 6291456 | tf_op jit(solution)/shard_map/last_best/pallas_call | solution.py:491
  78.0 17.6 %all_to_all.15 = f32[128,1,128]{2,1,0:T(1,128)S(1)} all-to-all(f32[128,1,128]{2,1,0:T(1,128)S(1)} %bitcast.11), channel_id=1, replica_groups=mesh['yh'=2,'x'=4,'c'=2,'yl'=2,'z'=4] {'z','c','yh','x','yl'}, dimensions={0} | all-to-all | bytes 131072 | tf_op jit(solution)/shard_map/all_to_all | solution.py:582
  95.6 0.0 copy-done
  95.6 0.0 copy-done.1
  95.6 0.9 picked.1
  (4 shorter events, 0.1 us)
Async XLA Ops:
  4.8 7.7 %copy-start.2 = (bf16[16,144,128]{2,1,0:T(8,128)(2,1)S(1)}, bf16[16,144,128]{2,1,0:T(8,128)(2,1)}, u32[]{:S(2)}) copy-start(bf16[16,144,128]{2,1,0:T(8,128)(2,1)} %get-tuple-element.23) | copy-start | bytes 1769476
  4.9 33.1 %all-to-all-start = ((bf16[16,400,128]{2,1,0:T(8,128)(2,1)}), bf16[16,400,128]{2,1,0:T(8,128)(2,1)S(1)}, u32[]{:S(2)}, u32[]{:S(2)}) async-start(bf16[16,400,128]{2,1,0:T(8,128)(2,1)} %get-tuple-element.22), calls=%async_computation | async-start | bytes 3276800 | tf_op jit(solution)/shard_map/all_to_all | solution.py:531
  12.6 16.6 %collective-permute-start.1 = (bf16[16,144,128]{2,1,0:T(8,128)(2,1)S(1)}, bf16[16,144,128]{2,1,0:T(8,128)(2,1)S(1)}, u32[]{:S(2)}, u32[]{:S(2)}) collective-permute-start(bf16[16,144,128]{2,1,0:T(8,128)(2,1)S(1)} %copy-done.2), channel_id=1, source_target_pairs={{0,1},{1,2},{2,3},{3,0},{8,9},{9,10},{10,11},{11,8},{4,5},{5,6},{6... | collective-permute-start | bytes 1769480 | tf_op jit(solution)/shard_map/ppermute | solution.py:537
  14.3 16.5 %collective-permute-start.2 = (bf16[16,144,128]{2,1,0:T(8,128)(2,1)S(1)}, bf16[16,144,128]{2,1,0:T(8,128)(2,1)S(1)}, u32[]{:S(2)}, u32[]{:S(2)}) collective-permute-start(bf16[16,144,128]{2,1,0:T(8,128)(2,1)S(1)} %copy-done.2), channel_id=1, source_target_pairs={{0,11},{1,8},{2,1},{3,2},{8,3},{9,0},{10,9},{11,10},{4,15},{5,12},... | collective-permute-start | bytes 1769480 | tf_op jit(solution)/shard_map/ppermute | solution.py:538
  37.9 12.9 %collective-permute-start.3 = (bf16[16,400,128]{2,1,0:T(8,128)(2,1)S(1)}, bf16[16,400,128]{2,1,0:T(8,128)(2,1)}, u32[]{:S(2)}, u32[]{:S(2)}) collective-permute-start(bf16[16,400,128]{2,1,0:T(8,128)(2,1)S(1)} %all-to-all-done.own_hbm), channel_id=1, source_target_pairs={{0,8},{8,0},{1,9},{9,1},{2,10},{10,2},{3,11},{11,3},{4,12},{12,4},... | collective-permute-start | bytes 4915208 | tf_op jit(solution)/shard_map/ppermute | solution.py:548
  39.1 22.9 %all-to-all-start.1 = ((bf16[16,272,128]{2,1,0:T(8,128)(2,1)}), bf16[16,272,128]{2,1,0:T(8,128)(2,1)S(1)}, u32[]{:S(2)}, u32[]{:S(2)}) async-start(bf16[16,272,128]{2,1,0:T(8,128)(2,1)} %pad_maximum_fusion), calls=%async_computation.1 | async-start | bytes 2228224 | tf_op jit(solution)/shard_map/all_to_all | solution.py:531
  43.9 27.6 %collective-permute-start.5 = (bf16[16,256,128]{2,1,0:T(8,128)(2,1)}, bf16[16,256,128]{2,1,0:T(8,128)(2,1)}, u32[]{:S(2)}, u32[]{:S(2)}) collective-permute-start(bf16[16,256,128]{2,1,0:T(8,128)(2,1)} %slice.34), channel_id=1, source_target_pairs={{0,1},{1,2},{2,3},{3,0},{8,9},{9,10},{10,11},{11,8},{4,5},{5,6},{6... | collective-permute-start | bytes 3145736 | tf_op jit(solution)/shard_map/ppermute | solution.py:546
  46.6 15.4 %collective-permute-start.4 = (bf16[16,128,128]{2,1,0:T(8,128)(2,1)}, bf16[16,128,128]{2,1,0:T(8,128)(2,1)}, u32[]{:S(2)}, u32[]{:S(2)}) collective-permute-start(bf16[16,128,128]{2,1,0:T(8,128)(2,1)} %get-tuple-element.39), channel_id=1, source_target_pairs={{0,11},{1,8},{2,1},{3,2},{8,3},{9,0},{10,9},{11,10},{4,15},{5,12},... | collective-permute-start | bytes 1572872 | tf_op jit(solution)/shard_map/ppermute | solution.py:545
  48.7 25.5 %collective-permute-start = (bf16[16,128,128]{2,1,0:T(8,128)(2,1)}, bf16[16,128,128]{2,1,0:T(8,128)(2,1)S(1)}, u32[]{:S(2)}, u32[]{:S(2)}) collective-permute-start(bf16[16,128,128]{2,1,0:T(8,128)(2,1)} %get-tuple-element.40), channel_id=1, source_target_pairs={{0,11},{1,8},{2,1},{3,2},{8,3},{9,0},{10,9},{11,10},{4,15},{5,12},... | collective-permute-start | bytes 1572872 | tf_op jit(solution)/shard_map/ppermute | solution.py:545
  74.3 21.3 %copy-start = (s32[1024]{0:T(1024)S(1)}, s32[1024]{0:T(1024)}, u32[]{:S(2)}) copy-start(s32[1024]{0:T(1024)} %param.3) | copy-start | bytes 12292
  74.3 21.3 %copy-start.1 = (s32[1,1024]{1,0:T(1,128)S(1)}, s32[1,1024]{1,0:T(1,128)}, u32[]{:S(2)}) copy-start(s32[1,1024]{1,0:T(1,128)} %get-tuple-element.38.place_ref) | copy-start | bytes 12292
